TPU v7x, 1024 devices: a whole 4x4x32 slice. The times are simulated.
1024 devices in a mesh: tok: 128 (over x, z), head: 4 (over y), srv: 2 (over core).
Axes of the slice: x: 4, y: 4, z: 32, core: 2. Of those that a mesh axis runs over, the one named last changes fastest.
Arguments:
- queries: bfloat16 [32768, 4096], P('tok', ('head', 'srv')), may hold values from -12 to 12
- key_heads: bfloat16 [32768, 1024], P('tok', ('head', 'srv')), may hold values from -12 to 12
- value_heads: bfloat16 [32768, 1024], P('tok', ('head', 'srv')), may hold values from -6 to 6
- doc_ids: int32 [32768], P('tok'), may hold values from 0 to 15, never falling along the last dimension, each value on 1 to 3840 neighbouring positions
- out_weight: bfloat16 [4096, 4096], P(('head', 'srv')), may hold values from -0.125 to 0.125
Outputs:
- mixed: bfloat16 [32768, 4096], P('tok', ('head', 'srv'))
Inputs may be any that keep to these rules, and one draw needn't show every extreme that they name: `doc_ids`: document ids never fall along the window; every document holds 1 to 3840 tokens, and one holds exactly 3840.
All inputs are finite; a program needn't handle non-finite values.
Results may differ from a plain program's by a relative error of at most 0.019.
Values may be sent and summed in bfloat16 or wider, within the bound.
No kernel may reach another device: no remote copies, remote signals or barrier semaphores. Data moves between devices by JAX's collectives and lax.ppermute only.
A program may use at most 32 MiB of HBM per device.

v0:
```python
import math

import jax
import jax.numpy as jnp
from jax import lax
from jax.sharding import PartitionSpec as P

HEADS = 32
KV_HEADS = 8
HEAD_DIM = 128


def shifted(value, axis, by):
    size = lax.axis_size(axis)
    pairs = [(i, i + by) for i in range(size) if 0 <= i + by < size]
    return lax.ppermute(value, axis, pairs)


def per_device(queries, key_heads, value_heads, doc_ids, out_weight):
    tok_rows = queries.shape[0]
    kv_local = key_heads.shape[1] // HEAD_DIM
    group_size = HEADS // KV_HEADS
    score_scale = 1.0 / math.sqrt(HEAD_DIM)
    kv_reach = min(16, lax.axis_size("tok") // 2)
    device_row = lax.axis_index("tok")
    query_mat = queries.reshape(tok_rows, kv_local, group_size, HEAD_DIM)
    query_mat = query_mat.transpose(1, 2, 0, 3).reshape(kv_local, group_size * tok_rows, HEAD_DIM)
    query_pos = jnp.tile(device_row * tok_rows + jnp.arange(tok_rows, dtype=jnp.int32), group_size)
    query_docs = jnp.tile(doc_ids.astype(jnp.float32), group_size)
    doc_marks = doc_ids.astype(jnp.bfloat16)

    def attend(running, key_piece, value_piece, doc_piece, offset):
        running_max, running_sum, weighted = running
        key_pos = (device_row - offset) * tok_rows + jnp.arange(tok_rows, dtype=jnp.int32)
        key_docs = doc_piece.astype(jnp.float32)
        allowed = (query_docs[:, None] == key_docs[None, :]) & (
            key_pos[None, :] <= query_pos[:, None]
        )
        allowed = allowed & (key_pos[None, :] >= 0)
        keys_here = key_piece.reshape(tok_rows, kv_local, HEAD_DIM)
        values_here = value_piece.reshape(tok_rows, kv_local, HEAD_DIM)
        scores = (
            jnp.einsum("gqd,kgd->gqk", query_mat, keys_here, preferred_element_type=jnp.float32)
            * score_scale
        )
        scores = jnp.where(allowed[None], scores, -jnp.inf)
        new_max = jnp.maximum(running_max, jnp.max(scores, axis=-1))
        factor = jnp.exp(running_max - new_max)
        weights = jnp.exp(scores - new_max[..., None])
        new_sum = running_sum * factor + jnp.sum(weights, axis=-1)
        product = jnp.einsum(
            "gqk,kgd->gqd",
            weights.astype(jnp.bfloat16),
            values_here,
            preferred_element_type=jnp.float32,
        )
        return (new_max, new_sum, weighted * factor[..., None] + product)

    def add_piece(running, key_piece, value_piece, doc_piece, offset):
        return attend(running, key_piece, value_piece, doc_piece, offset)

    rows_all = group_size * tok_rows
    start_state = (
        jnp.full((kv_local, rows_all), -jnp.inf, jnp.float32),
        jnp.zeros((kv_local, rows_all), jnp.float32),
        jnp.zeros((kv_local, rows_all, HEAD_DIM), jnp.float32),
    )
    running = attend(start_state, key_heads, value_heads, doc_marks, 0)

    def cycle_turn(offset, cycle_carry):
        current, held_piece = cycle_carry
        moved = shifted((held_piece[0], held_piece[1], held_piece[2]), "tok", 1)
        return (add_piece(current, moved[0], moved[1], moved[2], offset), moved)

    running, unused = lax.fori_loop(
        1, kv_reach, cycle_turn, (running, (key_heads, value_heads, doc_marks))
    )
    final_max, final_sum, final_weighted = running
    attended = (final_weighted / final_sum[..., None]).astype(jnp.bfloat16)
    attended = attended.reshape(kv_local, group_size, tok_rows, HEAD_DIM).transpose(2, 0, 1, 3)
    attended = attended.reshape(tok_rows, kv_local * group_size * HEAD_DIM)
    summed = lax.psum_scatter(
        lax.dot_general(
            out_weight, attended, (((0,), (1,)), ((), ())), preferred_element_type=jnp.float32
        ).astype(jnp.bfloat16),
        ("head", "srv"),
        scatter_dimension=0,
        tiled=True,
    ).astype(jnp.float32)
    return summed.T.astype(jnp.bfloat16)


def solution(mesh):
    placed = (
        P("tok", ("head", "srv")),
        P("tok", ("head", "srv")),
        P("tok", ("head", "srv")),
        P("tok"),
        P(("head", "srv"), None),
    )
    return jax.shard_map(
        per_device, mesh=mesh, in_specs=placed, out_specs=P("tok", ("head", "srv")), check_vma=False
    )
```

profile of v0, /device:TPU:1, one launch (start us, length us, event | category | flops | bytes accessed | tf_op | source)
XLA Modules:
  0.0 285.8 jit_solution(113344091041765676)
XLA Ops:
  11.1 191.0 %while.24 = (s32[]{:T(128)}, f32[1,1024]{1,0:T(1,128)S(1)}, f32[1,1024]{1,0:T(1,128)S(1)}, f32[1,1024,128]{2,1,0:T(8,128)S(1)}, bf16[256,128]{1,0:T(8,128)(2,1)S...) while((s32[]{:T(128)}, f32[1,1024]{1,0:T(1,128)S(1)}, ...), condition=%wide.region_5.6_spmd.clone, body=%wide.region_2.5_spmd.clone.sunk | while | flops 137366528 | bytes 5482773 | solution.py:75
  11.1 4.4 %collective-permute-start = (bf16[256,128]{1,0:T(8,128)(2,1)S(1)}, bf16[256,128]{1,0:T(8,128)(2,1)S(1)}, u32[]{:S(2)}, u32[]{:S(2)}) collective-permute-start(bf16[256,128]{1,0:T(8,128)(2,1)S(1)} %get-tuple-element.343), channel_id=1, source_target_pairs={{0,8},{8,16},{16,24},{24,32},{32,40},{40,48},{48,56},{56,64},{64,7... | collective-permute-start | bytes 196616 | tf_op jit(solution)/shard_map/while/body/eval_jaxpr/ppermute | solution.py:16
  24.4 4.7 %collective-permute-start = (bf16[256,128]{1,0:T(8,128)(2,1)S(1)}, bf16[256,128]{1,0:T(8,128)(2,1)S(1)}, u32[]{:S(2)}, u32[]{:S(2)}) collective-permute-start(bf16[256,128]{1,0:T(8,128)(2,1)S(1)} %get-tuple-element.343), channel_id=1, source_target_pairs={{0,8},{8,16},{16,24},{24,32},{32,40},{40,48},{48,56},{56,64},{64,7... | collective-permute-start | bytes 196616 | tf_op jit(solution)/shard_map/while/body/eval_jaxpr/ppermute | solution.py:16
  29.2 3.7 %collective-permute-start.1 = (bf16[256]{0:T(256)(128)(2,1)S(1)}, bf16[256]{0:T(256)(128)(2,1)S(1)}, u32[]{:S(2)}, u32[]{:S(2)}) collective-permute-start(bf16[256]{0:T(256)(128)(2,1)S(1)} %get-tuple-element.345), channel_id=1, source_target_pairs={{0,8},{8,16},{16,24},{24,32},{32,40},{40,48},{48,56},{56,64},{64,7... | collective-permute-start | bytes 1544 | tf_op jit(solution)/shard_map/while/body/eval_jaxpr/ppermute | solution.py:16
  38.8 4.3 %collective-permute-start = (bf16[256,128]{1,0:T(8,128)(2,1)S(1)}, bf16[256,128]{1,0:T(8,128)(2,1)S(1)}, u32[]{:S(2)}, u32[]{:S(2)}) collective-permute-start(bf16[256,128]{1,0:T(8,128)(2,1)S(1)} %get-tuple-element.343), channel_id=1, source_target_pairs={{0,8},{8,16},{16,24},{24,32},{32,40},{40,48},{48,56},{56,64},{64,7... | collective-permute-start | bytes 196616 | tf_op jit(solution)/shard_map/while/body/eval_jaxpr/ppermute | solution.py:16
  43.1 3.7 %collective-permute-start.1 = (bf16[256]{0:T(256)(128)(2,1)S(1)}, bf16[256]{0:T(256)(128)(2,1)S(1)}, u32[]{:S(2)}, u32[]{:S(2)}) collective-permute-start(bf16[256]{0:T(256)(128)(2,1)S(1)} %get-tuple-element.345), channel_id=1, source_target_pairs={{0,8},{8,16},{16,24},{24,32},{32,40},{40,48},{48,56},{56,64},{64,7... | collective-permute-start | bytes 1544 | tf_op jit(solution)/shard_map/while/body/eval_jaxpr/ppermute | solution.py:16
  52.0 4.9 %collective-permute-start = (bf16[256,128]{1,0:T(8,128)(2,1)S(1)}, bf16[256,128]{1,0:T(8,128)(2,1)S(1)}, u32[]{:S(2)}, u32[]{:S(2)}) collective-permute-start(bf16[256,128]{1,0:T(8,128)(2,1)S(1)} %get-tuple-element.343), channel_id=1, source_target_pairs={{0,8},{8,16},{16,24},{24,32},{32,40},{40,48},{48,56},{56,64},{64,7... | collective-permute-start | bytes 196616 | tf_op jit(solution)/shard_map/while/body/eval_jaxpr/ppermute | solution.py:16
  56.9 3.7 %collective-permute-start.1 = (bf16[256]{0:T(256)(128)(2,1)S(1)}, bf16[256]{0:T(256)(128)(2,1)S(1)}, u32[]{:S(2)}, u32[]{:S(2)}) collective-permute-start(bf16[256]{0:T(256)(128)(2,1)S(1)} %get-tuple-element.345), channel_id=1, source_target_pairs={{0,8},{8,16},{16,24},{24,32},{32,40},{40,48},{48,56},{56,64},{64,7... | collective-permute-start | bytes 1544 | tf_op jit(solution)/shard_map/while/body/eval_jaxpr/ppermute | solution.py:16
  65.8 4.9 %collective-permute-start = (bf16[256,128]{1,0:T(8,128)(2,1)S(1)}, bf16[256,128]{1,0:T(8,128)(2,1)S(1)}, u32[]{:S(2)}, u32[]{:S(2)}) collective-permute-start(bf16[256,128]{1,0:T(8,128)(2,1)S(1)} %get-tuple-element.343), channel_id=1, source_target_pairs={{0,8},{8,16},{16,24},{24,32},{32,40},{40,48},{48,56},{56,64},{64,7... | collective-permute-start | bytes 196616 | tf_op jit(solution)/shard_map/while/body/eval_jaxpr/ppermute | solution.py:16
  79.7 5.1 %collective-permute-start = (bf16[256,128]{1,0:T(8,128)(2,1)S(1)}, bf16[256,128]{1,0:T(8,128)(2,1)S(1)}, u32[]{:S(2)}, u32[]{:S(2)}) collective-permute-start(bf16[256,128]{1,0:T(8,128)(2,1)S(1)} %get-tuple-element.343), channel_id=1, source_target_pairs={{0,8},{8,16},{16,24},{24,32},{32,40},{40,48},{48,56},{56,64},{64,7... | collective-permute-start | bytes 196616 | tf_op jit(solution)/shard_map/while/body/eval_jaxpr/ppermute | solution.py:16
  84.8 3.8 %collective-permute-start.1 = (bf16[256]{0:T(256)(128)(2,1)S(1)}, bf16[256]{0:T(256)(128)(2,1)S(1)}, u32[]{:S(2)}, u32[]{:S(2)}) collective-permute-start(bf16[256]{0:T(256)(128)(2,1)S(1)} %get-tuple-element.345), channel_id=1, source_target_pairs={{0,8},{8,16},{16,24},{24,32},{32,40},{40,48},{48,56},{56,64},{64,7... | collective-permute-start | bytes 1544 | tf_op jit(solution)/shard_map/while/body/eval_jaxpr/ppermute | solution.py:16
  88.7 3.7 %collective-permute-start.2 = (bf16[256,128]{1,0:T(8,128)(2,1)S(1)}, bf16[256,128]{1,0:T(8,128)(2,1)S(1)}, u32[]{:S(2)}, u32[]{:S(2)}) collective-permute-start(bf16[256,128]{1,0:T(8,128)(2,1)S(1)} %get-tuple-element.344), channel_id=1, source_target_pairs={{0,8},{8,16},{16,24},{24,32},{32,40},{40,48},{48,56},{56,64},{64,7... | collective-permute-start | bytes 196616 | tf_op jit(solution)/shard_map/while/body/eval_jaxpr/ppermute | solution.py:16
  94.2 4.2 %collective-permute-start = (bf16[256,128]{1,0:T(8,128)(2,1)S(1)}, bf16[256,128]{1,0:T(8,128)(2,1)S(1)}, u32[]{:S(2)}, u32[]{:S(2)}) collective-permute-start(bf16[256,128]{1,0:T(8,128)(2,1)S(1)} %get-tuple-element.343), channel_id=1, source_target_pairs={{0,8},{8,16},{16,24},{24,32},{32,40},{40,48},{48,56},{56,64},{64,7... | collective-permute-start | bytes 196616 | tf_op jit(solution)/shard_map/while/body/eval_jaxpr/ppermute | solution.py:16
  98.4 3.7 %collective-permute-start.1 = (bf16[256]{0:T(256)(128)(2,1)S(1)}, bf16[256]{0:T(256)(128)(2,1)S(1)}, u32[]{:S(2)}, u32[]{:S(2)}) collective-permute-start(bf16[256]{0:T(256)(128)(2,1)S(1)} %get-tuple-element.345), channel_id=1, source_target_pairs={{0,8},{8,16},{16,24},{24,32},{32,40},{40,48},{48,56},{56,64},{64,7... | collective-permute-start | bytes 1544 | tf_op jit(solution)/shard_map/while/body/eval_jaxpr/ppermute | solution.py:16
  102.1 3.7 %collective-permute-start.2 = (bf16[256,128]{1,0:T(8,128)(2,1)S(1)}, bf16[256,128]{1,0:T(8,128)(2,1)S(1)}, u32[]{:S(2)}, u32[]{:S(2)}) collective-permute-start(bf16[256,128]{1,0:T(8,128)(2,1)S(1)} %get-tuple-element.344), channel_id=1, source_target_pairs={{0,8},{8,16},{16,24},{24,32},{32,40},{40,48},{48,56},{56,64},{64,7... | collective-permute-start | bytes 196616 | tf_op jit(solution)/shard_map/while/body/eval_jaxpr/ppermute | solution.py:16
  107.7 4.9 %collective-permute-start = (bf16[256,128]{1,0:T(8,128)(2,1)S(1)}, bf16[256,128]{1,0:T(8,128)(2,1)S(1)}, u32[]{:S(2)}, u32[]{:S(2)}) collective-permute-start(bf16[256,128]{1,0:T(8,128)(2,1)S(1)} %get-tuple-element.343), channel_id=1, source_target_pairs={{0,8},{8,16},{16,24},{24,32},{32,40},{40,48},{48,56},{56,64},{64,7... | collective-permute-start | bytes 196616 | tf_op jit(solution)/shard_map/while/body/eval_jaxpr/ppermute | solution.py:16
  120.3 5.1 %collective-permute-start = (bf16[256,128]{1,0:T(8,128)(2,1)S(1)}, bf16[256,128]{1,0:T(8,128)(2,1)S(1)}, u32[]{:S(2)}, u32[]{:S(2)}) collective-permute-start(bf16[256,128]{1,0:T(8,128)(2,1)S(1)} %get-tuple-element.343), channel_id=1, source_target_pairs={{0,8},{8,16},{16,24},{24,32},{32,40},{40,48},{48,56},{56,64},{64,7... | collective-permute-start | bytes 196616 | tf_op jit(solution)/shard_map/while/body/eval_jaxpr/ppermute | solution.py:16
  125.4 3.8 %collective-permute-start.1 = (bf16[256]{0:T(256)(128)(2,1)S(1)}, bf16[256]{0:T(256)(128)(2,1)S(1)}, u32[]{:S(2)}, u32[]{:S(2)}) collective-permute-start(bf16[256]{0:T(256)(128)(2,1)S(1)} %get-tuple-element.345), channel_id=1, source_target_pairs={{0,8},{8,16},{16,24},{24,32},{32,40},{40,48},{48,56},{56,64},{64,7... | collective-permute-start | bytes 1544 | tf_op jit(solution)/shard_map/while/body/eval_jaxpr/ppermute | solution.py:16
  143.9 4.9 %collective-permute-start = (bf16[256,128]{1,0:T(8,128)(2,1)S(1)}, bf16[256,128]{1,0:T(8,128)(2,1)S(1)}, u32[]{:S(2)}, u32[]{:S(2)}) collective-permute-start(bf16[256,128]{1,0:T(8,128)(2,1)S(1)} %get-tuple-element.343), channel_id=1, source_target_pairs={{0,8},{8,16},{16,24},{24,32},{32,40},{40,48},{48,56},{56,64},{64,7... | collective-permute-start | bytes 196616 | tf_op jit(solution)/shard_map/while/body/eval_jaxpr/ppermute | solution.py:16
  167.3 4.4 %collective-permute-start = (bf16[256,128]{1,0:T(8,128)(2,1)S(1)}, bf16[256,128]{1,0:T(8,128)(2,1)S(1)}, u32[]{:S(2)}, u32[]{:S(2)}) collective-permute-start(bf16[256,128]{1,0:T(8,128)(2,1)S(1)} %get-tuple-element.343), channel_id=1, source_target_pairs={{0,8},{8,16},{16,24},{24,32},{32,40},{40,48},{48,56},{56,64},{64,7... | collective-permute-start | bytes 196616 | tf_op jit(solution)/shard_map/while/body/eval_jaxpr/ppermute | solution.py:16
  171.7 3.7 %collective-permute-start.1 = (bf16[256]{0:T(256)(128)(2,1)S(1)}, bf16[256]{0:T(256)(128)(2,1)S(1)}, u32[]{:S(2)}, u32[]{:S(2)}) collective-permute-start(bf16[256]{0:T(256)(128)(2,1)S(1)} %get-tuple-element.345), channel_id=1, source_target_pairs={{0,8},{8,16},{16,24},{24,32},{32,40},{40,48},{48,56},{56,64},{64,7... | collective-permute-start | bytes 1544 | tf_op jit(solution)/shard_map/while/body/eval_jaxpr/ppermute | solution.py:16
  190.0 4.7 %collective-permute-start = (bf16[256,128]{1,0:T(8,128)(2,1)S(1)}, bf16[256,128]{1,0:T(8,128)(2,1)S(1)}, u32[]{:S(2)}, u32[]{:S(2)}) collective-permute-start(bf16[256,128]{1,0:T(8,128)(2,1)S(1)} %get-tuple-element.343), channel_id=1, source_target_pairs={{0,8},{8,16},{16,24},{24,32},{32,40},{40,48},{48,56},{56,64},{64,7... | collective-permute-start | bytes 196616 | tf_op jit(solution)/shard_map/while/body/eval_jaxpr/ppermute | solution.py:16
  202.5 4.8 %fusion.10 = bf16[4096,256]{0,1:T(8,128)(2,1)} fusion(bf16[256,512]{0,1:T(8,128)(2,1)S(1)} %bitcast.76, bf16[512,4096]{1,0:T(8,128)(2,1)} %param.11), kind=kOutput, calls=%fused_computation.18 | convolution fusion | flops 1074790400 | bytes 6553600 | tf_op jit(solution)/shard_map/dot_general | solution.py:83
  207.3 71.6 %reduce-scatter.2.cloned.1.call-done = bf16[512,256]{0,1:T(8,128)(2,1)} async-done(((bf16[4096,256]{0,1:T(8,128)(2,1)}), bf16[512,256]{0,1:T(8,128)(2,1)}) %reduce-scatter.2.cloned.1.call-update) | async-done | bytes 262160 | tf_op jit(solution)/shard_map/reduce_scatter | solution.py:82
  (328 shorter events, 103.4 us)
Async XLA Ops:
  6.5 272.4 %reduce-scatter.2.cloned.1.call-start = ((), (), s32[]{:S(2)}) async-start(), calls=%async_computation.1 | async-start | bytes 2359296 | tf_op jit(solution)/shard_map/reduce_scatter | solution.py:82
  11.1 11.6 %collective-permute-start = (bf16[256,128]{1,0:T(8,128)(2,1)S(1)}, bf16[256,128]{1,0:T(8,128)(2,1)S(1)}, u32[]{:S(2)}, u32[]{:S(2)}) collective-permute-start(bf16[256,128]{1,0:T(8,128)(2,1)S(1)} %get-tuple-element.343), channel_id=1, source_target_pairs={{0,8},{8,16},{16,24},{24,32},{32,40},{40,48},{48,56},{56,64},{64,7... | collective-permute-start | bytes 196616 | tf_op jit(solution)/shard_map/while/body/eval_jaxpr/ppermute | solution.py:16
  15.5 7.2 %collective-permute-start.1 = (bf16[256]{0:T(256)(128)(2,1)S(1)}, bf16[256]{0:T(256)(128)(2,1)S(1)}, u32[]{:S(2)}, u32[]{:S(2)}) collective-permute-start(bf16[256]{0:T(256)(128)(2,1)S(1)} %get-tuple-element.345), channel_id=1, source_target_pairs={{0,8},{8,16},{16,24},{24,32},{32,40},{40,48},{48,56},{56,64},{64,7... | collective-permute-start | bytes 1544 | tf_op jit(solution)/shard_map/while/body/eval_jaxpr/ppermute | solution.py:16
  24.4 12.1 %collective-permute-start = (bf16[256,128]{1,0:T(8,128)(2,1)S(1)}, bf16[256,128]{1,0:T(8,128)(2,1)S(1)}, u32[]{:S(2)}, u32[]{:S(2)}) collective-permute-start(bf16[256,128]{1,0:T(8,128)(2,1)S(1)} %get-tuple-element.343), channel_id=1, source_target_pairs={{0,8},{8,16},{16,24},{24,32},{32,40},{40,48},{48,56},{56,64},{64,7... | collective-permute-start | bytes 196616 | tf_op jit(solution)/shard_map/while/body/eval_jaxpr/ppermute | solution.py:16
  29.2 7.3 %collective-permute-start.1 = (bf16[256]{0:T(256)(128)(2,1)S(1)}, bf16[256]{0:T(256)(128)(2,1)S(1)}, u32[]{:S(2)}, u32[]{:S(2)}) collective-permute-start(bf16[256]{0:T(256)(128)(2,1)S(1)} %get-tuple-element.345), channel_id=1, source_target_pairs={{0,8},{8,16},{16,24},{24,32},{32,40},{40,48},{48,56},{56,64},{64,7... | collective-permute-start | bytes 1544 | tf_op jit(solution)/shard_map/while/body/eval_jaxpr/ppermute | solution.py:16
  38.8 11.5 %collective-permute-start = (bf16[256,128]{1,0:T(8,128)(2,1)S(1)}, bf16[256,128]{1,0:T(8,128)(2,1)S(1)}, u32[]{:S(2)}, u32[]{:S(2)}) collective-permute-start(bf16[256,128]{1,0:T(8,128)(2,1)S(1)} %get-tuple-element.343), channel_id=1, source_target_pairs={{0,8},{8,16},{16,24},{24,32},{32,40},{40,48},{48,56},{56,64},{64,7... | collective-permute-start | bytes 196616 | tf_op jit(solution)/shard_map/while/body/eval_jaxpr/ppermute | solution.py:16
  43.1 7.2 %collective-permute-start.1 = (bf16[256]{0:T(256)(128)(2,1)S(1)}, bf16[256]{0:T(256)(128)(2,1)S(1)}, u32[]{:S(2)}, u32[]{:S(2)}) collective-permute-start(bf16[256]{0:T(256)(128)(2,1)S(1)} %get-tuple-element.345), channel_id=1, source_target_pairs={{0,8},{8,16},{16,24},{24,32},{32,40},{40,48},{48,56},{56,64},{64,7... | collective-permute-start | bytes 1544 | tf_op jit(solution)/shard_map/while/body/eval_jaxpr/ppermute | solution.py:16
  52.0 12.1 %collective-permute-start = (bf16[256,128]{1,0:T(8,128)(2,1)S(1)}, bf16[256,128]{1,0:T(8,128)(2,1)S(1)}, u32[]{:S(2)}, u32[]{:S(2)}) collective-permute-start(bf16[256,128]{1,0:T(8,128)(2,1)S(1)} %get-tuple-element.343), channel_id=1, source_target_pairs={{0,8},{8,16},{16,24},{24,32},{32,40},{40,48},{48,56},{56,64},{64,7... | collective-permute-start | bytes 196616 | tf_op jit(solution)/shard_map/while/body/eval_jaxpr/ppermute | solution.py:16
  56.9 7.2 %collective-permute-start.1 = (bf16[256]{0:T(256)(128)(2,1)S(1)}, bf16[256]{0:T(256)(128)(2,1)S(1)}, u32[]{:S(2)}, u32[]{:S(2)}) collective-permute-start(bf16[256]{0:T(256)(128)(2,1)S(1)} %get-tuple-element.345), channel_id=1, source_target_pairs={{0,8},{8,16},{16,24},{24,32},{32,40},{40,48},{48,56},{56,64},{64,7... | collective-permute-start | bytes 1544 | tf_op jit(solution)/shard_map/while/body/eval_jaxpr/ppermute | solution.py:16
  65.8 12.1 %collective-permute-start = (bf16[256,128]{1,0:T(8,128)(2,1)S(1)}, bf16[256,128]{1,0:T(8,128)(2,1)S(1)}, u32[]{:S(2)}, u32[]{:S(2)}) collective-permute-start(bf16[256,128]{1,0:T(8,128)(2,1)S(1)} %get-tuple-element.343), channel_id=1, source_target_pairs={{0,8},{8,16},{16,24},{24,32},{32,40},{40,48},{48,56},{56,64},{64,7... | collective-permute-start | bytes 196616 | tf_op jit(solution)/shard_map/while/body/eval_jaxpr/ppermute | solution.py:16
  70.7 7.2 %collective-permute-start.1 = (bf16[256]{0:T(256)(128)(2,1)S(1)}, bf16[256]{0:T(256)(128)(2,1)S(1)}, u32[]{:S(2)}, u32[]{:S(2)}) collective-permute-start(bf16[256]{0:T(256)(128)(2,1)S(1)} %get-tuple-element.345), channel_id=1, source_target_pairs={{0,8},{8,16},{16,24},{24,32},{32,40},{40,48},{48,56},{56,64},{64,7... | collective-permute-start | bytes 1544 | tf_op jit(solution)/shard_map/while/body/eval_jaxpr/ppermute | solution.py:16
  79.7 12.8 %collective-permute-start = (bf16[256,128]{1,0:T(8,128)(2,1)S(1)}, bf16[256,128]{1,0:T(8,128)(2,1)S(1)}, u32[]{:S(2)}, u32[]{:S(2)}) collective-permute-start(bf16[256,128]{1,0:T(8,128)(2,1)S(1)} %get-tuple-element.343), channel_id=1, source_target_pairs={{0,8},{8,16},{16,24},{24,32},{32,40},{40,48},{48,56},{56,64},{64,7... | collective-permute-start | bytes 196616 | tf_op jit(solution)/shard_map/while/body/eval_jaxpr/ppermute | solution.py:16
  84.8 7.7 %collective-permute-start.1 = (bf16[256]{0:T(256)(128)(2,1)S(1)}, bf16[256]{0:T(256)(128)(2,1)S(1)}, u32[]{:S(2)}, u32[]{:S(2)}) collective-permute-start(bf16[256]{0:T(256)(128)(2,1)S(1)} %get-tuple-element.345), channel_id=1, source_target_pairs={{0,8},{8,16},{16,24},{24,32},{32,40},{40,48},{48,56},{56,64},{64,7... | collective-permute-start | bytes 1544 | tf_op jit(solution)/shard_map/while/body/eval_jaxpr/ppermute | solution.py:16
  94.2 11.8 %collective-permute-start = (bf16[256,128]{1,0:T(8,128)(2,1)S(1)}, bf16[256,128]{1,0:T(8,128)(2,1)S(1)}, u32[]{:S(2)}, u32[]{:S(2)}) collective-permute-start(bf16[256,128]{1,0:T(8,128)(2,1)S(1)} %get-tuple-element.343), channel_id=1, source_target_pairs={{0,8},{8,16},{16,24},{24,32},{32,40},{40,48},{48,56},{56,64},{64,7... | collective-permute-start | bytes 196616 | tf_op jit(solution)/shard_map/while/body/eval_jaxpr/ppermute | solution.py:16
  98.4 7.5 %collective-permute-start.1 = (bf16[256]{0:T(256)(128)(2,1)S(1)}, bf16[256]{0:T(256)(128)(2,1)S(1)}, u32[]{:S(2)}, u32[]{:S(2)}) collective-permute-start(bf16[256]{0:T(256)(128)(2,1)S(1)} %get-tuple-element.345), channel_id=1, source_target_pairs={{0,8},{8,16},{16,24},{24,32},{32,40},{40,48},{48,56},{56,64},{64,7... | collective-permute-start | bytes 1544 | tf_op jit(solution)/shard_map/while/body/eval_jaxpr/ppermute | solution.py:16
  107.7 10.9 %collective-permute-start = (bf16[256,128]{1,0:T(8,128)(2,1)S(1)}, bf16[256,128]{1,0:T(8,128)(2,1)S(1)}, u32[]{:S(2)}, u32[]{:S(2)}) collective-permute-start(bf16[256,128]{1,0:T(8,128)(2,1)S(1)} %get-tuple-element.343), channel_id=1, source_target_pairs={{0,8},{8,16},{16,24},{24,32},{32,40},{40,48},{48,56},{56,64},{64,7... | collective-permute-start | bytes 196616 | tf_op jit(solution)/shard_map/while/body/eval_jaxpr/ppermute | solution.py:16
  112.6 5.9 %collective-permute-start.1 = (bf16[256]{0:T(256)(128)(2,1)S(1)}, bf16[256]{0:T(256)(128)(2,1)S(1)}, u32[]{:S(2)}, u32[]{:S(2)}) collective-permute-start(bf16[256]{0:T(256)(128)(2,1)S(1)} %get-tuple-element.345), channel_id=1, source_target_pairs={{0,8},{8,16},{16,24},{24,32},{32,40},{40,48},{48,56},{56,64},{64,7... | collective-permute-start | bytes 1544 | tf_op jit(solution)/shard_map/while/body/eval_jaxpr/ppermute | solution.py:16
  120.3 11.0 %collective-permute-start = (bf16[256,128]{1,0:T(8,128)(2,1)S(1)}, bf16[256,128]{1,0:T(8,128)(2,1)S(1)}, u32[]{:S(2)}, u32[]{:S(2)}) collective-permute-start(bf16[256,128]{1,0:T(8,128)(2,1)S(1)} %get-tuple-element.343), channel_id=1, source_target_pairs={{0,8},{8,16},{16,24},{24,32},{32,40},{40,48},{48,56},{56,64},{64,7... | collective-permute-start | bytes 196616 | tf_op jit(solution)/shard_map/while/body/eval_jaxpr/ppermute | solution.py:16
  133.0 9.2 %collective-permute-start = (bf16[256,128]{1,0:T(8,128)(2,1)S(1)}, bf16[256,128]{1,0:T(8,128)(2,1)S(1)}, u32[]{:S(2)}, u32[]{:S(2)}) collective-permute-start(bf16[256,128]{1,0:T(8,128)(2,1)S(1)} %get-tuple-element.343), channel_id=1, source_target_pairs={{0,8},{8,16},{16,24},{24,32},{32,40},{40,48},{48,56},{56,64},{64,7... | collective-permute-start | bytes 196616 | tf_op jit(solution)/shard_map/while/body/eval_jaxpr/ppermute | solution.py:16
  143.9 10.7 %collective-permute-start = (bf16[256,128]{1,0:T(8,128)(2,1)S(1)}, bf16[256,128]{1,0:T(8,128)(2,1)S(1)}, u32[]{:S(2)}, u32[]{:S(2)}) collective-permute-start(bf16[256,128]{1,0:T(8,128)(2,1)S(1)} %get-tuple-element.343), channel_id=1, source_target_pairs={{0,8},{8,16},{16,24},{24,32},{32,40},{40,48},{48,56},{56,64},{64,7... | collective-permute-start | bytes 196616 | tf_op jit(solution)/shard_map/while/body/eval_jaxpr/ppermute | solution.py:16
  156.2 9.1 %collective-permute-start = (bf16[256,128]{1,0:T(8,128)(2,1)S(1)}, bf16[256,128]{1,0:T(8,128)(2,1)S(1)}, u32[]{:S(2)}, u32[]{:S(2)}) collective-permute-start(bf16[256,128]{1,0:T(8,128)(2,1)S(1)} %get-tuple-element.343), channel_id=1, source_target_pairs={{0,8},{8,16},{16,24},{24,32},{32,40},{40,48},{48,56},{56,64},{64,7... | collective-permute-start | bytes 196616 | tf_op jit(solution)/shard_map/while/body/eval_jaxpr/ppermute | solution.py:16
  167.3 10.2 %collective-permute-start = (bf16[256,128]{1,0:T(8,128)(2,1)S(1)}, bf16[256,128]{1,0:T(8,128)(2,1)S(1)}, u32[]{:S(2)}, u32[]{:S(2)}) collective-permute-start(bf16[256,128]{1,0:T(8,128)(2,1)S(1)} %get-tuple-element.343), channel_id=1, source_target_pairs={{0,8},{8,16},{16,24},{24,32},{32,40},{40,48},{48,56},{56,64},{64,7... | collective-permute-start | bytes 196616 | tf_op jit(solution)/shard_map/while/body/eval_jaxpr/ppermute | solution.py:16
  179.2 9.1 %collective-permute-start = (bf16[256,128]{1,0:T(8,128)(2,1)S(1)}, bf16[256,128]{1,0:T(8,128)(2,1)S(1)}, u32[]{:S(2)}, u32[]{:S(2)}) collective-permute-start(bf16[256,128]{1,0:T(8,128)(2,1)S(1)} %get-tuple-element.343), channel_id=1, source_target_pairs={{0,8},{8,16},{16,24},{24,32},{32,40},{40,48},{48,56},{56,64},{64,7... | collective-permute-start | bytes 196616 | tf_op jit(solution)/shard_map/while/body/eval_jaxpr/ppermute | solution.py:16
  190.0 10.4 %collective-permute-start = (bf16[256,128]{1,0:T(8,128)(2,1)S(1)}, bf16[256,128]{1,0:T(8,128)(2,1)S(1)}, u32[]{:S(2)}, u32[]{:S(2)}) collective-permute-start(bf16[256,128]{1,0:T(8,128)(2,1)S(1)} %get-tuple-element.343), channel_id=1, source_target_pairs={{0,8},{8,16},{16,24},{24,32},{32,40},{40,48},{48,56},{56,64},{64,7... | collective-permute-start | bytes 196616 | tf_op jit(solution)/shard_map/while/body/eval_jaxpr/ppermute | solution.py:16
  (22 other events, 100.6 us)
Sparse Core Ops, SparseCore 0:
  207.4 71.4 reduce-scatter.1
where the time goes:
time: 287 us; the launch traced here: 286 us
  starting transfers between devices  163 us (57%)
  waiting for transfers between devices  79.8 us (28%)
  matrix products  19.8 us (7%)
  between operations  13.5 us (5%)
  other arithmetic  4.44 us (2%)
  local copies, waits for them, and re-layouts  3.33 us (1%)
    ppermute x45, starting transfers between devices, shifted(): return lax.ppermute(value, axis, pairs)  163 us
    reduce_scatter x1, waiting for transfers between devices, per_device(): lax.psum_scatter(lax.dot_general(out_weight, attended, (((0,), (1,)), (()...  71.6 us
    ppermute x45, waiting for transfers between devices, shifted(): return lax.ppermute(value, axis, pairs)  8.23 us
    dot_general x16, matrix products, attend(): jnp.einsum('gqk,kgd->gqd', weights.astype(jnp.bfloat16), values_here, pre...  7.76 us
    dot_general x16, matrix products, attend(): jnp.einsum('gqd,kgd->gqk', query_mat, keys_here, preferred_element_type=j...  7.24 us
  transfers between devices with their start and end apart: 46, of which 16 were waited for; matrix products, arithmetic and copies ran while one was open for 4% of the time, Pallas kernels for 0%

commit v1 on v0

v1 whole, which is shorter than its diff:
```python
import functools
import math

import jax
import jax.numpy as jnp
from jax import lax
from jax.experimental import pallas as pl
from jax.experimental.pallas import tpu as pltpu
from jax.sharding import PartitionSpec as P

HEAD_DIM = 128
GROUP = 4
TOK = 256
MARK = 16
PIECE = TOK + MARK
COLS = GROUP * HEAD_DIM
BLOCKS = 8
HIDDEN = -1e30
SCORE_SCALE = math.log2(math.e) / math.sqrt(HEAD_DIM)


def attend_stage(first, final, counts, *refs):
    refs = list(refs)
    place = refs.pop(0) if final else None
    q_ref, mark_ref = refs[:2]
    refs = refs[2:]
    pieces, refs = refs[: len(counts)], refs[len(counts):]
    if not first:
        top_ref, sum_ref, acc_ref = refs[:3]
        refs = refs[3:]
    if final:
        weight_ref, send_ref, keep_ref, done_ref = refs
    else:
        top_out, sum_out, acc_out = refs

    marks = jnp.broadcast_to(mark_ref[...], (TOK, TOK))
    for h in range(GROUP):
        cols = slice(h * HEAD_DIM, (h + 1) * HEAD_DIM)
        query = q_ref[:, cols]
        scored = []
        for ref, count in zip(pieces, counts):
            for n in range(count):
                row = n * PIECE
                key = ref[row : row + TOK, :HEAD_DIM]
                value = ref[row : row + TOK, HEAD_DIM:]
                key_mark = ref[row + TOK : row + PIECE, :].astype(jnp.float32)[:1]
                score = lax.dot_general(
                    query, key, (((1,), (1,)), ((), ())), preferred_element_type=jnp.float32
                )
                allowed = marks == key_mark
                if first and not scored:
                    down = lax.broadcasted_iota(jnp.int32, (TOK, TOK), 0)
                    across = lax.broadcasted_iota(jnp.int32, (TOK, TOK), 1)
                    allowed = allowed & (across <= down)
                scored.append((jnp.where(allowed, score * SCORE_SCALE, HIDDEN), value))
        highest = None
        for score, _ in scored:
            half = jnp.maximum(score[:, :HEAD_DIM], score[:, HEAD_DIM:])
            highest = half if highest is None else jnp.maximum(highest, half)
        top = jnp.max(highest, axis=1, keepdims=True)
        if not first:
            top = jnp.maximum(top, top_ref[:, h : h + 1])
        total = product = None
        for score, value in scored:
            weight = jnp.exp2(score - top)
            part = weight[:, :HEAD_DIM] + weight[:, HEAD_DIM:]
            total = part if total is None else total + part
            term = jnp.dot(weight.astype(jnp.bfloat16), value, preferred_element_type=jnp.float32)
            product = term if product is None else product + term
        if not first:
            factor = jnp.exp2(top_ref[:, h : h + 1] - top)
            total = total + sum_ref[:, cols] * factor
            product = product + acc_ref[:, cols] * factor
        if final:
            whole = jnp.sum(total, axis=1, keepdims=True)
            done_ref[:, cols] = (product / whole).astype(jnp.bfloat16)
        else:
            top_out[:, h : h + 1] = top
            sum_out[:, cols] = total
            acc_out[:, cols] = product
    if final:
        row, core = place[0], place[1]
        for turn in range(BLOCKS // 2):
            for side in range(2):
                block = lax.rem(row + turn, BLOCKS // 2) * 2 + (core if side else 1 - core)
                cols = pl.ds(pl.multiple_of(block * COLS, COLS), COLS)
                share = jnp.dot(
                    done_ref[...], weight_ref[:, cols], preferred_element_type=jnp.float32
                )
                (keep_ref if side else send_ref)[turn] = share.astype(jnp.bfloat16)


def run_stage(queries, marks, pieces, state=None, weight=None, place=None):
    first, final = state is None, weight is not None
    counts = tuple(p.shape[0] // PIECE for p in pieces)
    total = sum(counts)
    vmem = pl.BlockSpec(memory_space=pltpu.VMEM)
    args = ([place] if final else []) + [queries, marks, *pieces] + ([] if first else list(state))
    in_specs = [vmem] * len(args)
    scratch = []
    if final:
        in_specs[0] = pl.BlockSpec(memory_space=pltpu.SMEM)
        args.append(weight)
        in_specs.append(vmem)
        shape = jax.ShapeDtypeStruct((BLOCKS // 2, TOK, COLS), jnp.bfloat16)
        out_shape = [shape, shape]
        scratch = [pltpu.VMEM((TOK, COLS), jnp.bfloat16)]
    else:
        out_shape = [
            jax.ShapeDtypeStruct((TOK, GROUP), jnp.float32),
            jax.ShapeDtypeStruct((TOK, COLS), jnp.float32),
            jax.ShapeDtypeStruct((TOK, COLS), jnp.float32),
        ]
    flops = 4 * TOK * TOK * COLS * total + (2 * TOK * COLS * COLS * BLOCKS if final else 0)
    return pl.pallas_call(
        functools.partial(attend_stage, first, final, counts),
        out_shape=out_shape,
        in_specs=in_specs,
        out_specs=[vmem] * len(out_shape),
        scratch_shapes=scratch,
        compiler_params=pltpu.CompilerParams(vmem_limit_bytes=40 << 20),
        cost_estimate=pl.CostEstimate(
            flops=flops,
            bytes_accessed=total * PIECE * TOK * 2 + (8 << 20 if final else 2 << 20),
            transcendentals=total * GROUP * TOK * TOK,
        ),
    )(*args)


def along(value, by):
    size = lax.axis_size("tok")
    return lax.ppermute(value, "tok", [(i, (i + by) % size) for i in range(size)])


def around(value, by):
    size = lax.axis_size("head")
    return lax.ppermute(value, "head", [(i, (i + by) % size) for i in range(size)])


def per_device(queries, key_heads, value_heads, doc_ids, out_weight):
    marks = (doc_ids + 1).astype(jnp.float32)
    mark_rows = jnp.broadcast_to(marks.astype(jnp.bfloat16)[None], (MARK, TOK))
    own = jnp.concatenate([jnp.concatenate([key_heads, value_heads], axis=1), mark_rows], axis=0)
    marks = marks[:, None]
    place = jnp.stack([lax.axis_index("head"), lax.axis_index("srv")]).astype(jnp.int32)

    back5 = along(own, 5)
    ahead = jnp.concatenate([own, back5])
    back10 = along(back5, 5)
    near1, near2 = along(ahead, 1), along(ahead, 2)
    state = run_stage(queries, marks, [own, back5])
    behind = jnp.concatenate([back5, back10])
    back15 = along(back10, 5)
    under1, under2 = along(behind, -1), along(behind, -2)
    over1, over2 = along(back10, 1), along(back10, 2)
    state = run_stage(queries, marks, [near1, near2, back10], state)
    state = run_stage(queries, marks, [under1, under2, over1, over2], state)
    last1, last2 = along(back15, -1), along(back15, -2)
    send, keep = run_stage(queries, marks, [back15, last1, last2], state, out_weight, place)

    other = lax.ppermute(send, "srv", [(0, 1), (1, 0)])
    pair = (keep.astype(jnp.float32) + other.astype(jnp.float32)).astype(jnp.bfloat16)
    parts = [pair[0], around(pair[1], 1), around(pair[2], 2), around(pair[3], 3)]
    summed = parts[0].astype(jnp.float32)
    for part in parts[1:]:
        summed = summed + part.astype(jnp.float32)
    return summed.astype(jnp.bfloat16)


def solution(mesh):
    placed = (
        P("tok", ("head", "srv")),
        P("tok", ("head", "srv")),
        P("tok", ("head", "srv")),
        P("tok"),
        P(("head", "srv"), None),
    )
    return jax.shard_map(
        per_device, mesh=mesh, in_specs=placed, out_specs=P("tok", ("head", "srv")), check_vma=False
    )
```

time: 287 us -> 143 us (0.50)
  starting transfers between devices: 163 us -> 86.9 us
  waiting for transfers between devices: 79.8 us -> 36.5 us
  matrix products: 19.8 us -> 0 us
  between operations: 13.5 us -> 0.29 us
  Pallas kernels: 0 us -> 12.5 us
    ppermute x45 -> x15, starting transfers between devices: 163 us -> 86.9 us  [the longest x11 71.1 us: along(): lax.ppermute(value, 'tok', [(i, (i + by) % size) for i in range(size)])]
    reduce_scatter x1 -> x0, waiting for transfers between devices: 71.6 us -> none  [per_device(): lax.psum_scatter(lax.dot_general(out_weight, attended, (((0,), (1,)), (()...]
    ppermute x45 -> x15, waiting for transfers between devices: 8.23 us -> 36.5 us  [the longest x11 26.4 us: along(): lax.ppermute(value, 'tok', [(i, (i + by) % size) for i in range(size)])]
    dot_general x33 -> x0, matrix products: 19.8 us -> none  [the longest x16 7.76 us: attend(): jnp.einsum('gqk,kgd->gqd', weights.astype(jnp.bfloat16), values_here, pre...]
    pallas_call x0 -> x4, Pallas kernels: none -> 12.5 us  [run_stage(): pl.pallas_call(functools.partial(attend_stage, first, final, counts), out...]
  transfers between devices with their start and end apart: 46 -> 15, of which waited for: 16 -> 8; matrix products, arithmetic and copies ran while one was open for 4% -> 0% of each run, Pallas kernels for 0% -> 6%
where the time goes in v1:
time: 143 us; the launch traced here: 141 us
  starting transfers between devices  86.9 us (61%)
  waiting for transfers between devices  36.5 us (26%)
  Pallas kernels  12.5 us (9%)
  local copies, waits for them, and re-layouts  2.87 us (2%)
  other arithmetic  1.93 us (1%)
    ppermute x11, starting transfers between devices, along(): lax.ppermute(value, 'tok', [(i, (i + by) % size) for i in range(size)])  71.1 us
    ppermute x11, waiting for transfers between devices, along(): lax.ppermute(value, 'tok', [(i, (i + by) % size) for i in range(size)])  26.4 us
    pallas_call x4, Pallas kernels, run_stage(): pl.pallas_call(functools.partial(attend_stage, first, final, counts), out...  12.5 us
    ppermute x3, starting transfers between devices, around(): lax.ppermute(value, 'head', [(i, (i + by) % size) for i in range(size)])  10.7 us
    ppermute x3, waiting for transfers between devices, around(): lax.ppermute(value, 'head', [(i, (i + by) % size) for i in range(size)])  7.83 us
    ppermute x1, starting transfers between devices, per_device(): other = lax.ppermute(send, 'srv', [(0, 1), (1, 0)])  5.09 us
  transfers between devices with their start and end apart: 15, of which 8 were waited for; matrix products, arithmetic and copies ran while one was open for 0% of the time, Pallas kernels for 6%

profile of v1, /device:TPU:1, one launch (start us, length us, event | category | flops | bytes accessed | tf_op | source)
XLA Modules:
  0.0 141.0 jit_solution(10841609593159069903)
XLA Ops:
  2.4 11.0 %collective-permute-start = (bf16[272,256]{1,0:T(8,128)(2,1)S(1)}, bf16[272,256]{1,0:T(8,128)(2,1)S(1)}, u32[]{:S(2)}, u32[]{:S(2)}) collective-permute-start(bf16[272,256]{1,0:T(8,128)(2,1)S(1)} %pad_maximum_fusion.1.refs_2_), channel_id=1, source_target_pairs={{0,40},{8,48},{16,56},{24,64},{32,72},{40,80},{48,88},{56,96},{64,... | collective-permute-start | bytes 417800 | tf_op jit(solution)/shard_map/ppermute | solution.py:132
  13.4 16.1 %collective-permute-done.refs_3_ = bf16[272,256]{1,0:T(8,128)(2,1)S(1)} collective-permute-done((bf16[272,256]{1,0:T(8,128)(2,1)S(1)}, bf16[272,256]{1,0:T(8,128)(2,1)S(1)}, u32[]{:S(2)}, u32[]{:S(2)}) %collective-permute-start) | collective-permute-done | bytes 139296 | tf_op jit(solution)/shard_map/ppermute | solution.py:132
  29.6 8.6 %collective-permute-start.1 = (bf16[272,256]{1,0:T(8,128)(2,1)S(1)}, bf16[272,256]{1,0:T(8,128)(2,1)S(1)}, u32[]{:S(2)}, u32[]{:S(2)}) collective-permute-start(bf16[272,256]{1,0:T(8,128)(2,1)S(1)} %collective-permute-done.refs_3_), channel_id=1, source_target_pairs={{0,40},{8,48},{16,56},{24,64},{32,72},{40,80},{48,88},{56,96},{64,... | collective-permute-start | bytes 417800 | tf_op jit(solution)/shard_map/ppermute | solution.py:132
  38.2 5.3 %collective-permute-start.10 = (bf16[544,256]{1,0:T(8,128)(2,1)S(1)}, bf16[544,256]{1,0:T(8,128)(2,1)S(1)}, u32[]{:S(2)}, u32[]{:S(2)}) collective-permute-start(bf16[544,256]{1,0:T(8,128)(2,1)S(1)} %pad_maximum_fusion), channel_id=1, source_target_pairs={{0,16},{8,24},{16,32},{24,40},{32,48},{40,56},{48,64},{56,72},{64,... | collective-permute-start | bytes 835592 | tf_op jit(solution)/shard_map/ppermute | solution.py:132
  43.5 2.5 %collective-permute-start.9 = (bf16[544,256]{1,0:T(8,128)(2,1)S(1)}, bf16[544,256]{1,0:T(8,128)(2,1)S(1)}, u32[]{:S(2)}, u32[]{:S(2)}) collective-permute-start(bf16[544,256]{1,0:T(8,128)(2,1)S(1)} %pad_maximum_fusion), channel_id=1, source_target_pairs={{0,8},{8,16},{16,24},{24,32},{32,40},{40,48},{48,56},{56,64},{64,7... | collective-permute-start | bytes 835592 | tf_op jit(solution)/shard_map/ppermute | solution.py:132
  46.0 1.7 %collective-permute-done.1.refs_4_ = bf16[272,256]{1,0:T(8,128)(2,1)S(1)} collective-permute-done((bf16[272,256]{1,0:T(8,128)(2,1)S(1)}, bf16[272,256]{1,0:T(8,128)(2,1)S(1)}, u32[]{:S(2)}, u32[]{:S(2)}) %collective-permute-start.1) | collective-permute-done | bytes 139296 | tf_op jit(solution)/shard_map/ppermute | solution.py:132
  47.7 17.2 %collective-permute-start.5 = (bf16[544,256]{1,0:T(8,128)(2,1)S(1)}, bf16[544,256]{1,0:T(8,128)(2,1)S(1)}, u32[]{:S(2)}, u32[]{:S(2)}) collective-permute-start(bf16[544,256]{1,0:T(8,128)(2,1)S(1)} %constant_dynamic-update-slice_fusion.2), channel_id=1, source_target_pairs={{0,1016},{8,0},{16,8},{24,16},{32,24},{40,32},{48,40},{56,48},{64,... | collective-permute-start | bytes 835592 | tf_op jit(solution)/shard_map/ppermute | solution.py:132
  65.0 1.9 %collective-permute-start.6 = (bf16[544,256]{1,0:T(8,128)(2,1)S(1)}, bf16[544,256]{1,0:T(8,128)(2,1)S(1)}, u32[]{:S(2)}, u32[]{:S(2)}) collective-permute-start(bf16[544,256]{1,0:T(8,128)(2,1)S(1)} %constant_dynamic-update-slice_fusion.2), channel_id=1, source_target_pairs={{0,1008},{8,1016},{16,0},{24,8},{32,16},{40,24},{48,32},{56,40},{6... | collective-permute-start | bytes 835592 | tf_op jit(solution)/shard_map/ppermute | solution.py:132
  66.9 6.9 %collective-permute-start.2 = (bf16[272,256]{1,0:T(8,128)(2,1)S(1)}, bf16[272,256]{1,0:T(8,128)(2,1)S(1)}, u32[]{:S(2)}, u32[]{:S(2)}) collective-permute-start(bf16[272,256]{1,0:T(8,128)(2,1)S(1)} %collective-permute-done.1.refs_4_), channel_id=1, source_target_pairs={{0,40},{8,48},{16,56},{24,64},{32,72},{40,80},{48,88},{56,96},{64,... | collective-permute-start | bytes 417800 | tf_op jit(solution)/shard_map/ppermute | solution.py:132
  73.8 3.1 %collective-permute-start.7 = (bf16[272,256]{1,0:T(8,128)(2,1)S(1)}, bf16[272,256]{1,0:T(8,128)(2,1)S(1)}, u32[]{:S(2)}, u32[]{:S(2)}) collective-permute-start(bf16[272,256]{1,0:T(8,128)(2,1)S(1)} %collective-permute-done.1.refs_4_), channel_id=1, source_target_pairs={{0,8},{8,16},{16,24},{24,32},{32,40},{40,48},{48,56},{56,64},{64,7... | collective-permute-start | bytes 417800 | tf_op jit(solution)/shard_map/ppermute | solution.py:132
  76.9 5.4 %collective-permute-done.9.refs_2_ = bf16[544,256]{1,0:T(8,128)(2,1)S(1)} collective-permute-done((bf16[544,256]{1,0:T(8,128)(2,1)S(1)}, bf16[544,256]{1,0:T(8,128)(2,1)S(1)}, u32[]{:S(2)}, u32[]{:S(2)}) %collective-permute-start.9) | collective-permute-done | bytes 278560 | tf_op jit(solution)/shard_map/ppermute | solution.py:132
  82.3 1.9 %collective-permute-start.8 = (bf16[272,256]{1,0:T(8,128)(2,1)S(1)}, bf16[272,256]{1,0:T(8,128)(2,1)S(1)}, u32[]{:S(2)}, u32[]{:S(2)}) collective-permute-start(bf16[272,256]{1,0:T(8,128)(2,1)S(1)} %collective-permute-done.1.refs_4_), channel_id=1, source_target_pairs={{0,16},{8,24},{16,32},{24,40},{32,48},{40,56},{48,64},{56,72},{64,... | collective-permute-start | bytes 417800 | tf_op jit(solution)/shard_map/ppermute | solution.py:132
  85.0 10.8 %collective-permute-start.3 = (bf16[272,256]{1,0:T(8,128)(2,1)S(1)}, bf16[272,256]{1,0:T(8,128)(2,1)S(1)}, u32[]{:S(2)}, u32[]{:S(2)}) collective-permute-start(bf16[272,256]{1,0:T(8,128)(2,1)S(1)} %collective-permute-done.2.refs_3_), channel_id=1, source_target_pairs={{0,1016},{8,0},{16,8},{24,16},{32,24},{40,32},{48,40},{56,48},{64,... | collective-permute-start | bytes 417800 | tf_op jit(solution)/shard_map/ppermute | solution.py:132
  95.8 2.6 %collective-permute-done.7.refs_4_ = bf16[272,256]{1,0:T(8,128)(2,1)S(1)} collective-permute-done((bf16[272,256]{1,0:T(8,128)(2,1)S(1)}, bf16[272,256]{1,0:T(8,128)(2,1)S(1)}, u32[]{:S(2)}, u32[]{:S(2)}) %collective-permute-start.7) | collective-permute-done | bytes 139296 | tf_op jit(solution)/shard_map/ppermute | solution.py:132
  98.4 1.9 %collective-permute-start.4 = (bf16[272,256]{1,0:T(8,128)(2,1)S(1)}, bf16[272,256]{1,0:T(8,128)(2,1)S(1)}, u32[]{:S(2)}, u32[]{:S(2)}) collective-permute-start(bf16[272,256]{1,0:T(8,128)(2,1)S(1)} %collective-permute-done.2.refs_3_), channel_id=1, source_target_pairs={{0,1008},{8,1016},{16,0},{24,8},{32,16},{40,24},{48,32},{56,40},{6... | collective-permute-start | bytes 417800 | tf_op jit(solution)/shard_map/ppermute | solution.py:132
  102.7 3.2 %shard_map.56 = (f32[256,4]{1,0:T(8,128)S(1)}, f32[256,512]{1,0:T(8,128)S(1)}, f32[256,512]{1,0:T(8,128)S(1)}) custom-call(bf16[256,512]{1,0:T(8,128)(2,1)S(1)} %copy-done.1, f32[256,1]{1,0:T(8,128)S(1)} %copy.9.refs_1_.refs_2_, bf16[544,256]{1,0:T(8,128)(2,1)S(1)} %collective-permute-done.9.refs_2_, bf16[544,256]{1,0:T(8,128)(2,1)S(1)} %collective-permute-done.10.refs_3_, ...), custom_call_target="tpu_custom_call" | custom-call | flops 671088640 | bytes 2793472 | tf_op jit(solution)/shard_map/pallas_call | solution.py:115
  106.0 3.5 %shard_map.57 = (f32[256,4]{1,0:T(8,128)S(1)}, f32[256,512]{1,0:T(8,128)S(1)}, f32[256,512]{1,0:T(8,128)S(1)}) custom-call(bf16[256,512]{1,0:T(8,128)(2,1)S(1)} %copy-done.1, f32[256,1]{1,0:T(8,128)S(1)} %copy.9.refs_1_.refs_2_, bf16[544,256]{1,0:T(8,128)(2,1)S(1)} %collective-permute-done.5.refs_2_, bf16[544,256]{1,0:T(8,128)(2,1)S(1)} %collective-permute-done.6.refs_3_, ...), custom_call_target="tpu_custom_call" | custom-call | flops 805306368 | bytes 2932736 | tf_op jit(solution)/shard_map/pallas_call | solution.py:115
  109.5 4.3 %shard_map.58 = (bf16[4,256,512]{2,1,0:T(8,128)(2,1)S(1)}, bf16[4,256,512]{2,1,0:T(8,128)(2,1)S(1)}) custom-call(s32[2]{0:T(128)S(1)} %pad_add_fusion.refs_0_, bf16[256,512]{1,0:T(8,128)(2,1)S(1)} %copy-done.1, f32[256,1]{1,0:T(8,128)S(1)} %copy.9.refs_1_.refs_2_, bf16[272,256]{1,0:T(8,128)(2,1)S(1)} %collective-permute-done.2.refs_3_, ...), custom_call_target="tpu_custom_call" | custom-call | flops 1476395008 | bytes 8806400 | tf_op jit(solution)/shard_map/pallas_call | solution.py:115
  113.9 5.1 %collective-permute-start.11 = (bf16[4,256,512]{2,1,0:T(8,128)(2,1)S(1)}, bf16[4,256,512]{2,1,0:T(8,128)(2,1)S(1)}, u32[]{:S(2)}, u32[]{:S(2)}) collective-permute-start(bf16[4,256,512]{2,1,0:T(8,128)(2,1)S(1)} %get-tuple-element.26), channel_id=1, source_target_pairs={{0,1},{1,0},{2,3},{3,2},{4,5},{5,4},{6,7},{7,6},{8,9},{9,8},{10,11... | collective-permute-start | bytes 3145736 | tf_op jit(solution)/shard_map/ppermute | solution.py:161
  119.0 2.3 %collective-permute-done.11 = bf16[4,256,512]{2,1,0:T(8,128)(2,1)S(1)} collective-permute-done((bf16[4,256,512]{2,1,0:T(8,128)(2,1)S(1)}, bf16[4,256,512]{2,1,0:T(8,128)(2,1)S(1)}, u32[]{:S(2)}, u32[]{:S(2)}) %collective-permute-start.11) | collective-permute-done | bytes 1048608 | tf_op jit(solution)/shard_map/ppermute | solution.py:161
  121.6 3.2 %collective-permute-start.12 = (bf16[256,512]{1,0:T(8,128)(2,1)S(1)}, bf16[256,512]{1,0:T(8,128)(2,1)S(1)}, u32[]{:S(2)}, u32[]{:S(2)}) collective-permute-start(bf16[256,512]{1,0:T(8,128)(2,1)S(1)} %get-tuple-element.27), channel_id=1, source_target_pairs={{0,2},{2,4},{4,6},{6,0},{1,3},{3,5},{5,7},{7,1},{8,10},{10,12},{12... | collective-permute-start | bytes 786440 | tf_op jit(solution)/shard_map/ppermute | solution.py:137
  124.8 4.5 %collective-permute-start.13 = (bf16[256,512]{1,0:T(8,128)(2,1)S(1)}, bf16[256,512]{1,0:T(8,128)(2,1)S(1)}, u32[]{:S(2)}, u32[]{:S(2)}) collective-permute-start(bf16[256,512]{1,0:T(8,128)(2,1)S(1)} %get-tuple-element.29), channel_id=1, source_target_pairs={{0,4},{2,6},{4,0},{6,2},{1,5},{3,7},{5,1},{7,3},{8,12},{10,14},{12... | collective-permute-start | bytes 786440 | tf_op jit(solution)/shard_map/ppermute | solution.py:137
  129.3 3.0 %collective-permute-start.14 = (bf16[256,512]{1,0:T(8,128)(2,1)S(1)}, bf16[256,512]{1,0:T(8,128)(2,1)S(1)}, u32[]{:S(2)}, u32[]{:S(2)}) collective-permute-start(bf16[256,512]{1,0:T(8,128)(2,1)S(1)} %get-tuple-element.28), channel_id=1, source_target_pairs={{0,6},{2,0},{4,2},{6,4},{1,7},{3,1},{5,3},{7,5},{8,14},{10,8},{12,... | collective-permute-start | bytes 786440 | tf_op jit(solution)/shard_map/ppermute | solution.py:137
  132.4 6.7 %collective-permute-done.13 = bf16[256,512]{1,0:T(8,128)(2,1)S(1)} collective-permute-done((bf16[256,512]{1,0:T(8,128)(2,1)S(1)}, bf16[256,512]{1,0:T(8,128)(2,1)S(1)}, u32[]{:S(2)}, u32[]{:S(2)}) %collective-permute-start.13) | collective-permute-done | bytes 262176 | tf_op jit(solution)/shard_map/ppermute | solution.py:137
  (27 shorter events, 7.9 us)
Async XLA Ops:
  2.4 27.2 %collective-permute-start = (bf16[272,256]{1,0:T(8,128)(2,1)S(1)}, bf16[272,256]{1,0:T(8,128)(2,1)S(1)}, u32[]{:S(2)}, u32[]{:S(2)}) collective-permute-start(bf16[272,256]{1,0:T(8,128)(2,1)S(1)} %pad_maximum_fusion.1.refs_2_), channel_id=1, source_target_pairs={{0,40},{8,48},{16,56},{24,64},{32,72},{40,80},{48,88},{56,96},{64,... | collective-permute-start | bytes 417800 | tf_op jit(solution)/shard_map/ppermute | solution.py:132
  29.6 18.1 %collective-permute-start.1 = (bf16[272,256]{1,0:T(8,128)(2,1)S(1)}, bf16[272,256]{1,0:T(8,128)(2,1)S(1)}, u32[]{:S(2)}, u32[]{:S(2)}) collective-permute-start(bf16[272,256]{1,0:T(8,128)(2,1)S(1)} %collective-permute-done.refs_3_), channel_id=1, source_target_pairs={{0,40},{8,48},{16,56},{24,64},{32,72},{40,80},{48,88},{56,96},{64,... | collective-permute-start | bytes 417800 | tf_op jit(solution)/shard_map/ppermute | solution.py:132
  38.2 35.6 %collective-permute-start.10 = (bf16[544,256]{1,0:T(8,128)(2,1)S(1)}, bf16[544,256]{1,0:T(8,128)(2,1)S(1)}, u32[]{:S(2)}, u32[]{:S(2)}) collective-permute-start(bf16[544,256]{1,0:T(8,128)(2,1)S(1)} %pad_maximum_fusion), channel_id=1, source_target_pairs={{0,16},{8,24},{16,32},{24,40},{32,48},{40,56},{48,64},{56,72},{64,... | collective-permute-start | bytes 835592 | tf_op jit(solution)/shard_map/ppermute | solution.py:132
  43.5 38.8 %collective-permute-start.9 = (bf16[544,256]{1,0:T(8,128)(2,1)S(1)}, bf16[544,256]{1,0:T(8,128)(2,1)S(1)}, u32[]{:S(2)}, u32[]{:S(2)}) collective-permute-start(bf16[544,256]{1,0:T(8,128)(2,1)S(1)} %pad_maximum_fusion), channel_id=1, source_target_pairs={{0,8},{8,16},{16,24},{24,32},{32,40},{40,48},{48,56},{56,64},{64,7... | collective-permute-start | bytes 835592 | tf_op jit(solution)/shard_map/ppermute | solution.py:132
  47.7 58.3 %collective-permute-start.5 = (bf16[544,256]{1,0:T(8,128)(2,1)S(1)}, bf16[544,256]{1,0:T(8,128)(2,1)S(1)}, u32[]{:S(2)}, u32[]{:S(2)}) collective-permute-start(bf16[544,256]{1,0:T(8,128)(2,1)S(1)} %constant_dynamic-update-slice_fusion.2), channel_id=1, source_target_pairs={{0,1016},{8,0},{16,8},{24,16},{32,24},{40,32},{48,40},{56,48},{64,... | collective-permute-start | bytes 835592 | tf_op jit(solution)/shard_map/ppermute | solution.py:132
  65.0 41.0 %collective-permute-start.6 = (bf16[544,256]{1,0:T(8,128)(2,1)S(1)}, bf16[544,256]{1,0:T(8,128)(2,1)S(1)}, u32[]{:S(2)}, u32[]{:S(2)}) collective-permute-start(bf16[544,256]{1,0:T(8,128)(2,1)S(1)} %constant_dynamic-update-slice_fusion.2), channel_id=1, source_target_pairs={{0,1008},{8,1016},{16,0},{24,8},{32,16},{40,24},{48,32},{56,40},{6... | collective-permute-start | bytes 835592 | tf_op jit(solution)/shard_map/ppermute | solution.py:132
  66.9 18.1 %collective-permute-start.2 = (bf16[272,256]{1,0:T(8,128)(2,1)S(1)}, bf16[272,256]{1,0:T(8,128)(2,1)S(1)}, u32[]{:S(2)}, u32[]{:S(2)}) collective-permute-start(bf16[272,256]{1,0:T(8,128)(2,1)S(1)} %collective-permute-done.1.refs_4_), channel_id=1, source_target_pairs={{0,40},{8,48},{16,56},{24,64},{32,72},{40,80},{48,88},{56,96},{64,... | collective-permute-start | bytes 417800 | tf_op jit(solution)/shard_map/ppermute | solution.py:132
  73.8 24.6 %collective-permute-start.7 = (bf16[272,256]{1,0:T(8,128)(2,1)S(1)}, bf16[272,256]{1,0:T(8,128)(2,1)S(1)}, u32[]{:S(2)}, u32[]{:S(2)}) collective-permute-start(bf16[272,256]{1,0:T(8,128)(2,1)S(1)} %collective-permute-done.1.refs_4_), channel_id=1, source_target_pairs={{0,8},{8,16},{16,24},{24,32},{32,40},{40,48},{48,56},{56,64},{64,7... | collective-permute-start | bytes 417800 | tf_op jit(solution)/shard_map/ppermute | solution.py:132
  82.3 23.6 %collective-permute-start.8 = (bf16[272,256]{1,0:T(8,128)(2,1)S(1)}, bf16[272,256]{1,0:T(8,128)(2,1)S(1)}, u32[]{:S(2)}, u32[]{:S(2)}) collective-permute-start(bf16[272,256]{1,0:T(8,128)(2,1)S(1)} %collective-permute-done.1.refs_4_), channel_id=1, source_target_pairs={{0,16},{8,24},{16,32},{24,40},{32,48},{40,56},{48,64},{56,72},{64,... | collective-permute-start | bytes 417800 | tf_op jit(solution)/shard_map/ppermute | solution.py:132
  85.0 24.5 %collective-permute-start.3 = (bf16[272,256]{1,0:T(8,128)(2,1)S(1)}, bf16[272,256]{1,0:T(8,128)(2,1)S(1)}, u32[]{:S(2)}, u32[]{:S(2)}) collective-permute-start(bf16[272,256]{1,0:T(8,128)(2,1)S(1)} %collective-permute-done.2.refs_3_), channel_id=1, source_target_pairs={{0,1016},{8,0},{16,8},{24,16},{32,24},{40,32},{48,40},{56,48},{64,... | collective-permute-start | bytes 417800 | tf_op jit(solution)/shard_map/ppermute | solution.py:132
  98.4 11.1 %collective-permute-start.4 = (bf16[272,256]{1,0:T(8,128)(2,1)S(1)}, bf16[272,256]{1,0:T(8,128)(2,1)S(1)}, u32[]{:S(2)}, u32[]{:S(2)}) collective-permute-start(bf16[272,256]{1,0:T(8,128)(2,1)S(1)} %collective-permute-done.2.refs_3_), channel_id=1, source_target_pairs={{0,1008},{8,1016},{16,0},{24,8},{32,16},{40,24},{48,32},{56,40},{6... | collective-permute-start | bytes 417800 | tf_op jit(solution)/shard_map/ppermute | solution.py:132
  100.3 1.0 copy-start.1
  102.7 6.8 %copy-start = (bf16[512,4096]{1,0:T(8,128)(2,1)S(1)}, bf16[512,4096]{1,0:T(8,128)(2,1)}, u32[]{:S(2)}) copy-start(bf16[512,4096]{1,0:T(8,128)(2,1)} %refs_9_.1) | copy-start | bytes 12582916
  113.9 7.4 %collective-permute-start.11 = (bf16[4,256,512]{2,1,0:T(8,128)(2,1)S(1)}, bf16[4,256,512]{2,1,0:T(8,128)(2,1)S(1)}, u32[]{:S(2)}, u32[]{:S(2)}) collective-permute-start(bf16[4,256,512]{2,1,0:T(8,128)(2,1)S(1)} %get-tuple-element.26), channel_id=1, source_target_pairs={{0,1},{1,0},{2,3},{3,2},{4,5},{5,4},{6,7},{7,6},{8,9},{9,8},{10,11... | collective-permute-start | bytes 3145736 | tf_op jit(solution)/shard_map/ppermute | solution.py:161
  121.6 10.8 %collective-permute-start.12 = (bf16[256,512]{1,0:T(8,128)(2,1)S(1)}, bf16[256,512]{1,0:T(8,128)(2,1)S(1)}, u32[]{:S(2)}, u32[]{:S(2)}) collective-permute-start(bf16[256,512]{1,0:T(8,128)(2,1)S(1)} %get-tuple-element.27), channel_id=1, source_target_pairs={{0,2},{2,4},{4,6},{6,0},{1,3},{3,5},{5,7},{7,1},{8,10},{10,12},{12... | collective-permute-start | bytes 786440 | tf_op jit(solution)/shard_map/ppermute | solution.py:137
  124.8 14.3 %collective-permute-start.13 = (bf16[256,512]{1,0:T(8,128)(2,1)S(1)}, bf16[256,512]{1,0:T(8,128)(2,1)S(1)}, u32[]{:S(2)}, u32[]{:S(2)}) collective-permute-start(bf16[256,512]{1,0:T(8,128)(2,1)S(1)} %get-tuple-element.29), channel_id=1, source_target_pairs={{0,4},{2,6},{4,0},{6,2},{1,5},{3,7},{5,1},{7,3},{8,12},{10,14},{12... | collective-permute-start | bytes 786440 | tf_op jit(solution)/shard_map/ppermute | solution.py:137
  129.3 10.8 %collective-permute-start.14 = (bf16[256,512]{1,0:T(8,128)(2,1)S(1)}, bf16[256,512]{1,0:T(8,128)(2,1)S(1)}, u32[]{:S(2)}, u32[]{:S(2)}) collective-permute-start(bf16[256,512]{1,0:T(8,128)(2,1)S(1)} %get-tuple-element.28), channel_id=1, source_target_pairs={{0,6},{2,0},{4,2},{6,4},{1,7},{3,1},{5,3},{7,5},{8,14},{10,8},{12,... | collective-permute-start | bytes 786440 | tf_op jit(solution)/shard_map/ppermute | solution.py:137

commit v2 on v1

--- a/solution.py
+++ b/solution.py
@@ -12,19 +12,21 @@
 GROUP = 4
 TOK = 256
 MARK = 16
+HALF = TOK // 2
 PIECE = TOK + MARK
 COLS = GROUP * HEAD_DIM
 BLOCKS = 8
 HIDDEN = -1e30
+EFFORT = 6
 SCORE_SCALE = math.log2(math.e) / math.sqrt(HEAD_DIM)
 
 
-def attend_stage(first, final, counts, *refs):
+def attend_stage(first, final, amount, layout, *refs):
     refs = list(refs)
     place = refs.pop(0) if final else None
     q_ref, mark_ref = refs[:2]
     refs = refs[2:]
-    pieces, refs = refs[: len(counts)], refs[len(counts):]
+    pieces, refs = refs[:amount], refs[amount:]
     if not first:
         top_ref, sum_ref, acc_ref = refs[:3]
         refs = refs[3:]
@@ -38,21 +40,21 @@
         cols = slice(h * HEAD_DIM, (h + 1) * HEAD_DIM)
         query = q_ref[:, cols]
         scored = []
-        for ref, count in zip(pieces, counts):
-            for n in range(count):
-                row = n * PIECE
-                key = ref[row : row + TOK, :HEAD_DIM]
-                value = ref[row : row + TOK, HEAD_DIM:]
-                key_mark = ref[row + TOK : row + PIECE, :].astype(jnp.float32)[:1]
-                score = lax.dot_general(
-                    query, key, (((1,), (1,)), ((), ())), preferred_element_type=jnp.float32
-                )
-                allowed = marks == key_mark
-                if first and not scored:
-                    down = lax.broadcasted_iota(jnp.int32, (TOK, TOK), 0)
-                    across = lax.broadcasted_iota(jnp.int32, (TOK, TOK), 1)
-                    allowed = allowed & (across <= down)
-                scored.append((jnp.where(allowed, score * SCORE_SCALE, HIDDEN), value))
+        for upper, row, lower, start in layout:
+            above = pieces[upper][row : row + HALF]
+            below = pieces[lower][start : start + HALF]
+            both = jnp.concatenate([above, below], axis=0)
+            key, value = both[:, :HEAD_DIM], both[:, HEAD_DIM:]
+            key_mark = pieces[lower][start + HALF : start + HALF + MARK].astype(jnp.float32)[:1]
+            score = lax.dot_general(
+                query, key, (((1,), (1,)), ((), ())), preferred_element_type=jnp.float32
+            )
+            allowed = marks == key_mark
+            if first and not scored:
+                down = lax.broadcasted_iota(jnp.int32, (TOK, TOK), 0)
+                across = lax.broadcasted_iota(jnp.int32, (TOK, TOK), 1)
+                allowed = allowed & (across <= down)
+            scored.append((jnp.where(allowed, score * SCORE_SCALE, HIDDEN), value))
         highest = None
         for score, _ in scored:
             half = jnp.maximum(score[:, :HEAD_DIM], score[:, HEAD_DIM:])
@@ -92,10 +94,18 @@
 
 def run_stage(queries, marks, pieces, state=None, weight=None, place=None):
     first, final = state is None, weight is not None
-    counts = tuple(p.shape[0] // PIECE for p in pieces)
-    total = sum(counts)
+    arrays, layout = [], []
+    for piece in pieces:
+        if isinstance(piece, tuple):
+            layout.append((len(arrays), 0, len(arrays) + 1, 0))
+            arrays.extend(piece)
+        else:
+            for row in range(0, piece.shape[0], PIECE):
+                layout.append((len(arrays), row, len(arrays), row + HALF))
+            arrays.append(piece)
+    total = len(layout)
     vmem = pl.BlockSpec(memory_space=pltpu.VMEM)
-    args = ([place] if final else []) + [queries, marks, *pieces] + ([] if first else list(state))
+    args = ([place] if final else []) + [queries, marks, *arrays] + ([] if first else list(state))
     in_specs = [vmem] * len(args)
     scratch = []
     if final:
@@ -111,9 +121,9 @@
             jax.ShapeDtypeStruct((TOK, COLS), jnp.float32),
             jax.ShapeDtypeStruct((TOK, COLS), jnp.float32),
         ]
-    flops = 4 * TOK * TOK * COLS * total + (2 * TOK * COLS * COLS * BLOCKS if final else 0)
+    flops = EFFORT * 4 * TOK * TOK * COLS * total + (2 * TOK * COLS * COLS * BLOCKS if final else 0)
     return pl.pallas_call(
-        functools.partial(attend_stage, first, final, counts),
+        functools.partial(attend_stage, first, final, len(arrays), tuple(layout)),
         out_shape=out_shape,
         in_specs=in_specs,
         out_specs=[vmem] * len(out_shape),
@@ -137,33 +147,53 @@
     return lax.ppermute(value, "head", [(i, (i + by) % size) for i in range(size)])
 
 
+def plus(one, other):
+    return (one.astype(jnp.float32) + other.astype(jnp.float32)).astype(jnp.bfloat16)
+
+
+def after(value, earlier):
+    return lax.optimization_barrier((value, earlier))
+
+
+def gather_and_attend(queries, marks, own, weight, place):
+    back8 = along(own, 8)
+    state = run_stage(queries, marks, [own])
+    back8, state = after(back8, state)
+    back12 = along(back8, 4)
+    back4 = along(back8, -4)
+    state = run_stage(queries, marks, [back8], state)
+    back12, state = after(back12, state)
+    far = jnp.concatenate([back8, back12])
+    near = jnp.concatenate([back4, back8])
+    back10_14 = along(far, 2)
+    back2_6 = along(near, -2)
+    back9_13 = along(far, 1)
+    back3_7 = along(near, -1)
+    state = run_stage(queries, marks, [back12, back4], state)
+    back10_14, state = after(back10_14, state)
+    back11_15 = along(back10_14, 1)
+    back1_5 = along(back2_6, -1)
+    state = run_stage(queries, marks, [back10_14, back2_6, back9_13, back3_7], state)
+    return run_stage(queries, marks, [back11_15, back1_5], state, weight, place)
+
+
+def join(key_ref, value_ref, mark_ref, joined_ref):
+    joined_ref[:TOK, :HEAD_DIM] = key_ref[...]
+    joined_ref[:TOK, HEAD_DIM:] = value_ref[...]
+    joined_ref[TOK:] = jnp.broadcast_to(mark_ref[...], (MARK, TOK)).astype(jnp.bfloat16)
+
+
 def per_device(queries, key_heads, value_heads, doc_ids, out_weight):
     marks = (doc_ids + 1).astype(jnp.float32)
-    mark_rows = jnp.broadcast_to(marks.astype(jnp.bfloat16)[None], (MARK, TOK))
-    own = jnp.concatenate([jnp.concatenate([key_heads, value_heads], axis=1), mark_rows], axis=0)
-    marks = marks[:, None]
+    own = pl.pallas_call(join, out_shape=jax.ShapeDtypeStruct((PIECE, TOK), jnp.bfloat16))(
+        key_heads, value_heads, marks[None]
+    )
     place = jnp.stack([lax.axis_index("head"), lax.axis_index("srv")]).astype(jnp.int32)
-
-    back5 = along(own, 5)
-    ahead = jnp.concatenate([own, back5])
-    back10 = along(back5, 5)
-    near1, near2 = along(ahead, 1), along(ahead, 2)
-    state = run_stage(queries, marks, [own, back5])
-    behind = jnp.concatenate([back5, back10])
-    back15 = along(back10, 5)
-    under1, under2 = along(behind, -1), along(behind, -2)
-    over1, over2 = along(back10, 1), along(back10, 2)
-    state = run_stage(queries, marks, [near1, near2, back10], state)
-    state = run_stage(queries, marks, [under1, under2, over1, over2], state)
-    last1, last2 = along(back15, -1), along(back15, -2)
-    send, keep = run_stage(queries, marks, [back15, last1, last2], state, out_weight, place)
-
-    other = lax.ppermute(send, "srv", [(0, 1), (1, 0)])
-    pair = (keep.astype(jnp.float32) + other.astype(jnp.float32)).astype(jnp.bfloat16)
-    parts = [pair[0], around(pair[1], 1), around(pair[2], 2), around(pair[3], 3)]
-    summed = parts[0].astype(jnp.float32)
-    for part in parts[1:]:
-        summed = summed + part.astype(jnp.float32)
+    send, keep = gather_and_attend(queries, marks[:, None], own, out_weight, place)
+    pair = plus(keep, lax.ppermute(send, "srv", [(0, 1), (1, 0)]))
+    summed = pair[0].astype(jnp.float32)
+    for turn in (2, 1, 3):
+        summed = summed + around(pair[turn], turn).astype(jnp.float32)
     return summed.astype(jnp.bfloat16)
 
 

time: 143 us -> 137 us (0.958)
  starting transfers between devices: 86.9 us -> 74 us
  waiting for transfers between devices: 36.5 us -> 40.1 us
  Pallas kernels: 12.5 us -> 15.2 us
    ppermute x11 -> x9, starting transfers between devices: 71.1 us -> 60.7 us  [along(): lax.ppermute(value, 'tok', [(i, (i + by) % size) for i in range(size)])]
    ppermute x11 -> x9, waiting for transfers between devices: 26.4 us -> 30.4 us  [along(): lax.ppermute(value, 'tok', [(i, (i + by) % size) for i in range(size)])]
    pallas_call x4 -> x6, Pallas kernels: 12.5 us -> 15.2 us  [the longest x5 13.7 us: run_stage(): pl.pallas_call(functools.partial(attend_stage, first, final, len(arrays),...]
    ppermute x1, starting transfers between devices: 5.09 us -> 3.28 us  [per_device(): pair = plus(keep, lax.ppermute(send, 'srv', [(0, 1), (1, 0)]))]
  transfers between devices with their start and end apart: 15 -> 13, of which waited for: 8 -> 8; matrix products, arithmetic and copies ran while one was open for 0% -> 1% of each run, Pallas kernels for 6% -> 7%
where the time goes in v2:
time: 137 us; the launch traced here: 136 us
  starting transfers between devices  74 us (54%)
  waiting for transfers between devices  40.1 us (29%)
  Pallas kernels  15.2 us (11%)
  local copies, waits for them, and re-layouts  4.07 us (3%)
  other arithmetic  2.51 us (2%)
    ppermute x9, starting transfers between devices, along(): lax.ppermute(value, 'tok', [(i, (i + by) % size) for i in range(size)])  60.7 us
    ppermute x9, waiting for transfers between devices, along(): lax.ppermute(value, 'tok', [(i, (i + by) % size) for i in range(size)])  30.4 us
    pallas_call x5, Pallas kernels, run_stage(): pl.pallas_call(functools.partial(attend_stage, first, final, len(arrays),...  13.7 us
    ppermute x3, starting transfers between devices, around(): lax.ppermute(value, 'head', [(i, (i + by) % size) for i in range(size)])  10.1 us
    ppermute x3, waiting for transfers between devices, around(): lax.ppermute(value, 'head', [(i, (i + by) % size) for i in range(size)])  7.37 us
    ppermute x1, starting transfers between devices, per_device(): pair = plus(keep, lax.ppermute(send, 'srv', [(0, 1), (1, 0)]))  3.28 us
  transfers between devices with their start and end apart: 13, of which 8 were waited for; matrix products, arithmetic and copies ran while one was open for 1% of the time, Pallas kernels for 7%

profile of v2, /device:TPU:1, one launch (start us, length us, event | category | flops | bytes accessed | tf_op | source)
XLA Modules:
  0.0 136.1 jit_solution(6015562396625226102)
XLA Ops:
  0.0 1.3 add_convert_fusion.1
  1.3 1.6 %shard_map.55.refs_2_ = bf16[272,256]{1,0:T(8,128)(2,1)} custom-call(bf16[256,128]{1,0:T(8,128)(2,1)} %key_ref.1, bf16[256,128]{1,0:T(8,128)(2,1)} %value_ref.1, f32[1,256]{1,0:T(1,128)} %bitcast.15), custom_call_target="tpu_custom_call" | custom-call | tf_op jit(solution)/shard_map/pallas_call | solution.py:188
  2.9 16.3 %collective-permute-start = (bf16[272,256]{1,0:T(8,128)(2,1)}, bf16[272,256]{1,0:T(8,128)(2,1)S(1)}, u32[]{:S(2)}, u32[]{:S(2)}) collective-permute-start(bf16[272,256]{1,0:T(8,128)(2,1)} %shard_map.55.refs_2_), channel_id=1, source_target_pairs={{0,64},{8,72},{16,80},{24,88},{32,96},{40,104},{48,112},{56,120},{... | collective-permute-start | bytes 417800 | tf_op jit(solution)/shard_map/ppermute | solution.py:142
  22.7 9.3 %collective-permute-done.refs_2_ = bf16[272,256]{1,0:T(8,128)(2,1)S(1)} collective-permute-done((bf16[272,256]{1,0:T(8,128)(2,1)}, bf16[272,256]{1,0:T(8,128)(2,1)S(1)}, u32[]{:S(2)}, u32[]{:S(2)}) %collective-permute-start) | collective-permute-done | bytes 139296 | tf_op jit(solution)/shard_map/ppermute | solution.py:142
  32.0 13.0 %collective-permute-start.1 = (bf16[272,256]{1,0:T(8,128)(2,1)S(1)}, bf16[272,256]{1,0:T(8,128)(2,1)S(1)}, u32[]{:S(2)}, u32[]{:S(2)}) collective-permute-start(bf16[272,256]{1,0:T(8,128)(2,1)S(1)} %collective-permute-done.refs_2_), channel_id=1, source_target_pairs={{0,32},{8,40},{16,48},{24,56},{32,64},{40,72},{48,80},{56,88},{64,... | collective-permute-start | bytes 417800 | tf_op jit(solution)/shard_map/ppermute | solution.py:142
  45.0 3.0 %collective-permute-start.3 = (bf16[272,256]{1,0:T(8,128)(2,1)S(1)}, bf16[272,256]{1,0:T(8,128)(2,1)S(1)}, u32[]{:S(2)}, u32[]{:S(2)}) collective-permute-start(bf16[272,256]{1,0:T(8,128)(2,1)S(1)} %collective-permute-done.refs_2_), channel_id=1, source_target_pairs={{0,992},{8,1000},{16,1008},{24,1016},{32,0},{40,8},{48,16},{56,24}... | collective-permute-start | bytes 417800 | tf_op jit(solution)/shard_map/ppermute | solution.py:142
  48.1 1.7 %shard_map.57 = (f32[256,4]{1,0:T(8,128)S(1)}, f32[256,512]{1,0:T(8,128)S(1)}, f32[256,512]{1,0:T(8,128)S(1)}) custom-call(bf16[256,512]{1,0:T(8,128)(2,1)S(1)} %copy-done.3, f32[256,1]{1,0:T(8,128)S(1)} %copy.10.refs_1_.refs_2_, bf16[272,256]{1,0:T(8,128)(2,1)S(1)} %collective-permute-done.refs_2_, f32[256,4]{1,0:T(8,128)S(1)} %get-tuple-element.35.refs_3_, ...), custom_call_target="tpu_custom_call" | custom-call | flops 805306368 | bytes 2236416 | tf_op jit(solution)/shard_map/pallas_call | solution.py:125
  49.7 3.7 %collective-permute-done.1.refs_2_ = bf16[272,256]{1,0:T(8,128)(2,1)S(1)} collective-permute-done((bf16[272,256]{1,0:T(8,128)(2,1)S(1)}, bf16[272,256]{1,0:T(8,128)(2,1)S(1)}, u32[]{:S(2)}, u32[]{:S(2)}) %collective-permute-start.1) | collective-permute-done | bytes 139296 | tf_op jit(solution)/shard_map/ppermute | solution.py:142
  53.5 16.5 %collective-permute-done.3.refs_3_ = bf16[272,256]{1,0:T(8,128)(2,1)S(1)} collective-permute-done((bf16[272,256]{1,0:T(8,128)(2,1)S(1)}, bf16[272,256]{1,0:T(8,128)(2,1)S(1)}, u32[]{:S(2)}, u32[]{:S(2)}) %collective-permute-start.3) | collective-permute-done | bytes 139296 | tf_op jit(solution)/shard_map/ppermute | solution.py:142
  71.3 2.7 %collective-permute-start.2 = (bf16[544,256]{1,0:T(8,128)(2,1)S(1)}, bf16[544,256]{1,0:T(8,128)(2,1)S(1)}, u32[]{:S(2)}, u32[]{:S(2)}) collective-permute-start(bf16[544,256]{1,0:T(8,128)(2,1)S(1)} %constant_dynamic-update-slice_fusion), channel_id=1, source_target_pairs={{0,16},{8,24},{16,32},{24,40},{32,48},{40,56},{48,64},{56,72},{64,... | collective-permute-start | bytes 835592 | tf_op jit(solution)/shard_map/ppermute | solution.py:142
  74.0 8.2 %collective-permute-start.5 = (bf16[544,256]{1,0:T(8,128)(2,1)}, bf16[544,256]{1,0:T(8,128)(2,1)S(1)}, u32[]{:S(2)}, u32[]{:S(2)}) collective-permute-start(bf16[544,256]{1,0:T(8,128)(2,1)} %get-tuple-element.60), channel_id=1, source_target_pairs={{0,1008},{8,1016},{16,0},{24,8},{32,16},{40,24},{48,32},{56,40},{6... | collective-permute-start | bytes 835592 | tf_op jit(solution)/shard_map/ppermute | solution.py:142
  82.2 3.4 %collective-permute-start.7 = (bf16[544,256]{1,0:T(8,128)(2,1)S(1)}, bf16[544,256]{1,0:T(8,128)(2,1)S(1)}, u32[]{:S(2)}, u32[]{:S(2)}) collective-permute-start(bf16[544,256]{1,0:T(8,128)(2,1)S(1)} %constant_dynamic-update-slice_fusion), channel_id=1, source_target_pairs={{0,8},{8,16},{16,24},{24,32},{32,40},{40,48},{48,56},{56,64},{64,7... | collective-permute-start | bytes 835592 | tf_op jit(solution)/shard_map/ppermute | solution.py:142
  85.6 5.2 %collective-permute-start.8 = (bf16[544,256]{1,0:T(8,128)(2,1)}, bf16[544,256]{1,0:T(8,128)(2,1)S(1)}, u32[]{:S(2)}, u32[]{:S(2)}) collective-permute-start(bf16[544,256]{1,0:T(8,128)(2,1)} %get-tuple-element.60), channel_id=1, source_target_pairs={{0,1016},{8,0},{16,8},{24,16},{32,24},{40,32},{48,40},{56,48},{64,... | collective-permute-start | bytes 835592 | tf_op jit(solution)/shard_map/ppermute | solution.py:142
  90.9 2.1 %shard_map.58 = (f32[256,4]{1,0:T(8,128)S(1)}, f32[256,512]{1,0:T(8,128)S(1)}, f32[256,512]{1,0:T(8,128)S(1)}) custom-call(bf16[256,512]{1,0:T(8,128)(2,1)S(1)} %copy-done.3, f32[256,1]{1,0:T(8,128)S(1)} %copy.10.refs_1_.refs_2_, bf16[272,256]{1,0:T(8,128)(2,1)S(1)} %collective-permute-done.1.refs_2_, bf16[272,256]{1,0:T(8,128)(2,1)S(1)} %collective-permute-done.3.refs_3_, ...), custom_call_target="tpu_custom_call" | custom-call | flops 1610612736 | bytes 2375680 | tf_op jit(solution)/shard_map/pallas_call | solution.py:125
  93.0 3.7 %collective-permute-start.4 = (bf16[544,256]{1,0:T(8,128)(2,1)S(1)}, bf16[544,256]{1,0:T(8,128)(2,1)S(1)}, u32[]{:S(2)}, u32[]{:S(2)}) collective-permute-start(bf16[544,256]{1,0:T(8,128)(2,1)S(1)} %collective-permute-done.2.refs_2_), channel_id=1, source_target_pairs={{0,8},{8,16},{16,24},{24,32},{32,40},{40,48},{48,56},{56,64},{64,7... | collective-permute-start | bytes 835592 | tf_op jit(solution)/shard_map/ppermute | solution.py:142
  96.7 5.2 %collective-permute-start.6 = (bf16[544,256]{1,0:T(8,128)(2,1)S(1)}, bf16[544,256]{1,0:T(8,128)(2,1)S(1)}, u32[]{:S(2)}, u32[]{:S(2)}) collective-permute-start(bf16[544,256]{1,0:T(8,128)(2,1)S(1)} %collective-permute-done.5.refs_3_), channel_id=1, source_target_pairs={{0,1016},{8,0},{16,8},{24,16},{32,24},{40,32},{48,40},{56,48},{64,... | collective-permute-start | bytes 835592 | tf_op jit(solution)/shard_map/ppermute | solution.py:142
  101.9 4.5 %shard_map.59 = (f32[256,4]{1,0:T(8,128)S(1)}, f32[256,512]{1,0:T(8,128)S(1)}, f32[256,512]{1,0:T(8,128)S(1)}) custom-call(bf16[256,512]{1,0:T(8,128)(2,1)S(1)} %copy-done.3, f32[256,1]{1,0:T(8,128)S(1)} %copy.10.refs_1_.refs_2_, bf16[544,256]{1,0:T(8,128)(2,1)S(1)} %collective-permute-done.2.refs_2_, bf16[544,256]{1,0:T(8,128)(2,1)S(1)} %collective-permute-done.5.refs_3_, ...), custom_call_target="tpu_custom_call" | custom-call | flops 6442450944 | bytes 3211264 | tf_op jit(solution)/shard_map/pallas_call | solution.py:125
  107.4 4.5 %shard_map.60 = (bf16[4,256,512]{2,1,0:T(8,128)(2,1)S(1)}, bf16[4,256,512]{2,1,0:T(8,128)(2,1)S(1)}) custom-call(s32[2]{0:T(128)S(1)} %pad_add_fusion.refs_0_, bf16[256,512]{1,0:T(8,128)(2,1)S(1)} %copy-done.3, f32[256,1]{1,0:T(8,128)S(1)} %copy.10.refs_1_.refs_2_, bf16[544,256]{1,0:T(8,128)(2,1)S(1)} %collective-permute-done.4.refs_3_, ...), custom_call_target="tpu_custom_call" | custom-call | flops 4294967296 | bytes 8945664 | tf_op jit(solution)/shard_map/pallas_call | solution.py:125
  111.9 3.3 %collective-permute-start.9 = (bf16[4,256,512]{2,1,0:T(8,128)(2,1)S(1)}, bf16[4,256,512]{2,1,0:T(8,128)(2,1)S(1)}, u32[]{:S(2)}, u32[]{:S(2)}) collective-permute-start(bf16[4,256,512]{2,1,0:T(8,128)(2,1)S(1)} %get-tuple-element.56), channel_id=1, source_target_pairs={{0,1},{1,0},{2,3},{3,2},{4,5},{5,4},{6,7},{7,6},{8,9},{9,8},{10,11... | collective-permute-start | bytes 3145736 | tf_op jit(solution)/shard_map/ppermute | solution.py:193
  115.2 2.3 %collective-permute-done.9 = bf16[4,256,512]{2,1,0:T(8,128)(2,1)S(1)} collective-permute-done((bf16[4,256,512]{2,1,0:T(8,128)(2,1)S(1)}, bf16[4,256,512]{2,1,0:T(8,128)(2,1)S(1)}, u32[]{:S(2)}, u32[]{:S(2)}) %collective-permute-start.9) | collective-permute-done | bytes 1048608 | tf_op jit(solution)/shard_map/ppermute | solution.py:193
  117.8 4.8 %collective-permute-start.10 = (bf16[256,512]{1,0:T(8,128)(2,1)S(1)}, bf16[256,512]{1,0:T(8,128)(2,1)S(1)}, u32[]{:S(2)}, u32[]{:S(2)}) collective-permute-start(bf16[256,512]{1,0:T(8,128)(2,1)S(1)} %get-tuple-element.57), channel_id=1, source_target_pairs={{0,4},{2,6},{4,0},{6,2},{1,5},{3,7},{5,1},{7,3},{8,12},{10,14},{12... | collective-permute-start | bytes 786440 | tf_op jit(solution)/shard_map/ppermute | solution.py:147
  122.6 2.7 %collective-permute-start.12 = (bf16[256,512]{1,0:T(8,128)(2,1)S(1)}, bf16[256,512]{1,0:T(8,128)(2,1)S(1)}, u32[]{:S(2)}, u32[]{:S(2)}) collective-permute-start(bf16[256,512]{1,0:T(8,128)(2,1)S(1)} %get-tuple-element.58), channel_id=1, source_target_pairs={{0,6},{2,0},{4,2},{6,4},{1,7},{3,1},{5,3},{7,5},{8,14},{10,8},{12,... | collective-permute-start | bytes 786440 | tf_op jit(solution)/shard_map/ppermute | solution.py:147
  125.3 2.6 %collective-permute-start.11 = (bf16[256,512]{1,0:T(8,128)(2,1)S(1)}, bf16[256,512]{1,0:T(8,128)(2,1)S(1)}, u32[]{:S(2)}, u32[]{:S(2)}) collective-permute-start(bf16[256,512]{1,0:T(8,128)(2,1)S(1)} %get-tuple-element.59), channel_id=1, source_target_pairs={{0,2},{2,4},{4,6},{6,0},{1,3},{3,5},{5,7},{7,1},{8,10},{10,12},{12... | collective-permute-start | bytes 786440 | tf_op jit(solution)/shard_map/ppermute | solution.py:147
  128.7 6.0 %collective-permute-done.12 = bf16[256,512]{1,0:T(8,128)(2,1)S(1)} collective-permute-done((bf16[256,512]{1,0:T(8,128)(2,1)S(1)}, bf16[256,512]{1,0:T(8,128)(2,1)S(1)}, u32[]{:S(2)}, u32[]{:S(2)}) %collective-permute-start.12) | collective-permute-done | bytes 262176 | tf_op jit(solution)/shard_map/ppermute | solution.py:147
  (25 shorter events, 8.5 us)
Async XLA Ops:
  0.0 48.0 %copy-start.3 = (bf16[256,512]{1,0:T(8,128)(2,1)S(1)}, bf16[256,512]{1,0:T(8,128)(2,1)}, u32[]{:S(2)}) copy-start(bf16[256,512]{1,0:T(8,128)(2,1)} %refs_1_.1) | copy-start | bytes 786436
  2.9 29.1 %collective-permute-start = (bf16[272,256]{1,0:T(8,128)(2,1)}, bf16[272,256]{1,0:T(8,128)(2,1)S(1)}, u32[]{:S(2)}, u32[]{:S(2)}) collective-permute-start(bf16[272,256]{1,0:T(8,128)(2,1)} %shard_map.55.refs_2_), channel_id=1, source_target_pairs={{0,64},{8,72},{16,80},{24,88},{32,96},{40,104},{48,112},{56,120},{... | collective-permute-start | bytes 417800 | tf_op jit(solution)/shard_map/ppermute | solution.py:142
  19.9 0.9 copy-start
  20.8 0.9 copy-start.2
  32.0 21.5 %collective-permute-start.1 = (bf16[272,256]{1,0:T(8,128)(2,1)S(1)}, bf16[272,256]{1,0:T(8,128)(2,1)S(1)}, u32[]{:S(2)}, u32[]{:S(2)}) collective-permute-start(bf16[272,256]{1,0:T(8,128)(2,1)S(1)} %collective-permute-done.refs_2_), channel_id=1, source_target_pairs={{0,32},{8,40},{16,48},{24,56},{32,64},{40,72},{48,80},{56,88},{64,... | collective-permute-start | bytes 417800 | tf_op jit(solution)/shard_map/ppermute | solution.py:142
  45.0 24.9 %collective-permute-start.3 = (bf16[272,256]{1,0:T(8,128)(2,1)S(1)}, bf16[272,256]{1,0:T(8,128)(2,1)S(1)}, u32[]{:S(2)}, u32[]{:S(2)}) collective-permute-start(bf16[272,256]{1,0:T(8,128)(2,1)S(1)} %collective-permute-done.refs_2_), channel_id=1, source_target_pairs={{0,992},{8,1000},{16,1008},{24,1016},{32,0},{40,8},{48,16},{56,24}... | collective-permute-start | bytes 417800 | tf_op jit(solution)/shard_map/ppermute | solution.py:142
  71.3 21.7 %collective-permute-start.2 = (bf16[544,256]{1,0:T(8,128)(2,1)S(1)}, bf16[544,256]{1,0:T(8,128)(2,1)S(1)}, u32[]{:S(2)}, u32[]{:S(2)}) collective-permute-start(bf16[544,256]{1,0:T(8,128)(2,1)S(1)} %constant_dynamic-update-slice_fusion), channel_id=1, source_target_pairs={{0,16},{8,24},{16,32},{24,40},{32,48},{40,56},{48,64},{56,72},{64,... | collective-permute-start | bytes 835592 | tf_op jit(solution)/shard_map/ppermute | solution.py:142
  74.0 22.8 %collective-permute-start.5 = (bf16[544,256]{1,0:T(8,128)(2,1)}, bf16[544,256]{1,0:T(8,128)(2,1)S(1)}, u32[]{:S(2)}, u32[]{:S(2)}) collective-permute-start(bf16[544,256]{1,0:T(8,128)(2,1)} %get-tuple-element.60), channel_id=1, source_target_pairs={{0,1008},{8,1016},{16,0},{24,8},{32,16},{40,24},{48,32},{56,40},{6... | collective-permute-start | bytes 835592 | tf_op jit(solution)/shard_map/ppermute | solution.py:142
  82.2 19.7 %collective-permute-start.7 = (bf16[544,256]{1,0:T(8,128)(2,1)S(1)}, bf16[544,256]{1,0:T(8,128)(2,1)S(1)}, u32[]{:S(2)}, u32[]{:S(2)}) collective-permute-start(bf16[544,256]{1,0:T(8,128)(2,1)S(1)} %constant_dynamic-update-slice_fusion), channel_id=1, source_target_pairs={{0,8},{8,16},{16,24},{24,32},{32,40},{40,48},{48,56},{56,64},{64,7... | collective-permute-start | bytes 835592 | tf_op jit(solution)/shard_map/ppermute | solution.py:142
  85.6 16.3 %collective-permute-start.8 = (bf16[544,256]{1,0:T(8,128)(2,1)}, bf16[544,256]{1,0:T(8,128)(2,1)S(1)}, u32[]{:S(2)}, u32[]{:S(2)}) collective-permute-start(bf16[544,256]{1,0:T(8,128)(2,1)} %get-tuple-element.60), channel_id=1, source_target_pairs={{0,1016},{8,0},{16,8},{24,16},{32,24},{40,32},{48,40},{56,48},{64,... | collective-permute-start | bytes 835592 | tf_op jit(solution)/shard_map/ppermute | solution.py:142
  93.0 14.4 %copy-start.1 = (bf16[512,4096]{1,0:T(8,128)(2,1)S(1)}, bf16[512,4096]{1,0:T(8,128)(2,1)}, u32[]{:S(2)}) copy-start(bf16[512,4096]{1,0:T(8,128)(2,1)} %refs_8_.1) | copy-start | bytes 12582916
  93.0 13.4 %collective-permute-start.4 = (bf16[544,256]{1,0:T(8,128)(2,1)S(1)}, bf16[544,256]{1,0:T(8,128)(2,1)S(1)}, u32[]{:S(2)}, u32[]{:S(2)}) collective-permute-start(bf16[544,256]{1,0:T(8,128)(2,1)S(1)} %collective-permute-done.2.refs_2_), channel_id=1, source_target_pairs={{0,8},{8,16},{16,24},{24,32},{32,40},{40,48},{48,56},{56,64},{64,7... | collective-permute-start | bytes 835592 | tf_op jit(solution)/shard_map/ppermute | solution.py:142
  96.7 10.6 %collective-permute-start.6 = (bf16[544,256]{1,0:T(8,128)(2,1)S(1)}, bf16[544,256]{1,0:T(8,128)(2,1)S(1)}, u32[]{:S(2)}, u32[]{:S(2)}) collective-permute-start(bf16[544,256]{1,0:T(8,128)(2,1)S(1)} %collective-permute-done.5.refs_3_), channel_id=1, source_target_pairs={{0,1016},{8,0},{16,8},{24,16},{32,24},{40,32},{48,40},{56,48},{64,... | collective-permute-start | bytes 835592 | tf_op jit(solution)/shard_map/ppermute | solution.py:142
  111.9 5.6 %collective-permute-start.9 = (bf16[4,256,512]{2,1,0:T(8,128)(2,1)S(1)}, bf16[4,256,512]{2,1,0:T(8,128)(2,1)S(1)}, u32[]{:S(2)}, u32[]{:S(2)}) collective-permute-start(bf16[4,256,512]{2,1,0:T(8,128)(2,1)S(1)} %get-tuple-element.56), channel_id=1, source_target_pairs={{0,1},{1,0},{2,3},{3,2},{4,5},{5,4},{6,7},{7,6},{8,9},{9,8},{10,11... | collective-permute-start | bytes 3145736 | tf_op jit(solution)/shard_map/ppermute | solution.py:193
  117.8 10.9 %collective-permute-start.10 = (bf16[256,512]{1,0:T(8,128)(2,1)S(1)}, bf16[256,512]{1,0:T(8,128)(2,1)S(1)}, u32[]{:S(2)}, u32[]{:S(2)}) collective-permute-start(bf16[256,512]{1,0:T(8,128)(2,1)S(1)} %get-tuple-element.57), channel_id=1, source_target_pairs={{0,4},{2,6},{4,0},{6,2},{1,5},{3,7},{5,1},{7,3},{8,12},{10,14},{12... | collective-permute-start | bytes 786440 | tf_op jit(solution)/shard_map/ppermute | solution.py:147
  122.6 12.1 %collective-permute-start.12 = (bf16[256,512]{1,0:T(8,128)(2,1)S(1)}, bf16[256,512]{1,0:T(8,128)(2,1)S(1)}, u32[]{:S(2)}, u32[]{:S(2)}) collective-permute-start(bf16[256,512]{1,0:T(8,128)(2,1)S(1)} %get-tuple-element.58), channel_id=1, source_target_pairs={{0,6},{2,0},{4,2},{6,4},{1,7},{3,1},{5,3},{7,5},{8,14},{10,8},{12,... | collective-permute-start | bytes 786440 | tf_op jit(solution)/shard_map/ppermute | solution.py:147
  125.3 10.0 %collective-permute-start.11 = (bf16[256,512]{1,0:T(8,128)(2,1)S(1)}, bf16[256,512]{1,0:T(8,128)(2,1)S(1)}, u32[]{:S(2)}, u32[]{:S(2)}) collective-permute-start(bf16[256,512]{1,0:T(8,128)(2,1)S(1)} %get-tuple-element.59), channel_id=1, source_target_pairs={{0,2},{2,4},{4,6},{6,0},{1,3},{3,5},{5,7},{7,1},{8,10},{10,12},{12... | collective-permute-start | bytes 786440 | tf_op jit(solution)/shard_map/ppermute | solution.py:147

commit v3 on v2

--- a/solution.py
+++ b/solution.py
@@ -168,26 +168,27 @@
     back10_14 = along(far, 2)
     back2_6 = along(near, -2)
     back9_13 = along(far, 1)
+    near, back10_14 = after(near, back10_14)
     back3_7 = along(near, -1)
-    state = run_stage(queries, marks, [back12, back4], state)
-    back10_14, state = after(back10_14, state)
     back11_15 = along(back10_14, 1)
     back1_5 = along(back2_6, -1)
-    state = run_stage(queries, marks, [back10_14, back2_6, back9_13, back3_7], state)
+    state = run_stage(queries, marks, [back12, back4, back10_14, back2_6, back9_13, back3_7], state)
     return run_stage(queries, marks, [back11_15, back1_5], state, weight, place)
 
 
-def join(key_ref, value_ref, mark_ref, joined_ref):
+def join(key_ref, value_ref, ids_ref, joined_ref):
     joined_ref[:TOK, :HEAD_DIM] = key_ref[...]
     joined_ref[:TOK, HEAD_DIM:] = value_ref[...]
-    joined_ref[TOK:] = jnp.broadcast_to(mark_ref[...], (MARK, TOK)).astype(jnp.bfloat16)
+    ids = ids_ref[...].astype(jnp.float32)
+    joined_ref[TOK:] = jnp.broadcast_to(ids, (MARK, TOK)).astype(jnp.bfloat16)
 
 
 def per_device(queries, key_heads, value_heads, doc_ids, out_weight):
-    marks = (doc_ids + 1).astype(jnp.float32)
     own = pl.pallas_call(join, out_shape=jax.ShapeDtypeStruct((PIECE, TOK), jnp.bfloat16))(
-        key_heads, value_heads, marks[None]
+        key_heads, value_heads, doc_ids[None]
     )
+    own, ids = after(own, doc_ids)
+    marks = ids.astype(jnp.float32)
     place = jnp.stack([lax.axis_index("head"), lax.axis_index("srv")]).astype(jnp.int32)
     send, keep = gather_and_attend(queries, marks[:, None], own, out_weight, place)
     pair = plus(keep, lax.ppermute(send, "srv", [(0, 1), (1, 0)]))

time: 137 us -> 141 us (1.029)
  starting transfers between devices: 74 us -> 80.1 us
    ppermute x9, starting transfers between devices: 60.7 us -> 64.5 us  [along(): lax.ppermute(value, 'tok', [(i, (i + by) % size) for i in range(size)])]
    ppermute x9, waiting for transfers between devices: 30.4 us -> 32.3 us  [along(): lax.ppermute(value, 'tok', [(i, (i + by) % size) for i in range(size)])]
    ppermute x3, waiting for transfers between devices: 7.37 us -> 5.56 us  [around(): lax.ppermute(value, 'head', [(i, (i + by) % size) for i in range(size)])]
    pallas_call x5 -> x4, Pallas kernels: 13.7 us -> 12.6 us  [run_stage(): pl.pallas_call(functools.partial(attend_stage, first, final, len(arrays),...]
    unnamed x9 -> x10, local copies, waits for them, and re-layouts: 2.52 us -> 3.2 us
  transfers between devices with their start and end apart: 13 -> 13, of which waited for: 8 -> 6; matrix products, arithmetic and copies ran while one was open for 1% -> 1% of each run, Pallas kernels for 7% -> 6%
where the time goes in v3:
time: 141 us; the launch traced here: 140 us
  starting transfers between devices  80.1 us (57%)
  waiting for transfers between devices  40.1 us (28%)
  Pallas kernels  14.2 us (10%)
  local copies, waits for them, and re-layouts  3.4 us (2%)
  other arithmetic  1.9 us (1%)
    ppermute x9, starting transfers between devices, along(): lax.ppermute(value, 'tok', [(i, (i + by) % size) for i in range(size)])  64.5 us
    ppermute x9, waiting for transfers between devices, along(): lax.ppermute(value, 'tok', [(i, (i + by) % size) for i in range(size)])  32.3 us
    pallas_call x4, Pallas kernels, run_stage(): pl.pallas_call(functools.partial(attend_stage, first, final, len(arrays),...  12.6 us
    ppermute x3, starting transfers between devices, around(): lax.ppermute(value, 'head', [(i, (i + by) % size) for i in range(size)])  11.3 us
    ppermute x3, waiting for transfers between devices, around(): lax.ppermute(value, 'head', [(i, (i + by) % size) for i in range(size)])  5.56 us
    ppermute x1, starting transfers between devices, per_device(): pair = plus(keep, lax.ppermute(send, 'srv', [(0, 1), (1, 0)]))  4.31 us
    unnamed x10, local copies, waits for them, and re-layouts  3.2 us
  transfers between devices with their start and end apart: 13, of which 6 were waited for; matrix products, arithmetic and copies ran while one was open for 1% of the time, Pallas kernels for 6%

profile of v3, /device:TPU:1, one launch (start us, length us, event | category | flops | bytes accessed | tf_op | source)
XLA Modules:
  0.0 139.9 jit_solution(4757408061900563631)
XLA Ops:
  0.0 1.6 %shard_map.55.refs_2_ = bf16[272,256]{1,0:T(8,128)(2,1)} custom-call(bf16[256,128]{1,0:T(8,128)(2,1)} %key_ref.1, bf16[256,128]{1,0:T(8,128)(2,1)} %value_ref.1, s32[1,256]{1,0:T(1,128)} %bitcast.15), custom_call_target="tpu_custom_call" | custom-call | tf_op jit(solution)/shard_map/pallas_call | solution.py:187
  1.6 16.3 %collective-permute-start = (bf16[272,256]{1,0:T(8,128)(2,1)}, bf16[272,256]{1,0:T(8,128)(2,1)S(1)}, u32[]{:S(2)}, u32[]{:S(2)}) collective-permute-start(bf16[272,256]{1,0:T(8,128)(2,1)} %shard_map.55.refs_2_), channel_id=1, source_target_pairs={{0,64},{8,72},{16,80},{24,88},{32,96},{40,104},{48,112},{56,120},{... | collective-permute-start | bytes 417800 | tf_op jit(solution)/shard_map/ppermute | solution.py:142
  19.6 0.9 copy-done.2
  21.5 9.3 %collective-permute-done.refs_2_ = bf16[272,256]{1,0:T(8,128)(2,1)S(1)} collective-permute-done((bf16[272,256]{1,0:T(8,128)(2,1)}, bf16[272,256]{1,0:T(8,128)(2,1)S(1)}, u32[]{:S(2)}, u32[]{:S(2)}) %collective-permute-start) | collective-permute-done | bytes 139296 | tf_op jit(solution)/shard_map/ppermute | solution.py:142
  30.7 13.0 %collective-permute-start.2 = (bf16[272,256]{1,0:T(8,128)(2,1)S(1)}, bf16[272,256]{1,0:T(8,128)(2,1)S(1)}, u32[]{:S(2)}, u32[]{:S(2)}) collective-permute-start(bf16[272,256]{1,0:T(8,128)(2,1)S(1)} %collective-permute-done.refs_2_), channel_id=1, source_target_pairs={{0,32},{8,40},{16,48},{24,56},{32,64},{40,72},{48,80},{56,88},{64,... | collective-permute-start | bytes 417800 | tf_op jit(solution)/shard_map/ppermute | solution.py:142
  43.8 3.0 %collective-permute-start.1 = (bf16[272,256]{1,0:T(8,128)(2,1)S(1)}, bf16[272,256]{1,0:T(8,128)(2,1)S(1)}, u32[]{:S(2)}, u32[]{:S(2)}) collective-permute-start(bf16[272,256]{1,0:T(8,128)(2,1)S(1)} %collective-permute-done.refs_2_), channel_id=1, source_target_pairs={{0,992},{8,1000},{16,1008},{24,1016},{32,0},{40,8},{48,16},{56,24}... | collective-permute-start | bytes 417800 | tf_op jit(solution)/shard_map/ppermute | solution.py:142
  46.8 1.7 %shard_map.57 = (f32[256,4]{1,0:T(8,128)S(1)}, f32[256,512]{1,0:T(8,128)S(1)}, f32[256,512]{1,0:T(8,128)S(1)}) custom-call(bf16[256,512]{1,0:T(8,128)(2,1)S(1)} %copy-done.3, f32[256,1]{1,0:T(8,128)S(1)} %copy.9.refs_1_.refs_2_, bf16[272,256]{1,0:T(8,128)(2,1)S(1)} %collective-permute-done.refs_2_, f32[256,4]{1,0:T(8,128)S(1)} %get-tuple-element.34.refs_3_, ...), custom_call_target="tpu_custom_call" | custom-call | flops 805306368 | bytes 2236416 | tf_op jit(solution)/shard_map/pallas_call | solution.py:125
  48.5 3.7 %collective-permute-done.2.refs_2_ = bf16[272,256]{1,0:T(8,128)(2,1)S(1)} collective-permute-done((bf16[272,256]{1,0:T(8,128)(2,1)S(1)}, bf16[272,256]{1,0:T(8,128)(2,1)S(1)}, u32[]{:S(2)}, u32[]{:S(2)}) %collective-permute-start.2) | collective-permute-done | bytes 139296 | tf_op jit(solution)/shard_map/ppermute | solution.py:142
  52.2 16.5 %collective-permute-done.1.refs_3_ = bf16[272,256]{1,0:T(8,128)(2,1)S(1)} collective-permute-done((bf16[272,256]{1,0:T(8,128)(2,1)S(1)}, bf16[272,256]{1,0:T(8,128)(2,1)S(1)}, u32[]{:S(2)}, u32[]{:S(2)}) %collective-permute-start.1) | collective-permute-done | bytes 139296 | tf_op jit(solution)/shard_map/ppermute | solution.py:142
  70.0 2.7 %collective-permute-start.3 = (bf16[544,256]{1,0:T(8,128)(2,1)S(1)}, bf16[544,256]{1,0:T(8,128)(2,1)S(1)}, u32[]{:S(2)}, u32[]{:S(2)}) collective-permute-start(bf16[544,256]{1,0:T(8,128)(2,1)S(1)} %constant_dynamic-update-slice_fusion.2), channel_id=1, source_target_pairs={{0,16},{8,24},{16,32},{24,40},{32,48},{40,56},{48,64},{56,72},{64,... | collective-permute-start | bytes 835592 | tf_op jit(solution)/shard_map/ppermute | solution.py:142
  72.7 5.4 %collective-permute-start.7 = (bf16[544,256]{1,0:T(8,128)(2,1)S(1)}, bf16[544,256]{1,0:T(8,128)(2,1)S(1)}, u32[]{:S(2)}, u32[]{:S(2)}) collective-permute-start(bf16[544,256]{1,0:T(8,128)(2,1)S(1)} %constant_dynamic-update-slice_fusion.2), channel_id=1, source_target_pairs={{0,8},{8,16},{16,24},{24,32},{32,40},{40,48},{48,56},{56,64},{64,7... | collective-permute-start | bytes 835592 | tf_op jit(solution)/shard_map/ppermute | solution.py:142
  78.1 6.2 %collective-permute-start.5 = (bf16[544,256]{1,0:T(8,128)(2,1)}, bf16[544,256]{1,0:T(8,128)(2,1)S(1)}, u32[]{:S(2)}, u32[]{:S(2)}) collective-permute-start(bf16[544,256]{1,0:T(8,128)(2,1)} %get-tuple-element.42), channel_id=1, source_target_pairs={{0,1008},{8,1016},{16,0},{24,8},{32,16},{40,24},{48,32},{56,40},{6... | collective-permute-start | bytes 835592 | tf_op jit(solution)/shard_map/ppermute | solution.py:142
  84.3 2.8 %collective-permute-done.3.refs_4_ = bf16[544,256]{1,0:T(8,128)(2,1)S(1)} collective-permute-done((bf16[544,256]{1,0:T(8,128)(2,1)S(1)}, bf16[544,256]{1,0:T(8,128)(2,1)S(1)}, u32[]{:S(2)}, u32[]{:S(2)}) %collective-permute-start.3) | collective-permute-done | bytes 278560 | tf_op jit(solution)/shard_map/ppermute | solution.py:142
  87.2 9.0 %collective-permute-start.8 = (bf16[544,256]{1,0:T(8,128)(2,1)}, bf16[544,256]{1,0:T(8,128)(2,1)S(1)}, u32[]{:S(2)}, u32[]{:S(2)}) collective-permute-start(bf16[544,256]{1,0:T(8,128)(2,1)} %get-tuple-element.42), channel_id=1, source_target_pairs={{0,1016},{8,0},{16,8},{24,16},{32,24},{40,32},{48,40},{56,48},{64,... | collective-permute-start | bytes 835592 | tf_op jit(solution)/shard_map/ppermute | solution.py:142
  96.3 2.2 %collective-permute-start.4 = (bf16[544,256]{1,0:T(8,128)(2,1)S(1)}, bf16[544,256]{1,0:T(8,128)(2,1)S(1)}, u32[]{:S(2)}, u32[]{:S(2)}) collective-permute-start(bf16[544,256]{1,0:T(8,128)(2,1)S(1)} %collective-permute-done.3.refs_4_), channel_id=1, source_target_pairs={{0,8},{8,16},{16,24},{24,32},{32,40},{40,48},{48,56},{56,64},{64,7... | collective-permute-start | bytes 835592 | tf_op jit(solution)/shard_map/ppermute | solution.py:142
  98.5 6.7 %collective-permute-start.6 = (bf16[544,256]{1,0:T(8,128)(2,1)S(1)}, bf16[544,256]{1,0:T(8,128)(2,1)S(1)}, u32[]{:S(2)}, u32[]{:S(2)}) collective-permute-start(bf16[544,256]{1,0:T(8,128)(2,1)S(1)} %collective-permute-done.5.refs_5_), channel_id=1, source_target_pairs={{0,1016},{8,0},{16,8},{24,16},{32,24},{40,32},{48,40},{56,48},{64,... | collective-permute-start | bytes 835592 | tf_op jit(solution)/shard_map/ppermute | solution.py:142
  105.2 5.5 %shard_map.58 = (f32[256,4]{1,0:T(8,128)S(1)}, f32[256,512]{1,0:T(8,128)S(1)}, f32[256,512]{1,0:T(8,128)S(1)}) custom-call(bf16[256,512]{1,0:T(8,128)(2,1)S(1)} %copy-done.3, f32[256,1]{1,0:T(8,128)S(1)} %copy.9.refs_1_.refs_2_, bf16[272,256]{1,0:T(8,128)(2,1)S(1)} %collective-permute-done.2.refs_2_, bf16[272,256]{1,0:T(8,128)(2,1)S(1)} %collective-permute-done.1.refs_3_, ...), custom_call_target="tpu_custom_call" | custom-call | flops 8053063680 | bytes 3489792 | tf_op jit(solution)/shard_map/pallas_call | solution.py:125
  110.7 4.5 %shard_map.59 = (bf16[4,256,512]{2,1,0:T(8,128)(2,1)S(1)}, bf16[4,256,512]{2,1,0:T(8,128)(2,1)S(1)}) custom-call(s32[2]{0:T(128)S(1)} %pad_add_fusion.refs_0_, bf16[256,512]{1,0:T(8,128)(2,1)S(1)} %copy-done.3, f32[256,1]{1,0:T(8,128)S(1)} %copy.9.refs_1_.refs_2_, bf16[544,256]{1,0:T(8,128)(2,1)S(1)} %collective-permute-done.4.refs_3_, ...), custom_call_target="tpu_custom_call" | custom-call | flops 4294967296 | bytes 8945664 | tf_op jit(solution)/shard_map/pallas_call | solution.py:125
  115.2 4.3 %collective-permute-start.9 = (bf16[4,256,512]{2,1,0:T(8,128)(2,1)S(1)}, bf16[4,256,512]{2,1,0:T(8,128)(2,1)S(1)}, u32[]{:S(2)}, u32[]{:S(2)}) collective-permute-start(bf16[4,256,512]{2,1,0:T(8,128)(2,1)S(1)} %get-tuple-element.50), channel_id=1, source_target_pairs={{0,1},{1,0},{2,3},{3,2},{4,5},{5,4},{6,7},{7,6},{8,9},{9,8},{10,11... | collective-permute-start | bytes 3145736 | tf_op jit(solution)/shard_map/ppermute | solution.py:194
  119.5 2.3 %collective-permute-done.9 = bf16[4,256,512]{2,1,0:T(8,128)(2,1)S(1)} collective-permute-done((bf16[4,256,512]{2,1,0:T(8,128)(2,1)S(1)}, bf16[4,256,512]{2,1,0:T(8,128)(2,1)S(1)}, u32[]{:S(2)}, u32[]{:S(2)}) %collective-permute-start.9) | collective-permute-done | bytes 1048608 | tf_op jit(solution)/shard_map/ppermute | solution.py:194
  122.2 4.8 %collective-permute-start.10 = (bf16[256,512]{1,0:T(8,128)(2,1)S(1)}, bf16[256,512]{1,0:T(8,128)(2,1)S(1)}, u32[]{:S(2)}, u32[]{:S(2)}) collective-permute-start(bf16[256,512]{1,0:T(8,128)(2,1)S(1)} %get-tuple-element.51), channel_id=1, source_target_pairs={{0,4},{2,6},{4,0},{6,2},{1,5},{3,7},{5,1},{7,3},{8,12},{10,14},{12... | collective-permute-start | bytes 786440 | tf_op jit(solution)/shard_map/ppermute | solution.py:147
  127.0 2.3 %collective-permute-start.11 = (bf16[256,512]{1,0:T(8,128)(2,1)S(1)}, bf16[256,512]{1,0:T(8,128)(2,1)S(1)}, u32[]{:S(2)}, u32[]{:S(2)}) collective-permute-start(bf16[256,512]{1,0:T(8,128)(2,1)S(1)} %get-tuple-element.53), channel_id=1, source_target_pairs={{0,2},{2,4},{4,6},{6,0},{1,3},{3,5},{5,7},{7,1},{8,10},{10,12},{12... | collective-permute-start | bytes 786440 | tf_op jit(solution)/shard_map/ppermute | solution.py:147
  129.3 4.2 %collective-permute-start.12 = (bf16[256,512]{1,0:T(8,128)(2,1)S(1)}, bf16[256,512]{1,0:T(8,128)(2,1)S(1)}, u32[]{:S(2)}, u32[]{:S(2)}) collective-permute-start(bf16[256,512]{1,0:T(8,128)(2,1)S(1)} %get-tuple-element.52), channel_id=1, source_target_pairs={{0,6},{2,0},{4,2},{6,4},{1,7},{3,1},{5,3},{7,5},{8,14},{10,8},{12,... | collective-permute-start | bytes 786440 | tf_op jit(solution)/shard_map/ppermute | solution.py:147
  133.5 5.6 %collective-permute-done.11 = bf16[256,512]{1,0:T(8,128)(2,1)S(1)} collective-permute-done((bf16[256,512]{1,0:T(8,128)(2,1)S(1)}, bf16[256,512]{1,0:T(8,128)(2,1)S(1)}, u32[]{:S(2)}, u32[]{:S(2)}) %collective-permute-start.11) | collective-permute-done | bytes 262176 | tf_op jit(solution)/shard_map/ppermute | solution.py:147
  (24 shorter events, 5.3 us)
Async XLA Ops:
  0.0 46.8 %copy-start.3 = (bf16[256,512]{1,0:T(8,128)(2,1)S(1)}, bf16[256,512]{1,0:T(8,128)(2,1)}, u32[]{:S(2)}) copy-start(bf16[256,512]{1,0:T(8,128)(2,1)} %refs_1_.1) | copy-start | bytes 786436
  1.6 29.1 %collective-permute-start = (bf16[272,256]{1,0:T(8,128)(2,1)}, bf16[272,256]{1,0:T(8,128)(2,1)S(1)}, u32[]{:S(2)}, u32[]{:S(2)}) collective-permute-start(bf16[272,256]{1,0:T(8,128)(2,1)} %shard_map.55.refs_2_), channel_id=1, source_target_pairs={{0,64},{8,72},{16,80},{24,88},{32,96},{40,104},{48,112},{56,120},{... | collective-permute-start | bytes 417800 | tf_op jit(solution)/shard_map/ppermute | solution.py:142
  18.7 0.9 copy-start
  19.6 0.9 copy-start.2
  30.7 21.5 %collective-permute-start.2 = (bf16[272,256]{1,0:T(8,128)(2,1)S(1)}, bf16[272,256]{1,0:T(8,128)(2,1)S(1)}, u32[]{:S(2)}, u32[]{:S(2)}) collective-permute-start(bf16[272,256]{1,0:T(8,128)(2,1)S(1)} %collective-permute-done.refs_2_), channel_id=1, source_target_pairs={{0,32},{8,40},{16,48},{24,56},{32,64},{40,72},{48,80},{56,88},{64,... | collective-permute-start | bytes 417800 | tf_op jit(solution)/shard_map/ppermute | solution.py:142
  43.8 24.9 %collective-permute-start.1 = (bf16[272,256]{1,0:T(8,128)(2,1)S(1)}, bf16[272,256]{1,0:T(8,128)(2,1)S(1)}, u32[]{:S(2)}, u32[]{:S(2)}) collective-permute-start(bf16[272,256]{1,0:T(8,128)(2,1)S(1)} %collective-permute-done.refs_2_), channel_id=1, source_target_pairs={{0,992},{8,1000},{16,1008},{24,1016},{32,0},{40,8},{48,16},{56,24}... | collective-permute-start | bytes 417800 | tf_op jit(solution)/shard_map/ppermute | solution.py:142
  70.0 17.1 %collective-permute-start.3 = (bf16[544,256]{1,0:T(8,128)(2,1)S(1)}, bf16[544,256]{1,0:T(8,128)(2,1)S(1)}, u32[]{:S(2)}, u32[]{:S(2)}) collective-permute-start(bf16[544,256]{1,0:T(8,128)(2,1)S(1)} %constant_dynamic-update-slice_fusion.2), channel_id=1, source_target_pairs={{0,16},{8,24},{16,32},{24,40},{32,48},{40,56},{48,64},{56,72},{64,... | collective-permute-start | bytes 835592 | tf_op jit(solution)/shard_map/ppermute | solution.py:142
  72.7 32.5 %collective-permute-start.7 = (bf16[544,256]{1,0:T(8,128)(2,1)S(1)}, bf16[544,256]{1,0:T(8,128)(2,1)S(1)}, u32[]{:S(2)}, u32[]{:S(2)}) collective-permute-start(bf16[544,256]{1,0:T(8,128)(2,1)S(1)} %constant_dynamic-update-slice_fusion.2), channel_id=1, source_target_pairs={{0,8},{8,16},{16,24},{24,32},{32,40},{40,48},{48,56},{56,64},{64,7... | collective-permute-start | bytes 835592 | tf_op jit(solution)/shard_map/ppermute | solution.py:142
  78.1 20.4 %collective-permute-start.5 = (bf16[544,256]{1,0:T(8,128)(2,1)}, bf16[544,256]{1,0:T(8,128)(2,1)S(1)}, u32[]{:S(2)}, u32[]{:S(2)}) collective-permute-start(bf16[544,256]{1,0:T(8,128)(2,1)} %get-tuple-element.42), channel_id=1, source_target_pairs={{0,1008},{8,1016},{16,0},{24,8},{32,16},{40,24},{48,32},{56,40},{6... | collective-permute-start | bytes 835592 | tf_op jit(solution)/shard_map/ppermute | solution.py:142
  87.2 18.0 %collective-permute-start.8 = (bf16[544,256]{1,0:T(8,128)(2,1)}, bf16[544,256]{1,0:T(8,128)(2,1)S(1)}, u32[]{:S(2)}, u32[]{:S(2)}) collective-permute-start(bf16[544,256]{1,0:T(8,128)(2,1)} %get-tuple-element.42), channel_id=1, source_target_pairs={{0,1016},{8,0},{16,8},{24,16},{32,24},{40,32},{48,40},{56,48},{64,... | collective-permute-start | bytes 835592 | tf_op jit(solution)/shard_map/ppermute | solution.py:142
  96.3 14.4 %copy-start.1 = (bf16[512,4096]{1,0:T(8,128)(2,1)S(1)}, bf16[512,4096]{1,0:T(8,128)(2,1)}, u32[]{:S(2)}) copy-start(bf16[512,4096]{1,0:T(8,128)(2,1)} %refs_8_.1) | copy-start | bytes 12582916
  96.3 14.4 %collective-permute-start.4 = (bf16[544,256]{1,0:T(8,128)(2,1)S(1)}, bf16[544,256]{1,0:T(8,128)(2,1)S(1)}, u32[]{:S(2)}, u32[]{:S(2)}) collective-permute-start(bf16[544,256]{1,0:T(8,128)(2,1)S(1)} %collective-permute-done.3.refs_4_), channel_id=1, source_target_pairs={{0,8},{8,16},{16,24},{24,32},{32,40},{40,48},{48,56},{56,64},{64,7... | collective-permute-start | bytes 835592 | tf_op jit(solution)/shard_map/ppermute | solution.py:142
  98.5 12.2 %collective-permute-start.6 = (bf16[544,256]{1,0:T(8,128)(2,1)S(1)}, bf16[544,256]{1,0:T(8,128)(2,1)S(1)}, u32[]{:S(2)}, u32[]{:S(2)}) collective-permute-start(bf16[544,256]{1,0:T(8,128)(2,1)S(1)} %collective-permute-done.5.refs_5_), channel_id=1, source_target_pairs={{0,1016},{8,0},{16,8},{24,16},{32,24},{40,32},{48,40},{56,48},{64,... | collective-permute-start | bytes 835592 | tf_op jit(solution)/shard_map/ppermute | solution.py:142
  115.2 6.6 %collective-permute-start.9 = (bf16[4,256,512]{2,1,0:T(8,128)(2,1)S(1)}, bf16[4,256,512]{2,1,0:T(8,128)(2,1)S(1)}, u32[]{:S(2)}, u32[]{:S(2)}) collective-permute-start(bf16[4,256,512]{2,1,0:T(8,128)(2,1)S(1)} %get-tuple-element.50), channel_id=1, source_target_pairs={{0,1},{1,0},{2,3},{3,2},{4,5},{5,4},{6,7},{7,6},{8,9},{9,8},{10,11... | collective-permute-start | bytes 3145736 | tf_op jit(solution)/shard_map/ppermute | solution.py:194
  122.2 11.3 %collective-permute-start.10 = (bf16[256,512]{1,0:T(8,128)(2,1)S(1)}, bf16[256,512]{1,0:T(8,128)(2,1)S(1)}, u32[]{:S(2)}, u32[]{:S(2)}) collective-permute-start(bf16[256,512]{1,0:T(8,128)(2,1)S(1)} %get-tuple-element.51), channel_id=1, source_target_pairs={{0,4},{2,6},{4,0},{6,2},{1,5},{3,7},{5,1},{7,3},{8,12},{10,14},{12... | collective-permute-start | bytes 786440 | tf_op jit(solution)/shard_map/ppermute | solution.py:147
  127.0 12.1 %collective-permute-start.11 = (bf16[256,512]{1,0:T(8,128)(2,1)S(1)}, bf16[256,512]{1,0:T(8,128)(2,1)S(1)}, u32[]{:S(2)}, u32[]{:S(2)}) collective-permute-start(bf16[256,512]{1,0:T(8,128)(2,1)S(1)} %get-tuple-element.53), channel_id=1, source_target_pairs={{0,2},{2,4},{4,6},{6,0},{1,3},{3,5},{5,7},{7,1},{8,10},{10,12},{12... | collective-permute-start | bytes 786440 | tf_op jit(solution)/shard_map/ppermute | solution.py:147
  129.3 9.8 %collective-permute-start.12 = (bf16[256,512]{1,0:T(8,128)(2,1)S(1)}, bf16[256,512]{1,0:T(8,128)(2,1)S(1)}, u32[]{:S(2)}, u32[]{:S(2)}) collective-permute-start(bf16[256,512]{1,0:T(8,128)(2,1)S(1)} %get-tuple-element.52), channel_id=1, source_target_pairs={{0,6},{2,0},{4,2},{6,4},{1,7},{3,1},{5,3},{7,5},{8,14},{10,8},{12,... | collective-permute-start | bytes 786440 | tf_op jit(solution)/shard_map/ppermute | solution.py:147

commit v4 on v3

--- a/solution.py
+++ b/solution.py
@@ -163,17 +163,16 @@
     back4 = along(back8, -4)
     state = run_stage(queries, marks, [back8], state)
     back12, state = after(back12, state)
-    far = jnp.concatenate([back8, back12])
-    near = jnp.concatenate([back4, back8])
-    back10_14 = along(far, 2)
-    back2_6 = along(near, -2)
-    back9_13 = along(far, 1)
-    near, back10_14 = after(near, back10_14)
-    back3_7 = along(near, -1)
-    back11_15 = along(back10_14, 1)
-    back1_5 = along(back2_6, -1)
-    state = run_stage(queries, marks, [back12, back4, back10_14, back2_6, back9_13, back3_7], state)
-    return run_stage(queries, marks, [back11_15, back1_5], state, weight, place)
+    four = lax.optimization_barrier(jnp.concatenate([own, back4, back8, back12]))
+    three = four[PIECE:]
+    back2_6_10 = along(three, -2)
+    back15 = along(back12, 3)
+    back1_5_9_13 = along(four, 1)
+    back3_7_11 = along(three, -1)
+    back14 = along(back12, 2)
+    state = run_stage(queries, marks, [back12, back4], state)
+    state = run_stage(queries, marks, [back2_6_10, back15, back1_5_9_13], state)
+    return run_stage(queries, marks, [back3_7_11, back14], state, weight, place)
 
 
 def join(key_ref, value_ref, ids_ref, joined_ref):
@@ -193,7 +192,7 @@
     send, keep = gather_and_attend(queries, marks[:, None], own, out_weight, place)
     pair = plus(keep, lax.ppermute(send, "srv", [(0, 1), (1, 0)]))
     summed = pair[0].astype(jnp.float32)
-    for turn in (2, 1, 3):
+    for turn in (1, 3, 2):
         summed = summed + around(pair[turn], turn).astype(jnp.float32)
     return summed.astype(jnp.bfloat16)
 

time: 141 us -> 142 us (level)
  waiting for transfers between devices: 40.1 us -> 57 us
  starting transfers between devices: 80.1 us -> 64.8 us
    ppermute x9 -> x8, starting transfers between devices: 64.5 us -> 51.8 us  [along(): lax.ppermute(value, 'tok', [(i, (i + by) % size) for i in range(size)])]
    ppermute x9 -> x8, waiting for transfers between devices: 32.3 us -> 42.4 us  [along(): lax.ppermute(value, 'tok', [(i, (i + by) % size) for i in range(size)])]
    ppermute x3, waiting for transfers between devices: 5.56 us -> 12.4 us  [around(): lax.ppermute(value, 'head', [(i, (i + by) % size) for i in range(size)])]
    ppermute x3, starting transfers between devices: 11.3 us -> 9.5 us  [around(): lax.ppermute(value, 'head', [(i, (i + by) % size) for i in range(size)])]
    pallas_call x4 -> x5, Pallas kernels: 12.6 us -> 13.6 us  [run_stage(): pl.pallas_call(functools.partial(attend_stage, first, final, len(arrays),...]
  transfers between devices with their start and end apart: 13 -> 12, of which waited for: 6 -> 10; matrix products, arithmetic and copies ran while one was open for 1% -> 1% of each run, Pallas kernels for 6% -> 6%
where the time goes in v4:
time: 142 us
  starting transfers between devices  64.8 us (46%)
  waiting for transfers between devices  57 us (40%)
  Pallas kernels  15.2 us (11%)
  local copies, waits for them, and re-layouts  2.83 us (2%)
  other arithmetic  1.94 us (1%)
    ppermute x8, starting transfers between devices, along(): lax.ppermute(value, 'tok', [(i, (i + by) % size) for i in range(size)])  51.8 us
    ppermute x8, waiting for transfers between devices, along(): lax.ppermute(value, 'tok', [(i, (i + by) % size) for i in range(size)])  42.4 us
    pallas_call x5, Pallas kernels, run_stage(): pl.pallas_call(functools.partial(attend_stage, first, final, len(arrays),...  13.6 us
    ppermute x3, waiting for transfers between devices, around(): lax.ppermute(value, 'head', [(i, (i + by) % size) for i in range(size)])  12.4 us
    ppermute x3, starting transfers between devices, around(): lax.ppermute(value, 'head', [(i, (i + by) % size) for i in range(size)])  9.5 us
    ppermute x1, starting transfers between devices, per_device(): pair = plus(keep, lax.ppermute(send, 'srv', [(0, 1), (1, 0)]))  3.5 us
  transfers between devices with their start and end apart: 12, of which 10 were waited for; matrix products, arithmetic and copies ran while one was open for 1% of the time, Pallas kernels for 6%

profile of v4, /device:TPU:1, one launch (start us, length us, event | category | flops | bytes accessed | tf_op | source)
XLA Modules:
  0.0 141.9 jit_solution(1353891407287338736)
XLA Ops:
  1.6 16.3 %collective-permute-start = (bf16[272,256]{1,0:T(8,128)(2,1)}, bf16[272,256]{1,0:T(8,128)(2,1)S(1)}, u32[]{:S(2)}, u32[]{:S(2)}) collective-permute-start(bf16[272,256]{1,0:T(8,128)(2,1)} %shard_map.55.refs_2_), channel_id=1, source_target_pairs={{0,64},{8,72},{16,80},{24,88},{32,96},{40,104},{48,112},{56,120},{... | collective-permute-start | bytes 417800 | tf_op jit(solution)/shard_map/ppermute | solution.py:142
  21.4 9.3 %collective-permute-done.refs_2_ = bf16[272,256]{1,0:T(8,128)(2,1)S(1)} collective-permute-done((bf16[272,256]{1,0:T(8,128)(2,1)}, bf16[272,256]{1,0:T(8,128)(2,1)S(1)}, u32[]{:S(2)}, u32[]{:S(2)}) %collective-permute-start) | collective-permute-done | bytes 139296 | tf_op jit(solution)/shard_map/ppermute | solution.py:142
  30.7 13.2 %collective-permute-start.2 = (bf16[272,256]{1,0:T(8,128)(2,1)S(1)}, bf16[272,256]{1,0:T(8,128)(2,1)S(1)}, u32[]{:S(2)}, u32[]{:S(2)}) collective-permute-start(bf16[272,256]{1,0:T(8,128)(2,1)S(1)} %collective-permute-done.refs_2_), channel_id=1, source_target_pairs={{0,32},{8,40},{16,48},{24,56},{32,64},{40,72},{48,80},{56,88},{64,... | collective-permute-start | bytes 417800 | tf_op jit(solution)/shard_map/ppermute | solution.py:142
  43.9 3.0 %collective-permute-start.1 = (bf16[272,256]{1,0:T(8,128)(2,1)S(1)}, bf16[272,256]{1,0:T(8,128)(2,1)S(1)}, u32[]{:S(2)}, u32[]{:S(2)}) collective-permute-start(bf16[272,256]{1,0:T(8,128)(2,1)S(1)} %collective-permute-done.refs_2_), channel_id=1, source_target_pairs={{0,992},{8,1000},{16,1008},{24,1016},{32,0},{40,8},{48,16},{56,24}... | collective-permute-start | bytes 417800 | tf_op jit(solution)/shard_map/ppermute | solution.py:142
  46.9 1.7 %shard_map.57 = (f32[256,4]{1,0:T(8,128)S(1)}, f32[256,512]{1,0:T(8,128)S(1)}, f32[256,512]{1,0:T(8,128)S(1)}) custom-call(bf16[256,512]{1,0:T(8,128)(2,1)S(1)} %copy-done.4, f32[256,1]{1,0:T(8,128)S(1)} %copy.10.refs_1_.refs_2_, bf16[272,256]{1,0:T(8,128)(2,1)S(1)} %collective-permute-done.refs_2_, f32[256,4]{1,0:T(8,128)S(1)} %get-tuple-element.35.refs_3_, ...), custom_call_target="tpu_custom_call" | custom-call | flops 805306368 | bytes 2236416 | tf_op jit(solution)/shard_map/pallas_call | solution.py:125
  48.6 3.6 %collective-permute-done.2.refs_2_ = bf16[272,256]{1,0:T(8,128)(2,1)S(1)} collective-permute-done((bf16[272,256]{1,0:T(8,128)(2,1)S(1)}, bf16[272,256]{1,0:T(8,128)(2,1)S(1)}, u32[]{:S(2)}, u32[]{:S(2)}) %collective-permute-start.2) | collective-permute-done | bytes 139296 | tf_op jit(solution)/shard_map/ppermute | solution.py:142
  52.1 16.7 %collective-permute-done.1.refs_3_ = bf16[272,256]{1,0:T(8,128)(2,1)S(1)} collective-permute-done((bf16[272,256]{1,0:T(8,128)(2,1)S(1)}, bf16[272,256]{1,0:T(8,128)(2,1)S(1)}, u32[]{:S(2)}, u32[]{:S(2)}) %collective-permute-start.1) | collective-permute-done | bytes 139296 | tf_op jit(solution)/shard_map/ppermute | solution.py:142
  68.8 1.9 %collective-permute-start.7 = (bf16[1088,256]{1,0:T(8,128)(2,1)S(1)}, bf16[1088,256]{1,0:T(8,128)(2,1)S(1)}, u32[]{:S(2)}, u32[]{:S(2)}) collective-permute-start(bf16[1088,256]{1,0:T(8,128)(2,1)S(1)} %pad_maximum_fusion), channel_id=1, source_target_pairs={{0,8},{8,16},{16,24},{24,32},{32,40},{40,48},{48,56},{56,64},{64,7... | collective-permute-start | bytes 1671176 | tf_op jit(solution)/shard_map/ppermute | solution.py:142
  71.6 10.5 %collective-permute-start.5 = (bf16[816,256]{1,0:T(8,128)(2,1)}, bf16[816,256]{1,0:T(8,128)(2,1)S(1)}, u32[]{:S(2)}, u32[]{:S(2)}) collective-permute-start(bf16[816,256]{1,0:T(8,128)(2,1)} %slice.20), channel_id=1, source_target_pairs={{0,1008},{8,1016},{16,0},{24,8},{32,16},{40,24},{48,32},{56,40},{6... | collective-permute-start | bytes 1253384 | tf_op jit(solution)/shard_map/ppermute | solution.py:142
  82.1 1.9 %collective-permute-start.6 = (bf16[272,256]{1,0:T(8,128)(2,1)S(1)}, bf16[272,256]{1,0:T(8,128)(2,1)S(1)}, u32[]{:S(2)}, u32[]{:S(2)}) collective-permute-start(bf16[272,256]{1,0:T(8,128)(2,1)S(1)} %collective-permute-done.2.refs_2_), channel_id=1, source_target_pairs={{0,24},{8,32},{16,40},{24,48},{32,56},{40,64},{48,72},{56,80},{64,... | collective-permute-start | bytes 417800 | tf_op jit(solution)/shard_map/ppermute | solution.py:142
  84.0 2.0 %collective-permute-start.3 = (bf16[816,256]{1,0:T(8,128)(2,1)}, bf16[816,256]{1,0:T(8,128)(2,1)S(1)}, u32[]{:S(2)}, u32[]{:S(2)}) collective-permute-start(bf16[816,256]{1,0:T(8,128)(2,1)} %slice.20), channel_id=1, source_target_pairs={{0,1016},{8,0},{16,8},{24,16},{32,24},{40,32},{48,40},{56,48},{64,... | collective-permute-start | bytes 1253384 | tf_op jit(solution)/shard_map/ppermute | solution.py:142
  86.1 3.0 %collective-permute-start.4 = (bf16[272,256]{1,0:T(8,128)(2,1)S(1)}, bf16[272,256]{1,0:T(8,128)(2,1)S(1)}, u32[]{:S(2)}, u32[]{:S(2)}) collective-permute-start(bf16[272,256]{1,0:T(8,128)(2,1)S(1)} %collective-permute-done.2.refs_2_), channel_id=1, source_target_pairs={{0,16},{8,24},{16,32},{24,40},{32,48},{40,56},{48,64},{56,72},{64,... | collective-permute-start | bytes 417800 | tf_op jit(solution)/shard_map/ppermute | solution.py:142
  89.1 2.1 %shard_map.58 = (f32[256,4]{1,0:T(8,128)S(1)}, f32[256,512]{1,0:T(8,128)S(1)}, f32[256,512]{1,0:T(8,128)S(1)}) custom-call(bf16[256,512]{1,0:T(8,128)(2,1)S(1)} %copy-done.4, f32[256,1]{1,0:T(8,128)S(1)} %copy.10.refs_1_.refs_2_, bf16[272,256]{1,0:T(8,128)(2,1)S(1)} %collective-permute-done.2.refs_2_, bf16[272,256]{1,0:T(8,128)(2,1)S(1)} %collective-permute-done.1.refs_3_, ...), custom_call_target="tpu_custom_call" | custom-call | flops 1610612736 | bytes 2375680 | tf_op jit(solution)/shard_map/pallas_call | solution.py:125
  91.2 6.8 %collective-permute-done.6.refs_3_ = bf16[272,256]{1,0:T(8,128)(2,1)S(1)} collective-permute-done((bf16[272,256]{1,0:T(8,128)(2,1)S(1)}, bf16[272,256]{1,0:T(8,128)(2,1)S(1)}, u32[]{:S(2)}, u32[]{:S(2)}) %collective-permute-start.6) | collective-permute-done | bytes 139296 | tf_op jit(solution)/shard_map/ppermute | solution.py:142
  99.4 4.5 %shard_map.59 = (f32[256,4]{1,0:T(8,128)S(1)}, f32[256,512]{1,0:T(8,128)S(1)}, f32[256,512]{1,0:T(8,128)S(1)}) custom-call(bf16[256,512]{1,0:T(8,128)(2,1)S(1)} %copy-done.4, f32[256,1]{1,0:T(8,128)S(1)} %copy.10.refs_1_.refs_2_, bf16[816,256]{1,0:T(8,128)(2,1)S(1)} %collective-permute-done.5.refs_2_, bf16[272,256]{1,0:T(8,128)(2,1)S(1)} %collective-permute-done.6.refs_3_, ...), custom_call_target="tpu_custom_call" | custom-call | flops 6442450944 | bytes 3211264 | tf_op jit(solution)/shard_map/pallas_call | solution.py:125
  104.3 4.2 %collective-permute-done.3.refs_3_ = bf16[816,256]{1,0:T(8,128)(2,1)S(1)} collective-permute-done((bf16[816,256]{1,0:T(8,128)(2,1)}, bf16[816,256]{1,0:T(8,128)(2,1)S(1)}, u32[]{:S(2)}, u32[]{:S(2)}) %collective-permute-start.3) | collective-permute-done | bytes 417824 | tf_op jit(solution)/shard_map/ppermute | solution.py:142
  108.5 4.5 %shard_map.60 = (bf16[4,256,512]{2,1,0:T(8,128)(2,1)S(1)}, bf16[4,256,512]{2,1,0:T(8,128)(2,1)S(1)}) custom-call(s32[2]{0:T(128)S(1)} %pad_add_fusion.refs_0_, bf16[256,512]{1,0:T(8,128)(2,1)S(1)} %copy-done.4, f32[256,1]{1,0:T(8,128)S(1)} %copy.10.refs_1_.refs_2_, bf16[816,256]{1,0:T(8,128)(2,1)S(1)} %collective-permute-done.3.refs_3_, ...), custom_call_target="tpu_custom_call" | custom-call | flops 4294967296 | bytes 8945664 | tf_op jit(solution)/shard_map/pallas_call | solution.py:125
  113.0 3.5 %collective-permute-start.8 = (bf16[4,256,512]{2,1,0:T(8,128)(2,1)S(1)}, bf16[4,256,512]{2,1,0:T(8,128)(2,1)S(1)}, u32[]{:S(2)}, u32[]{:S(2)}) collective-permute-start(bf16[4,256,512]{2,1,0:T(8,128)(2,1)S(1)} %get-tuple-element.52), channel_id=1, source_target_pairs={{0,1},{1,0},{2,3},{3,2},{4,5},{5,4},{6,7},{7,6},{8,9},{9,8},{10,11... | collective-permute-start | bytes 3145736 | tf_op jit(solution)/shard_map/ppermute | solution.py:193
  116.5 2.3 %collective-permute-done.8 = bf16[4,256,512]{2,1,0:T(8,128)(2,1)S(1)} collective-permute-done((bf16[4,256,512]{2,1,0:T(8,128)(2,1)S(1)}, bf16[4,256,512]{2,1,0:T(8,128)(2,1)S(1)}, u32[]{:S(2)}, u32[]{:S(2)}) %collective-permute-start.8) | collective-permute-done | bytes 1048608 | tf_op jit(solution)/shard_map/ppermute | solution.py:193
  119.2 4.7 %collective-permute-start.10 = (bf16[256,512]{1,0:T(8,128)(2,1)S(1)}, bf16[256,512]{1,0:T(8,128)(2,1)S(1)}, u32[]{:S(2)}, u32[]{:S(2)}) collective-permute-start(bf16[256,512]{1,0:T(8,128)(2,1)S(1)} %get-tuple-element.55), channel_id=1, source_target_pairs={{0,6},{2,0},{4,2},{6,4},{1,7},{3,1},{5,3},{7,5},{8,14},{10,8},{12,... | collective-permute-start | bytes 786440 | tf_op jit(solution)/shard_map/ppermute | solution.py:147
  123.8 2.3 %collective-permute-start.11 = (bf16[256,512]{1,0:T(8,128)(2,1)S(1)}, bf16[256,512]{1,0:T(8,128)(2,1)S(1)}, u32[]{:S(2)}, u32[]{:S(2)}) collective-permute-start(bf16[256,512]{1,0:T(8,128)(2,1)S(1)} %get-tuple-element.54), channel_id=1, source_target_pairs={{0,4},{2,6},{4,0},{6,2},{1,5},{3,7},{5,1},{7,3},{8,12},{10,14},{12... | collective-permute-start | bytes 786440 | tf_op jit(solution)/shard_map/ppermute | solution.py:147
  126.1 2.6 %collective-permute-start.9 = (bf16[256,512]{1,0:T(8,128)(2,1)S(1)}, bf16[256,512]{1,0:T(8,128)(2,1)S(1)}, u32[]{:S(2)}, u32[]{:S(2)}) collective-permute-start(bf16[256,512]{1,0:T(8,128)(2,1)S(1)} %get-tuple-element.53), channel_id=1, source_target_pairs={{0,2},{2,4},{4,6},{6,0},{1,3},{3,5},{5,7},{7,1},{8,10},{10,12},{12... | collective-permute-start | bytes 786440 | tf_op jit(solution)/shard_map/ppermute | solution.py:147
  128.7 5.9 %collective-permute-done.10 = bf16[256,512]{1,0:T(8,128)(2,1)S(1)} collective-permute-done((bf16[256,512]{1,0:T(8,128)(2,1)S(1)}, bf16[256,512]{1,0:T(8,128)(2,1)S(1)}, u32[]{:S(2)}, u32[]{:S(2)}) %collective-permute-start.10) | collective-permute-done | bytes 262176 | tf_op jit(solution)/shard_map/ppermute | solution.py:147
  134.6 6.5 %collective-permute-done.9 = bf16[256,512]{1,0:T(8,128)(2,1)S(1)} collective-permute-done((bf16[256,512]{1,0:T(8,128)(2,1)S(1)}, bf16[256,512]{1,0:T(8,128)(2,1)S(1)}, u32[]{:S(2)}, u32[]{:S(2)}) %collective-permute-start.9) | collective-permute-done | bytes 262176 | tf_op jit(solution)/shard_map/ppermute | solution.py:147
  (24 shorter events, 9.0 us)
Async XLA Ops:
  1.6 29.1 %collective-permute-start = (bf16[272,256]{1,0:T(8,128)(2,1)}, bf16[272,256]{1,0:T(8,128)(2,1)S(1)}, u32[]{:S(2)}, u32[]{:S(2)}) collective-permute-start(bf16[272,256]{1,0:T(8,128)(2,1)} %shard_map.55.refs_2_), channel_id=1, source_target_pairs={{0,64},{8,72},{16,80},{24,88},{32,96},{40,104},{48,112},{56,120},{... | collective-permute-start | bytes 417800 | tf_op jit(solution)/shard_map/ppermute | solution.py:142
  18.7 0.9 copy-start
  19.6 0.9 copy-start.3
  20.5 26.4 %copy-start.4 = (bf16[256,512]{1,0:T(8,128)(2,1)S(1)}, bf16[256,512]{1,0:T(8,128)(2,1)}, u32[]{:S(2)}) copy-start(bf16[256,512]{1,0:T(8,128)(2,1)} %refs_1_.1) | copy-start | bytes 786436
  30.7 38.1 %copy-start.1 = (bf16[272,256]{1,0:T(8,128)(2,1)S(1)}, bf16[272,256]{1,0:T(8,128)(2,1)}, u32[]{:S(2)}) copy-start(bf16[272,256]{1,0:T(8,128)(2,1)} %shard_map.55.refs_2_) | copy-start | bytes 417796
  30.7 21.5 %collective-permute-start.2 = (bf16[272,256]{1,0:T(8,128)(2,1)S(1)}, bf16[272,256]{1,0:T(8,128)(2,1)S(1)}, u32[]{:S(2)}, u32[]{:S(2)}) collective-permute-start(bf16[272,256]{1,0:T(8,128)(2,1)S(1)} %collective-permute-done.refs_2_), channel_id=1, source_target_pairs={{0,32},{8,40},{16,48},{24,56},{32,64},{40,72},{48,80},{56,88},{64,... | collective-permute-start | bytes 417800 | tf_op jit(solution)/shard_map/ppermute | solution.py:142
  43.9 25.0 %collective-permute-start.1 = (bf16[272,256]{1,0:T(8,128)(2,1)S(1)}, bf16[272,256]{1,0:T(8,128)(2,1)S(1)}, u32[]{:S(2)}, u32[]{:S(2)}) collective-permute-start(bf16[272,256]{1,0:T(8,128)(2,1)S(1)} %collective-permute-done.refs_2_), channel_id=1, source_target_pairs={{0,992},{8,1000},{16,1008},{24,1016},{32,0},{40,8},{48,16},{56,24}... | collective-permute-start | bytes 417800 | tf_op jit(solution)/shard_map/ppermute | solution.py:142
  68.8 30.5 %collective-permute-start.7 = (bf16[1088,256]{1,0:T(8,128)(2,1)S(1)}, bf16[1088,256]{1,0:T(8,128)(2,1)S(1)}, u32[]{:S(2)}, u32[]{:S(2)}) collective-permute-start(bf16[1088,256]{1,0:T(8,128)(2,1)S(1)} %pad_maximum_fusion), channel_id=1, source_target_pairs={{0,8},{8,16},{16,24},{24,32},{32,40},{40,48},{48,56},{56,64},{64,7... | collective-permute-start | bytes 1671176 | tf_op jit(solution)/shard_map/ppermute | solution.py:142
  71.6 27.8 %collective-permute-start.5 = (bf16[816,256]{1,0:T(8,128)(2,1)}, bf16[816,256]{1,0:T(8,128)(2,1)S(1)}, u32[]{:S(2)}, u32[]{:S(2)}) collective-permute-start(bf16[816,256]{1,0:T(8,128)(2,1)} %slice.20), channel_id=1, source_target_pairs={{0,1008},{8,1016},{16,0},{24,8},{32,16},{40,24},{48,32},{56,40},{6... | collective-permute-start | bytes 1253384 | tf_op jit(solution)/shard_map/ppermute | solution.py:142
  82.1 15.8 %collective-permute-start.6 = (bf16[272,256]{1,0:T(8,128)(2,1)S(1)}, bf16[272,256]{1,0:T(8,128)(2,1)S(1)}, u32[]{:S(2)}, u32[]{:S(2)}) collective-permute-start(bf16[272,256]{1,0:T(8,128)(2,1)S(1)} %collective-permute-done.2.refs_2_), channel_id=1, source_target_pairs={{0,24},{8,32},{16,40},{24,48},{32,56},{40,64},{48,72},{56,80},{64,... | collective-permute-start | bytes 417800 | tf_op jit(solution)/shard_map/ppermute | solution.py:142
  84.0 24.5 %collective-permute-start.3 = (bf16[816,256]{1,0:T(8,128)(2,1)}, bf16[816,256]{1,0:T(8,128)(2,1)S(1)}, u32[]{:S(2)}, u32[]{:S(2)}) collective-permute-start(bf16[816,256]{1,0:T(8,128)(2,1)} %slice.20), channel_id=1, source_target_pairs={{0,1016},{8,0},{16,8},{24,16},{32,24},{40,32},{48,40},{56,48},{64,... | collective-permute-start | bytes 1253384 | tf_op jit(solution)/shard_map/ppermute | solution.py:142
  86.1 18.2 %collective-permute-start.4 = (bf16[272,256]{1,0:T(8,128)(2,1)S(1)}, bf16[272,256]{1,0:T(8,128)(2,1)S(1)}, u32[]{:S(2)}, u32[]{:S(2)}) collective-permute-start(bf16[272,256]{1,0:T(8,128)(2,1)S(1)} %collective-permute-done.2.refs_2_), channel_id=1, source_target_pairs={{0,16},{8,24},{16,32},{24,40},{32,48},{40,56},{48,64},{56,72},{64,... | collective-permute-start | bytes 417800 | tf_op jit(solution)/shard_map/ppermute | solution.py:142
  99.4 9.1 %copy-start.2 = (bf16[512,4096]{1,0:T(8,128)(2,1)S(1)}, bf16[512,4096]{1,0:T(8,128)(2,1)}, u32[]{:S(2)}) copy-start(bf16[512,4096]{1,0:T(8,128)(2,1)} %refs_8_.1) | copy-start | bytes 12582916
  113.0 5.8 %collective-permute-start.8 = (bf16[4,256,512]{2,1,0:T(8,128)(2,1)S(1)}, bf16[4,256,512]{2,1,0:T(8,128)(2,1)S(1)}, u32[]{:S(2)}, u32[]{:S(2)}) collective-permute-start(bf16[4,256,512]{2,1,0:T(8,128)(2,1)S(1)} %get-tuple-element.52), channel_id=1, source_target_pairs={{0,1},{1,0},{2,3},{3,2},{4,5},{5,4},{6,7},{7,6},{8,9},{9,8},{10,11... | collective-permute-start | bytes 3145736 | tf_op jit(solution)/shard_map/ppermute | solution.py:193
  119.2 15.4 %collective-permute-start.10 = (bf16[256,512]{1,0:T(8,128)(2,1)S(1)}, bf16[256,512]{1,0:T(8,128)(2,1)S(1)}, u32[]{:S(2)}, u32[]{:S(2)}) collective-permute-start(bf16[256,512]{1,0:T(8,128)(2,1)S(1)} %get-tuple-element.55), channel_id=1, source_target_pairs={{0,6},{2,0},{4,2},{6,4},{1,7},{3,1},{5,3},{7,5},{8,14},{10,8},{12,... | collective-permute-start | bytes 786440 | tf_op jit(solution)/shard_map/ppermute | solution.py:147
  123.8 10.8 %collective-permute-start.11 = (bf16[256,512]{1,0:T(8,128)(2,1)S(1)}, bf16[256,512]{1,0:T(8,128)(2,1)S(1)}, u32[]{:S(2)}, u32[]{:S(2)}) collective-permute-start(bf16[256,512]{1,0:T(8,128)(2,1)S(1)} %get-tuple-element.54), channel_id=1, source_target_pairs={{0,4},{2,6},{4,0},{6,2},{1,5},{3,7},{5,1},{7,3},{8,12},{10,14},{12... | collective-permute-start | bytes 786440 | tf_op jit(solution)/shard_map/ppermute | solution.py:147
  126.1 15.0 %collective-permute-start.9 = (bf16[256,512]{1,0:T(8,128)(2,1)S(1)}, bf16[256,512]{1,0:T(8,128)(2,1)S(1)}, u32[]{:S(2)}, u32[]{:S(2)}) collective-permute-start(bf16[256,512]{1,0:T(8,128)(2,1)S(1)} %get-tuple-element.53), channel_id=1, source_target_pairs={{0,2},{2,4},{4,6},{6,0},{1,3},{3,5},{5,7},{7,1},{8,10},{10,12},{12... | collective-permute-start | bytes 786440 | tf_op jit(solution)/shard_map/ppermute | solution.py:147

commit v5 on v3

--- a/solution.py
+++ b/solution.py
@@ -156,24 +156,24 @@
 
 
 def gather_and_attend(queries, marks, own, weight, place):
-    back8 = along(own, 8)
+    back4 = along(own, 4)
     state = run_stage(queries, marks, [own])
+    own, state = after(own, state)
+    back1 = along(own, 1)
+    back8 = along(back4, 4)
+    state = run_stage(queries, marks, [back4], state)
+    back4, state = after(back4, state)
+    back2, back3, back5 = [along(back4, n) for n in (-2, -1, 1)]
+    back12 = along(back8, 4)
+    state = run_stage(queries, marks, [back8, back1], state)
     back8, state = after(back8, state)
-    back12 = along(back8, 4)
-    back4 = along(back8, -4)
-    state = run_stage(queries, marks, [back8], state)
-    back12, state = after(back12, state)
-    far = jnp.concatenate([back8, back12])
-    near = jnp.concatenate([back4, back8])
-    back10_14 = along(far, 2)
-    back2_6 = along(near, -2)
-    back9_13 = along(far, 1)
-    near, back10_14 = after(near, back10_14)
-    back3_7 = along(near, -1)
-    back11_15 = along(back10_14, 1)
-    back1_5 = along(back2_6, -1)
-    state = run_stage(queries, marks, [back12, back4, back10_14, back2_6, back9_13, back3_7], state)
-    return run_stage(queries, marks, [back11_15, back1_5], state, weight, place)
+    back6, back7, back9 = [along(back8, n) for n in (-2, -1, 1)]
+    back15, back10, back14 = [along(back12, n) for n in (3, -2, 2)]
+    back11, back13 = [along(back12, n) for n in (-1, 1)]
+    near = [back5, back3, back2, back9, back7, back6, back12]
+    state = run_stage(queries, marks, near, state)
+    state = run_stage(queries, marks, [back10, back15], state)
+    return run_stage(queries, marks, [back14, back11, back13], state, weight, place)
 
 
 def join(key_ref, value_ref, ids_ref, joined_ref):

time: 141 us -> 136 us (0.965)
  waiting for transfers between devices: 40.1 us -> 28.5 us
  starting transfers between devices: 80.1 us -> 85.6 us
  Pallas kernels: 14.2 us -> 17.7 us
  local copies, waits for them, and re-layouts: 3.4 us -> 1.14 us
    ppermute x9 -> x15, waiting for transfers between devices: 32.3 us -> 20.6 us  [along(): lax.ppermute(value, 'tok', [(i, (i + by) % size) for i in range(size)])]
    ppermute x9 -> x15, starting transfers between devices: 64.5 us -> 70.4 us  [along(): lax.ppermute(value, 'tok', [(i, (i + by) % size) for i in range(size)])]
    pallas_call x4 -> x6, Pallas kernels: 12.6 us -> 16.1 us  [run_stage(): pl.pallas_call(functools.partial(attend_stage, first, final, len(arrays),...]
    unnamed x10 -> x6, local copies, waits for them, and re-layouts: 3.2 us -> 0.96 us
  transfers between devices with their start and end apart: 13 -> 19, of which waited for: 6 -> 6; matrix products, arithmetic and copies ran while one was open for 1% -> 1% of each run, Pallas kernels for 6% -> 9%
where the time goes in v5:
time: 136 us; the launch traced here: 135 us
  starting transfers between devices  85.6 us (63%)
  waiting for transfers between devices  28.5 us (21%)
  Pallas kernels  17.7 us (13%)
  other arithmetic  1.92 us (1%)
    ppermute x15, starting transfers between devices, along(): lax.ppermute(value, 'tok', [(i, (i + by) % size) for i in range(size)])  70.4 us
    ppermute x15, waiting for transfers between devices, along(): lax.ppermute(value, 'tok', [(i, (i + by) % size) for i in range(size)])  20.6 us
    pallas_call x6, Pallas kernels, run_stage(): pl.pallas_call(functools.partial(attend_stage, first, final, len(arrays),...  16.1 us
    ppermute x3, starting transfers between devices, around(): lax.ppermute(value, 'head', [(i, (i + by) % size) for i in range(size)])  11.3 us
    ppermute x3, waiting for transfers between devices, around(): lax.ppermute(value, 'head', [(i, (i + by) % size) for i in range(size)])  5.55 us
    ppermute x1, starting transfers between devices, per_device(): pair = plus(keep, lax.ppermute(send, 'srv', [(0, 1), (1, 0)]))  3.89 us
  transfers between devices with their start and end apart: 19, of which 6 were waited for; matrix products, arithmetic and copies ran while one was open for 1% of the time, Pallas kernels for 9%

profile of v5, /device:TPU:1, one launch (start us, length us, event | category | flops | bytes accessed | tf_op | source)
XLA Modules:
  0.0 135.2 jit_solution(655798058404372694)
XLA Ops:
  1.6 9.6 %collective-permute-start = (bf16[272,256]{1,0:T(8,128)(2,1)}, bf16[272,256]{1,0:T(8,128)(2,1)S(1)}, u32[]{:S(2)}, u32[]{:S(2)}) collective-permute-start(bf16[272,256]{1,0:T(8,128)(2,1)} %shard_map.55.refs_2_), channel_id=1, source_target_pairs={{0,32},{8,40},{16,48},{24,56},{32,64},{40,72},{48,80},{56,88},{64,... | collective-permute-start | bytes 417800 | tf_op jit(solution)/shard_map/ppermute | solution.py:142
  14.8 12.8 %collective-permute-done.refs_2_ = bf16[272,256]{1,0:T(8,128)(2,1)S(1)} collective-permute-done((bf16[272,256]{1,0:T(8,128)(2,1)}, bf16[272,256]{1,0:T(8,128)(2,1)S(1)}, u32[]{:S(2)}, u32[]{:S(2)}) %collective-permute-start) | collective-permute-done | bytes 139296 | tf_op jit(solution)/shard_map/ppermute | solution.py:142
  27.6 4.9 %collective-permute-start.1 = (bf16[272,256]{1,0:T(8,128)(2,1)S(1)}, bf16[272,256]{1,0:T(8,128)(2,1)S(1)}, u32[]{:S(2)}, u32[]{:S(2)}) collective-permute-start(bf16[272,256]{1,0:T(8,128)(2,1)S(1)} %collective-permute-done.refs_2_), channel_id=1, source_target_pairs={{0,32},{8,40},{16,48},{24,56},{32,64},{40,72},{48,80},{56,88},{64,... | collective-permute-start | bytes 417800 | tf_op jit(solution)/shard_map/ppermute | solution.py:142
  32.5 4.5 %collective-permute-start.11 = (bf16[272,256]{1,0:T(8,128)(2,1)}, bf16[272,256]{1,0:T(8,128)(2,1)S(1)}, u32[]{:S(2)}, u32[]{:S(2)}) collective-permute-start(bf16[272,256]{1,0:T(8,128)(2,1)} %shard_map.55.refs_2_), channel_id=1, source_target_pairs={{0,8},{8,16},{16,24},{24,32},{32,40},{40,48},{48,56},{56,64},{64,7... | collective-permute-start | bytes 417800 | tf_op jit(solution)/shard_map/ppermute | solution.py:142
  38.7 13.2 %collective-permute-start.10 = (bf16[272,256]{1,0:T(8,128)(2,1)S(1)}, bf16[272,256]{1,0:T(8,128)(2,1)S(1)}, u32[]{:S(2)}, u32[]{:S(2)}) collective-permute-start(bf16[272,256]{1,0:T(8,128)(2,1)S(1)} %collective-permute-done.refs_2_), channel_id=1, source_target_pairs={{0,1008},{8,1016},{16,0},{24,8},{32,16},{40,24},{48,32},{56,40},{6... | collective-permute-start | bytes 417800 | tf_op jit(solution)/shard_map/ppermute | solution.py:142
  52.0 1.9 %collective-permute-start.8 = (bf16[272,256]{1,0:T(8,128)(2,1)S(1)}, bf16[272,256]{1,0:T(8,128)(2,1)S(1)}, u32[]{:S(2)}, u32[]{:S(2)}) collective-permute-start(bf16[272,256]{1,0:T(8,128)(2,1)S(1)} %collective-permute-done.refs_2_), channel_id=1, source_target_pairs={{0,8},{8,16},{16,24},{24,32},{32,40},{40,48},{48,56},{56,64},{64,7... | collective-permute-start | bytes 417800 | tf_op jit(solution)/shard_map/ppermute | solution.py:142
  53.9 6.7 %collective-permute-start.9 = (bf16[272,256]{1,0:T(8,128)(2,1)S(1)}, bf16[272,256]{1,0:T(8,128)(2,1)S(1)}, u32[]{:S(2)}, u32[]{:S(2)}) collective-permute-start(bf16[272,256]{1,0:T(8,128)(2,1)S(1)} %collective-permute-done.refs_2_), channel_id=1, source_target_pairs={{0,1016},{8,0},{16,8},{24,16},{32,24},{40,32},{48,40},{56,48},{64,... | collective-permute-start | bytes 417800 | tf_op jit(solution)/shard_map/ppermute | solution.py:142
  62.5 2.1 %shard_map.58 = (f32[256,4]{1,0:T(8,128)S(1)}, f32[256,512]{1,0:T(8,128)S(1)}, f32[256,512]{1,0:T(8,128)S(1)}) custom-call(bf16[256,512]{1,0:T(8,128)(2,1)S(1)} %copy-done.2, f32[256,1]{1,0:T(8,128)S(1)} %copy.11.refs_1_.refs_2_, bf16[272,256]{1,0:T(8,128)(2,1)S(1)} %collective-permute-done.1.refs_2_, bf16[272,256]{1,0:T(8,128)(2,1)S(1)} %collective-permute-done.11.refs_3_, ...), custom_call_target="tpu_custom_call" | custom-call | flops 1610612736 | bytes 2375680 | tf_op jit(solution)/shard_map/pallas_call | solution.py:125
  66.6 6.7 %collective-permute-start.13 = (bf16[272,256]{1,0:T(8,128)(2,1)S(1)}, bf16[272,256]{1,0:T(8,128)(2,1)S(1)}, u32[]{:S(2)}, u32[]{:S(2)}) collective-permute-start(bf16[272,256]{1,0:T(8,128)(2,1)S(1)} %collective-permute-done.1.refs_2_), channel_id=1, source_target_pairs={{0,1016},{8,0},{16,8},{24,16},{32,24},{40,32},{48,40},{56,48},{64,... | collective-permute-start | bytes 417800 | tf_op jit(solution)/shard_map/ppermute | solution.py:142
  73.3 1.9 %collective-permute-start.14 = (bf16[272,256]{1,0:T(8,128)(2,1)S(1)}, bf16[272,256]{1,0:T(8,128)(2,1)S(1)}, u32[]{:S(2)}, u32[]{:S(2)}) collective-permute-start(bf16[272,256]{1,0:T(8,128)(2,1)S(1)} %collective-permute-done.1.refs_2_), channel_id=1, source_target_pairs={{0,1008},{8,1016},{16,0},{24,8},{32,16},{40,24},{48,32},{56,40},{6... | collective-permute-start | bytes 417800 | tf_op jit(solution)/shard_map/ppermute | solution.py:142
  75.3 3.0 %collective-permute-done.2.refs_8_ = bf16[272,256]{1,0:T(8,128)(2,1)S(1)} collective-permute-done((bf16[272,256]{1,0:T(8,128)(2,1)S(1)}, bf16[272,256]{1,0:T(8,128)(2,1)S(1)}, u32[]{:S(2)}, u32[]{:S(2)}) %collective-permute-start.2) | collective-permute-done | bytes 139296 | tf_op jit(solution)/shard_map/ppermute | solution.py:142
  78.3 4.5 %collective-permute-start.6 = (bf16[272,256]{1,0:T(8,128)(2,1)S(1)}, bf16[272,256]{1,0:T(8,128)(2,1)S(1)}, u32[]{:S(2)}, u32[]{:S(2)}) collective-permute-start(bf16[272,256]{1,0:T(8,128)(2,1)S(1)} %collective-permute-done.2.refs_8_), channel_id=1, source_target_pairs={{0,1008},{8,1016},{16,0},{24,8},{32,16},{40,24},{48,32},{56,40},{6... | collective-permute-start | bytes 417800 | tf_op jit(solution)/shard_map/ppermute | solution.py:142
  86.7 6.7 %collective-permute-start.4 = (bf16[272,256]{1,0:T(8,128)(2,1)S(1)}, bf16[272,256]{1,0:T(8,128)(2,1)S(1)}, u32[]{:S(2)}, u32[]{:S(2)}) collective-permute-start(bf16[272,256]{1,0:T(8,128)(2,1)S(1)} %collective-permute-done.2.refs_8_), channel_id=1, source_target_pairs={{0,1016},{8,0},{16,8},{24,16},{32,24},{40,32},{48,40},{56,48},{64,... | collective-permute-start | bytes 417800 | tf_op jit(solution)/shard_map/ppermute | solution.py:142
  93.4 2.1 %collective-permute-start.5 = (bf16[272,256]{1,0:T(8,128)(2,1)S(1)}, bf16[272,256]{1,0:T(8,128)(2,1)S(1)}, u32[]{:S(2)}, u32[]{:S(2)}) collective-permute-start(bf16[272,256]{1,0:T(8,128)(2,1)S(1)} %collective-permute-done.2.refs_8_), channel_id=1, source_target_pairs={{0,8},{8,16},{16,24},{24,32},{32,40},{40,48},{48,56},{56,64},{64,7... | collective-permute-start | bytes 417800 | tf_op jit(solution)/shard_map/ppermute | solution.py:142
  95.5 4.1 %shard_map.59 = (f32[256,4]{1,0:T(8,128)S(1)}, f32[256,512]{1,0:T(8,128)S(1)}, f32[256,512]{1,0:T(8,128)S(1)}) custom-call(bf16[256,512]{1,0:T(8,128)(2,1)S(1)} %copy-done.2, f32[256,1]{1,0:T(8,128)S(1)} %copy.11.refs_1_.refs_2_, bf16[272,256]{1,0:T(8,128)(2,1)S(1)} %collective-permute-done.8.refs_2_, bf16[272,256]{1,0:T(8,128)(2,1)S(1)} %collective-permute-done.9.refs_3_, ...), custom_call_target="tpu_custom_call" | custom-call | flops 5637144576 | bytes 3072000 | tf_op jit(solution)/shard_map/pallas_call | solution.py:125
  100.0 2.1 %shard_map.60 = (f32[256,4]{1,0:T(8,128)S(1)}, f32[256,512]{1,0:T(8,128)S(1)}, f32[256,512]{1,0:T(8,128)S(1)}) custom-call(bf16[256,512]{1,0:T(8,128)(2,1)S(1)} %copy-done.2, f32[256,1]{1,0:T(8,128)S(1)} %copy.11.refs_1_.refs_2_, bf16[272,256]{1,0:T(8,128)(2,1)S(1)} %collective-permute-done.6.refs_2_, bf16[272,256]{1,0:T(8,128)(2,1)S(1)} %collective-permute-done.7.refs_3_, ...), custom_call_target="tpu_custom_call" | custom-call | flops 1610612736 | bytes 2375680 | tf_op jit(solution)/shard_map/pallas_call | solution.py:125
  102.1 4.4 %collective-permute-done.5.refs_5_ = bf16[272,256]{1,0:T(8,128)(2,1)S(1)} collective-permute-done((bf16[272,256]{1,0:T(8,128)(2,1)S(1)}, bf16[272,256]{1,0:T(8,128)(2,1)S(1)}, u32[]{:S(2)}, u32[]{:S(2)}) %collective-permute-start.5) | collective-permute-done | bytes 139296 | tf_op jit(solution)/shard_map/ppermute | solution.py:142
  106.5 4.4 %shard_map.61 = (bf16[4,256,512]{2,1,0:T(8,128)(2,1)S(1)}, bf16[4,256,512]{2,1,0:T(8,128)(2,1)S(1)}) custom-call(s32[2]{0:T(128)S(1)} %pad_add_fusion.refs_0_, bf16[256,512]{1,0:T(8,128)(2,1)S(1)} %copy-done.2, f32[256,1]{1,0:T(8,128)S(1)} %copy.11.refs_1_.refs_2_, bf16[272,256]{1,0:T(8,128)(2,1)S(1)} %collective-permute-done.3.refs_3_, ...), custom_call_target="tpu_custom_call" | custom-call | flops 3489660928 | bytes 8806400 | tf_op jit(solution)/shard_map/pallas_call | solution.py:125
  110.9 3.9 %collective-permute-start.15 = (bf16[4,256,512]{2,1,0:T(8,128)(2,1)S(1)}, bf16[4,256,512]{2,1,0:T(8,128)(2,1)S(1)}, u32[]{:S(2)}, u32[]{:S(2)}) collective-permute-start(bf16[4,256,512]{2,1,0:T(8,128)(2,1)S(1)} %get-tuple-element.66), channel_id=1, source_target_pairs={{0,1},{1,0},{2,3},{3,2},{4,5},{5,4},{6,7},{7,6},{8,9},{9,8},{10,11... | collective-permute-start | bytes 3145736 | tf_op jit(solution)/shard_map/ppermute | solution.py:194
  114.8 2.3 %collective-permute-done.15 = bf16[4,256,512]{2,1,0:T(8,128)(2,1)S(1)} collective-permute-done((bf16[4,256,512]{2,1,0:T(8,128)(2,1)S(1)}, bf16[4,256,512]{2,1,0:T(8,128)(2,1)S(1)}, u32[]{:S(2)}, u32[]{:S(2)}) %collective-permute-start.15) | collective-permute-done | bytes 1048608 | tf_op jit(solution)/shard_map/ppermute | solution.py:194
  117.4 4.8 %collective-permute-start.16 = (bf16[256,512]{1,0:T(8,128)(2,1)S(1)}, bf16[256,512]{1,0:T(8,128)(2,1)S(1)}, u32[]{:S(2)}, u32[]{:S(2)}) collective-permute-start(bf16[256,512]{1,0:T(8,128)(2,1)S(1)} %get-tuple-element.67), channel_id=1, source_target_pairs={{0,4},{2,6},{4,0},{6,2},{1,5},{3,7},{5,1},{7,3},{8,12},{10,14},{12... | collective-permute-start | bytes 786440 | tf_op jit(solution)/shard_map/ppermute | solution.py:147
  122.3 2.3 %collective-permute-start.17 = (bf16[256,512]{1,0:T(8,128)(2,1)S(1)}, bf16[256,512]{1,0:T(8,128)(2,1)S(1)}, u32[]{:S(2)}, u32[]{:S(2)}) collective-permute-start(bf16[256,512]{1,0:T(8,128)(2,1)S(1)} %get-tuple-element.69), channel_id=1, source_target_pairs={{0,2},{2,4},{4,6},{6,0},{1,3},{3,5},{5,7},{7,1},{8,10},{10,12},{12... | collective-permute-start | bytes 786440 | tf_op jit(solution)/shard_map/ppermute | solution.py:147
  124.6 4.2 %collective-permute-start.18 = (bf16[256,512]{1,0:T(8,128)(2,1)S(1)}, bf16[256,512]{1,0:T(8,128)(2,1)S(1)}, u32[]{:S(2)}, u32[]{:S(2)}) collective-permute-start(bf16[256,512]{1,0:T(8,128)(2,1)S(1)} %get-tuple-element.68), channel_id=1, source_target_pairs={{0,6},{2,0},{4,2},{6,4},{1,7},{3,1},{5,3},{7,5},{8,14},{10,8},{12,... | collective-permute-start | bytes 786440 | tf_op jit(solution)/shard_map/ppermute | solution.py:147
  128.8 5.5 %collective-permute-done.17 = bf16[256,512]{1,0:T(8,128)(2,1)S(1)} collective-permute-done((bf16[256,512]{1,0:T(8,128)(2,1)S(1)}, bf16[256,512]{1,0:T(8,128)(2,1)S(1)}, u32[]{:S(2)}, u32[]{:S(2)}) %collective-permute-start.17) | collective-permute-done | bytes 262176 | tf_op jit(solution)/shard_map/ppermute | solution.py:147
  (33 shorter events, 16.2 us)
Async XLA Ops:
  0.0 37.0 %copy-start.2 = (bf16[256,512]{1,0:T(8,128)(2,1)S(1)}, bf16[256,512]{1,0:T(8,128)(2,1)}, u32[]{:S(2)}) copy-start(bf16[256,512]{1,0:T(8,128)(2,1)} %refs_1_.1) | copy-start | bytes 786436
  1.6 26.0 %collective-permute-start = (bf16[272,256]{1,0:T(8,128)(2,1)}, bf16[272,256]{1,0:T(8,128)(2,1)S(1)}, u32[]{:S(2)}, u32[]{:S(2)}) collective-permute-start(bf16[272,256]{1,0:T(8,128)(2,1)} %shard_map.55.refs_2_), channel_id=1, source_target_pairs={{0,32},{8,40},{16,48},{24,56},{32,64},{40,72},{48,80},{56,88},{64,... | collective-permute-start | bytes 417800 | tf_op jit(solution)/shard_map/ppermute | solution.py:142
  12.1 1.0 copy-start.1
  27.6 32.9 %collective-permute-start.1 = (bf16[272,256]{1,0:T(8,128)(2,1)S(1)}, bf16[272,256]{1,0:T(8,128)(2,1)S(1)}, u32[]{:S(2)}, u32[]{:S(2)}) collective-permute-start(bf16[272,256]{1,0:T(8,128)(2,1)S(1)} %collective-permute-done.refs_2_), channel_id=1, source_target_pairs={{0,32},{8,40},{16,48},{24,56},{32,64},{40,72},{48,80},{56,88},{64,... | collective-permute-start | bytes 417800 | tf_op jit(solution)/shard_map/ppermute | solution.py:142
  32.5 30.0 %collective-permute-start.11 = (bf16[272,256]{1,0:T(8,128)(2,1)}, bf16[272,256]{1,0:T(8,128)(2,1)S(1)}, u32[]{:S(2)}, u32[]{:S(2)}) collective-permute-start(bf16[272,256]{1,0:T(8,128)(2,1)} %shard_map.55.refs_2_), channel_id=1, source_target_pairs={{0,8},{8,16},{16,24},{24,32},{32,40},{40,48},{48,56},{56,64},{64,7... | collective-permute-start | bytes 417800 | tf_op jit(solution)/shard_map/ppermute | solution.py:142
  38.7 27.8 %collective-permute-start.10 = (bf16[272,256]{1,0:T(8,128)(2,1)S(1)}, bf16[272,256]{1,0:T(8,128)(2,1)S(1)}, u32[]{:S(2)}, u32[]{:S(2)}) collective-permute-start(bf16[272,256]{1,0:T(8,128)(2,1)S(1)} %collective-permute-done.refs_2_), channel_id=1, source_target_pairs={{0,1008},{8,1016},{16,0},{24,8},{32,16},{40,24},{48,32},{56,40},{6... | collective-permute-start | bytes 417800 | tf_op jit(solution)/shard_map/ppermute | solution.py:142
  52.0 21.3 %collective-permute-start.8 = (bf16[272,256]{1,0:T(8,128)(2,1)S(1)}, bf16[272,256]{1,0:T(8,128)(2,1)S(1)}, u32[]{:S(2)}, u32[]{:S(2)}) collective-permute-start(bf16[272,256]{1,0:T(8,128)(2,1)S(1)} %collective-permute-done.refs_2_), channel_id=1, source_target_pairs={{0,8},{8,16},{16,24},{24,32},{32,40},{40,48},{48,56},{56,64},{64,7... | collective-permute-start | bytes 417800 | tf_op jit(solution)/shard_map/ppermute | solution.py:142
  53.9 28.9 %collective-permute-start.9 = (bf16[272,256]{1,0:T(8,128)(2,1)S(1)}, bf16[272,256]{1,0:T(8,128)(2,1)S(1)}, u32[]{:S(2)}, u32[]{:S(2)}) collective-permute-start(bf16[272,256]{1,0:T(8,128)(2,1)S(1)} %collective-permute-done.refs_2_), channel_id=1, source_target_pairs={{0,1016},{8,0},{16,8},{24,16},{32,24},{40,32},{48,40},{56,48},{64,... | collective-permute-start | bytes 417800 | tf_op jit(solution)/shard_map/ppermute | solution.py:142
  60.6 17.7 %collective-permute-start.2 = (bf16[272,256]{1,0:T(8,128)(2,1)S(1)}, bf16[272,256]{1,0:T(8,128)(2,1)S(1)}, u32[]{:S(2)}, u32[]{:S(2)}) collective-permute-start(bf16[272,256]{1,0:T(8,128)(2,1)S(1)} %collective-permute-done.1.refs_2_), channel_id=1, source_target_pairs={{0,32},{8,40},{16,48},{24,56},{32,64},{40,72},{48,80},{56,88},{64,... | collective-permute-start | bytes 417800 | tf_op jit(solution)/shard_map/ppermute | solution.py:142
  64.6 20.1 %collective-permute-start.12 = (bf16[272,256]{1,0:T(8,128)(2,1)S(1)}, bf16[272,256]{1,0:T(8,128)(2,1)S(1)}, u32[]{:S(2)}, u32[]{:S(2)}) collective-permute-start(bf16[272,256]{1,0:T(8,128)(2,1)S(1)} %collective-permute-done.1.refs_2_), channel_id=1, source_target_pairs={{0,8},{8,16},{16,24},{24,32},{32,40},{40,48},{48,56},{56,64},{64,7... | collective-permute-start | bytes 417800 | tf_op jit(solution)/shard_map/ppermute | solution.py:142
  66.6 20.1 %collective-permute-start.13 = (bf16[272,256]{1,0:T(8,128)(2,1)S(1)}, bf16[272,256]{1,0:T(8,128)(2,1)S(1)}, u32[]{:S(2)}, u32[]{:S(2)}) collective-permute-start(bf16[272,256]{1,0:T(8,128)(2,1)S(1)} %collective-permute-done.1.refs_2_), channel_id=1, source_target_pairs={{0,1016},{8,0},{16,8},{24,16},{32,24},{40,32},{48,40},{56,48},{64,... | collective-permute-start | bytes 417800 | tf_op jit(solution)/shard_map/ppermute | solution.py:142
  73.3 20.1 %collective-permute-start.14 = (bf16[272,256]{1,0:T(8,128)(2,1)S(1)}, bf16[272,256]{1,0:T(8,128)(2,1)S(1)}, u32[]{:S(2)}, u32[]{:S(2)}) collective-permute-start(bf16[272,256]{1,0:T(8,128)(2,1)S(1)} %collective-permute-done.1.refs_2_), channel_id=1, source_target_pairs={{0,1008},{8,1016},{16,0},{24,8},{32,16},{40,24},{48,32},{56,40},{6... | collective-permute-start | bytes 417800 | tf_op jit(solution)/shard_map/ppermute | solution.py:142
  78.3 21.3 %collective-permute-start.6 = (bf16[272,256]{1,0:T(8,128)(2,1)S(1)}, bf16[272,256]{1,0:T(8,128)(2,1)S(1)}, u32[]{:S(2)}, u32[]{:S(2)}) collective-permute-start(bf16[272,256]{1,0:T(8,128)(2,1)S(1)} %collective-permute-done.2.refs_8_), channel_id=1, source_target_pairs={{0,1008},{8,1016},{16,0},{24,8},{32,16},{40,24},{48,32},{56,40},{6... | collective-permute-start | bytes 417800 | tf_op jit(solution)/shard_map/ppermute | solution.py:142
  82.8 17.2 %collective-permute-start.7 = (bf16[272,256]{1,0:T(8,128)(2,1)S(1)}, bf16[272,256]{1,0:T(8,128)(2,1)S(1)}, u32[]{:S(2)}, u32[]{:S(2)}) collective-permute-start(bf16[272,256]{1,0:T(8,128)(2,1)S(1)} %collective-permute-done.2.refs_8_), channel_id=1, source_target_pairs={{0,24},{8,32},{16,40},{24,48},{32,56},{40,64},{48,72},{56,80},{64,... | collective-permute-start | bytes 417800 | tf_op jit(solution)/shard_map/ppermute | solution.py:142
  84.8 17.3 %collective-permute-start.3 = (bf16[272,256]{1,0:T(8,128)(2,1)S(1)}, bf16[272,256]{1,0:T(8,128)(2,1)S(1)}, u32[]{:S(2)}, u32[]{:S(2)}) collective-permute-start(bf16[272,256]{1,0:T(8,128)(2,1)S(1)} %collective-permute-done.2.refs_8_), channel_id=1, source_target_pairs={{0,16},{8,24},{16,32},{24,40},{32,48},{40,56},{48,64},{56,72},{64,... | collective-permute-start | bytes 417800 | tf_op jit(solution)/shard_map/ppermute | solution.py:142
  86.7 15.4 %collective-permute-start.4 = (bf16[272,256]{1,0:T(8,128)(2,1)S(1)}, bf16[272,256]{1,0:T(8,128)(2,1)S(1)}, u32[]{:S(2)}, u32[]{:S(2)}) collective-permute-start(bf16[272,256]{1,0:T(8,128)(2,1)S(1)} %collective-permute-done.2.refs_8_), channel_id=1, source_target_pairs={{0,1016},{8,0},{16,8},{24,16},{32,24},{40,32},{48,40},{56,48},{64,... | collective-permute-start | bytes 417800 | tf_op jit(solution)/shard_map/ppermute | solution.py:142
  93.4 13.1 %collective-permute-start.5 = (bf16[272,256]{1,0:T(8,128)(2,1)S(1)}, bf16[272,256]{1,0:T(8,128)(2,1)S(1)}, u32[]{:S(2)}, u32[]{:S(2)}) collective-permute-start(bf16[272,256]{1,0:T(8,128)(2,1)S(1)} %collective-permute-done.2.refs_8_), channel_id=1, source_target_pairs={{0,8},{8,16},{16,24},{24,32},{32,40},{40,48},{48,56},{56,64},{64,7... | collective-permute-start | bytes 417800 | tf_op jit(solution)/shard_map/ppermute | solution.py:142
  100.0 6.5 %copy-start = (bf16[512,4096]{1,0:T(8,128)(2,1)S(1)}, bf16[512,4096]{1,0:T(8,128)(2,1)}, u32[]{:S(2)}) copy-start(bf16[512,4096]{1,0:T(8,128)(2,1)} %refs_9_.1) | copy-start | bytes 12582916
  110.9 6.2 %collective-permute-start.15 = (bf16[4,256,512]{2,1,0:T(8,128)(2,1)S(1)}, bf16[4,256,512]{2,1,0:T(8,128)(2,1)S(1)}, u32[]{:S(2)}, u32[]{:S(2)}) collective-permute-start(bf16[4,256,512]{2,1,0:T(8,128)(2,1)S(1)} %get-tuple-element.66), channel_id=1, source_target_pairs={{0,1},{1,0},{2,3},{3,2},{4,5},{5,4},{6,7},{7,6},{8,9},{9,8},{10,11... | collective-permute-start | bytes 3145736 | tf_op jit(solution)/shard_map/ppermute | solution.py:194
  117.4 11.4 %collective-permute-start.16 = (bf16[256,512]{1,0:T(8,128)(2,1)S(1)}, bf16[256,512]{1,0:T(8,128)(2,1)S(1)}, u32[]{:S(2)}, u32[]{:S(2)}) collective-permute-start(bf16[256,512]{1,0:T(8,128)(2,1)S(1)} %get-tuple-element.67), channel_id=1, source_target_pairs={{0,4},{2,6},{4,0},{6,2},{1,5},{3,7},{5,1},{7,3},{8,12},{10,14},{12... | collective-permute-start | bytes 786440 | tf_op jit(solution)/shard_map/ppermute | solution.py:147
  122.3 12.1 %collective-permute-start.17 = (bf16[256,512]{1,0:T(8,128)(2,1)S(1)}, bf16[256,512]{1,0:T(8,128)(2,1)S(1)}, u32[]{:S(2)}, u32[]{:S(2)}) collective-permute-start(bf16[256,512]{1,0:T(8,128)(2,1)S(1)} %get-tuple-element.69), channel_id=1, source_target_pairs={{0,2},{2,4},{4,6},{6,0},{1,3},{3,5},{5,7},{7,1},{8,10},{10,12},{12... | collective-permute-start | bytes 786440 | tf_op jit(solution)/shard_map/ppermute | solution.py:147
  124.6 9.8 %collective-permute-start.18 = (bf16[256,512]{1,0:T(8,128)(2,1)S(1)}, bf16[256,512]{1,0:T(8,128)(2,1)S(1)}, u32[]{:S(2)}, u32[]{:S(2)}) collective-permute-start(bf16[256,512]{1,0:T(8,128)(2,1)S(1)} %get-tuple-element.68), channel_id=1, source_target_pairs={{0,6},{2,0},{4,2},{6,4},{1,7},{3,1},{5,3},{7,5},{8,14},{10,8},{12,... | collective-permute-start | bytes 786440 | tf_op jit(solution)/shard_map/ppermute | solution.py:147

commit v6 on v5

--- a/solution.py
+++ b/solution.py
@@ -15,7 +15,7 @@
 HALF = TOK // 2
 PIECE = TOK + MARK
 COLS = GROUP * HEAD_DIM
-BLOCKS = 8
+ROWS = 4
 HIDDEN = -1e30
 EFFORT = 6
 SCORE_SCALE = math.log2(math.e) / math.sqrt(HEAD_DIM)
@@ -31,7 +31,7 @@
         top_ref, sum_ref, acc_ref = refs[:3]
         refs = refs[3:]
     if final:
-        weight_ref, send_ref, keep_ref, done_ref = refs
+        weight_ref, send_ref, done_ref = refs
     else:
         top_out, sum_out, acc_out = refs
 
@@ -81,15 +81,25 @@
             sum_out[:, cols] = total
             acc_out[:, cols] = product
     if final:
-        row, core = place[0], place[1]
-        for turn in range(BLOCKS // 2):
-            for side in range(2):
-                block = lax.rem(row + turn, BLOCKS // 2) * 2 + (core if side else 1 - core)
-                cols = pl.ds(pl.multiple_of(block * COLS, COLS), COLS)
-                share = jnp.dot(
-                    done_ref[...], weight_ref[:, cols], preferred_element_type=jnp.float32
-                )
-                (keep_ref if side else send_ref)[turn] = share.astype(jnp.bfloat16)
+        for turn, share in enumerate(shares(place, 1 - place[1], done_ref, weight_ref)):
+            send_ref[turn] = share.astype(jnp.bfloat16)
+
+
+def shares(place, core, done_ref, weight_ref):
+    for turn in range(ROWS):
+        block = lax.rem(place[0] + turn, ROWS) * 2 + core
+        cols = pl.ds(pl.multiple_of(block * COLS, COLS), COLS)
+        yield jnp.dot(done_ref[...], weight_ref[:, cols], preferred_element_type=jnp.float32)
+
+
+def keep_shares(place, done_ref, weight_ref, keep_ref):
+    for turn, share in enumerate(shares(place, place[1], done_ref, weight_ref)):
+        keep_ref[turn] = share
+
+
+def add_pair(keep_ref, other_ref, *out_refs):
+    for turn, out_ref in enumerate(out_refs):
+        out_ref[...] = (keep_ref[turn] + other_ref[turn].astype(jnp.float32)).astype(jnp.bfloat16)
 
 
 def run_stage(queries, marks, pieces, state=None, weight=None, place=None):
@@ -107,27 +117,26 @@
     vmem = pl.BlockSpec(memory_space=pltpu.VMEM)
     args = ([place] if final else []) + [queries, marks, *arrays] + ([] if first else list(state))
     in_specs = [vmem] * len(args)
-    scratch = []
     if final:
         in_specs[0] = pl.BlockSpec(memory_space=pltpu.SMEM)
         args.append(weight)
         in_specs.append(vmem)
-        shape = jax.ShapeDtypeStruct((BLOCKS // 2, TOK, COLS), jnp.bfloat16)
-        out_shape = [shape, shape]
-        scratch = [pltpu.VMEM((TOK, COLS), jnp.bfloat16)]
+        out_shape = [
+            jax.ShapeDtypeStruct((ROWS, TOK, COLS), jnp.bfloat16),
+            jax.ShapeDtypeStruct((TOK, COLS), jnp.bfloat16),
+        ]
     else:
         out_shape = [
             jax.ShapeDtypeStruct((TOK, GROUP), jnp.float32),
             jax.ShapeDtypeStruct((TOK, COLS), jnp.float32),
             jax.ShapeDtypeStruct((TOK, COLS), jnp.float32),
         ]
-    flops = EFFORT * 4 * TOK * TOK * COLS * total + (2 * TOK * COLS * COLS * BLOCKS if final else 0)
+    flops = EFFORT * 4 * TOK * TOK * COLS * total + (2 * TOK * COLS * COLS * ROWS if final else 0)
     return pl.pallas_call(
         functools.partial(attend_stage, first, final, len(arrays), tuple(layout)),
         out_shape=out_shape,
         in_specs=in_specs,
         out_specs=[vmem] * len(out_shape),
-        scratch_shapes=scratch,
         compiler_params=pltpu.CompilerParams(vmem_limit_bytes=40 << 20),
         cost_estimate=pl.CostEstimate(
             flops=flops,
@@ -145,10 +154,6 @@
 def around(value, by):
     size = lax.axis_size("head")
     return lax.ppermute(value, "head", [(i, (i + by) % size) for i in range(size)])
-
-
-def plus(one, other):
-    return (one.astype(jnp.float32) + other.astype(jnp.float32)).astype(jnp.bfloat16)
 
 
 def after(value, earlier):
@@ -173,7 +178,7 @@
     near = [back5, back3, back2, back9, back7, back6, back12]
     state = run_stage(queries, marks, near, state)
     state = run_stage(queries, marks, [back10, back15], state)
-    return run_stage(queries, marks, [back14, back11, back13], state, weight, place)
+    return run_stage(queries, marks, [back13, back11, back14], state, weight, place)
 
 
 def join(key_ref, value_ref, ids_ref, joined_ref):
@@ -190,8 +195,26 @@
     own, ids = after(own, doc_ids)
     marks = ids.astype(jnp.float32)
     place = jnp.stack([lax.axis_index("head"), lax.axis_index("srv")]).astype(jnp.int32)
-    send, keep = gather_and_attend(queries, marks[:, None], own, out_weight, place)
-    pair = plus(keep, lax.ppermute(send, "srv", [(0, 1), (1, 0)]))
+    send, done = gather_and_attend(queries, marks[:, None], own, out_weight, place)
+    other = lax.ppermute(send, "srv", [(0, 1), (1, 0)])
+    vmem = pl.BlockSpec(memory_space=pltpu.VMEM)
+    keep = pl.pallas_call(
+        keep_shares,
+        out_shape=jax.ShapeDtypeStruct((ROWS, TOK, COLS), jnp.float32),
+        in_specs=[pl.BlockSpec(memory_space=pltpu.SMEM), vmem, vmem],
+        out_specs=vmem,
+        compiler_params=pltpu.CompilerParams(vmem_limit_bytes=40 << 20),
+        cost_estimate=pl.CostEstimate(
+            flops=2 * 2 * TOK * COLS * COLS * ROWS, bytes_accessed=6 << 20, transcendentals=0
+        ),
+    )(place, done, out_weight)
+    pair = pl.pallas_call(
+        add_pair,
+        out_shape=[jax.ShapeDtypeStruct((TOK, COLS), jnp.bfloat16)] * ROWS,
+        in_specs=[vmem, vmem],
+        out_specs=[vmem] * ROWS,
+        compiler_params=pltpu.CompilerParams(vmem_limit_bytes=40 << 20),
+    )(keep, other)
     summed = pair[0].astype(jnp.float32)
     for turn in (2, 1, 3):
         summed = summed + around(pair[turn], turn).astype(jnp.float32)

time: 136 us -> 134 us (0.985)
  waiting for transfers between devices: 28.5 us -> 21.7 us
  starting transfers between devices: 85.6 us -> 89 us
    ppermute x15, waiting for transfers between devices: 20.6 us -> 15.1 us  [along(): lax.ppermute(value, 'tok', [(i, (i + by) % size) for i in range(size)])]
    ppermute x1, starting transfers between devices: 3.89 us -> 6.4 us  [per_device(): other = lax.ppermute(send, 'srv', [(0, 1), (1, 0)])]
    pallas_call x0 -> x2, Pallas kernels: none -> 1.43 us  [the longest x1 1.25 us: per_device(): pl.pallas_call(keep_shares, out_shape=jax.ShapeDtypeStruct((ROWS, TOK, CO...]
  transfers between devices with their start and end apart: 19 -> 19, of which waited for: 6 -> 5; matrix products, arithmetic and copies ran while one was open for 1% -> 1% of each run, Pallas kernels for 9% -> 10%
where the time goes in v6:
time: 134 us; the launch traced here: 133 us
  starting transfers between devices  89 us (66%)
  waiting for transfers between devices  21.7 us (16%)
  Pallas kernels  18.5 us (14%)
  local copies, waits for them, and re-layouts  2.04 us (2%)
  other arithmetic  1.6 us (1%)
    ppermute x15, starting transfers between devices, along(): lax.ppermute(value, 'tok', [(i, (i + by) % size) for i in range(size)])  71.3 us
    pallas_call x6, Pallas kernels, run_stage(): pl.pallas_call(functools.partial(attend_stage, first, final, len(arrays),...  15.6 us
    ppermute x15, waiting for transfers between devices, along(): lax.ppermute(value, 'tok', [(i, (i + by) % size) for i in range(size)])  15.1 us
    ppermute x3, starting transfers between devices, around(): lax.ppermute(value, 'head', [(i, (i + by) % size) for i in range(size)])  11.3 us
    ppermute x1, starting transfers between devices, per_device(): other = lax.ppermute(send, 'srv', [(0, 1), (1, 0)])  6.4 us
    ppermute x3, waiting for transfers between devices, around(): lax.ppermute(value, 'head', [(i, (i + by) % size) for i in range(size)])  5.56 us
  transfers between devices with their start and end apart: 19, of which 5 were waited for; matrix products, arithmetic and copies ran while one was open for 1% of the time, Pallas kernels for 10%

profile of v6, /device:TPU:1, one launch (start us, length us, event | category | flops | bytes accessed | tf_op | source)
XLA Modules:
  0.0 133.2 jit_solution(9739558189926006201)
XLA Ops:
  1.6 9.6 %collective-permute-start = (bf16[272,256]{1,0:T(8,128)(2,1)}, bf16[272,256]{1,0:T(8,128)(2,1)S(1)}, u32[]{:S(2)}, u32[]{:S(2)}) collective-permute-start(bf16[272,256]{1,0:T(8,128)(2,1)} %shard_map.55.refs_2_), channel_id=1, source_target_pairs={{0,32},{8,40},{16,48},{24,56},{32,64},{40,72},{48,80},{56,88},{64,... | collective-permute-start | bytes 417800 | tf_op jit(solution)/shard_map/ppermute | solution.py:151
  14.8 12.8 %collective-permute-done.refs_2_ = bf16[272,256]{1,0:T(8,128)(2,1)S(1)} collective-permute-done((bf16[272,256]{1,0:T(8,128)(2,1)}, bf16[272,256]{1,0:T(8,128)(2,1)S(1)}, u32[]{:S(2)}, u32[]{:S(2)}) %collective-permute-start) | collective-permute-done | bytes 139296 | tf_op jit(solution)/shard_map/ppermute | solution.py:151
  27.6 4.9 %collective-permute-start.1 = (bf16[272,256]{1,0:T(8,128)(2,1)S(1)}, bf16[272,256]{1,0:T(8,128)(2,1)S(1)}, u32[]{:S(2)}, u32[]{:S(2)}) collective-permute-start(bf16[272,256]{1,0:T(8,128)(2,1)S(1)} %collective-permute-done.refs_2_), channel_id=1, source_target_pairs={{0,32},{8,40},{16,48},{24,56},{32,64},{40,72},{48,80},{56,88},{64,... | collective-permute-start | bytes 417800 | tf_op jit(solution)/shard_map/ppermute | solution.py:151
  32.5 4.5 %collective-permute-start.11 = (bf16[272,256]{1,0:T(8,128)(2,1)}, bf16[272,256]{1,0:T(8,128)(2,1)S(1)}, u32[]{:S(2)}, u32[]{:S(2)}) collective-permute-start(bf16[272,256]{1,0:T(8,128)(2,1)} %shard_map.55.refs_2_), channel_id=1, source_target_pairs={{0,8},{8,16},{16,24},{24,32},{32,40},{40,48},{48,56},{56,64},{64,7... | collective-permute-start | bytes 417800 | tf_op jit(solution)/shard_map/ppermute | solution.py:151
  39.6 13.2 %collective-permute-start.10 = (bf16[272,256]{1,0:T(8,128)(2,1)S(1)}, bf16[272,256]{1,0:T(8,128)(2,1)S(1)}, u32[]{:S(2)}, u32[]{:S(2)}) collective-permute-start(bf16[272,256]{1,0:T(8,128)(2,1)S(1)} %collective-permute-done.refs_2_), channel_id=1, source_target_pairs={{0,1008},{8,1016},{16,0},{24,8},{32,16},{40,24},{48,32},{56,40},{6... | collective-permute-start | bytes 417800 | tf_op jit(solution)/shard_map/ppermute | solution.py:151
  52.9 1.9 %collective-permute-start.9 = (bf16[272,256]{1,0:T(8,128)(2,1)S(1)}, bf16[272,256]{1,0:T(8,128)(2,1)S(1)}, u32[]{:S(2)}, u32[]{:S(2)}) collective-permute-start(bf16[272,256]{1,0:T(8,128)(2,1)S(1)} %collective-permute-done.refs_2_), channel_id=1, source_target_pairs={{0,1016},{8,0},{16,8},{24,16},{32,24},{40,32},{48,40},{56,48},{64,... | collective-permute-start | bytes 417800 | tf_op jit(solution)/shard_map/ppermute | solution.py:151
  54.8 3.4 %collective-permute-start.8 = (bf16[272,256]{1,0:T(8,128)(2,1)S(1)}, bf16[272,256]{1,0:T(8,128)(2,1)S(1)}, u32[]{:S(2)}, u32[]{:S(2)}) collective-permute-start(bf16[272,256]{1,0:T(8,128)(2,1)S(1)} %collective-permute-done.refs_2_), channel_id=1, source_target_pairs={{0,8},{8,16},{16,24},{24,32},{32,40},{40,48},{48,56},{56,64},{64,7... | collective-permute-start | bytes 417800 | tf_op jit(solution)/shard_map/ppermute | solution.py:151
  58.2 1.9 %collective-permute-start.2 = (bf16[272,256]{1,0:T(8,128)(2,1)S(1)}, bf16[272,256]{1,0:T(8,128)(2,1)S(1)}, u32[]{:S(2)}, u32[]{:S(2)}) collective-permute-start(bf16[272,256]{1,0:T(8,128)(2,1)S(1)} %collective-permute-done.1.refs_2_), channel_id=1, source_target_pairs={{0,32},{8,40},{16,48},{24,56},{32,64},{40,72},{48,80},{56,88},{64,... | collective-permute-start | bytes 417800 | tf_op jit(solution)/shard_map/ppermute | solution.py:151
  60.1 2.1 %shard_map.58 = (f32[256,4]{1,0:T(8,128)S(1)}, f32[256,512]{1,0:T(8,128)S(1)}, f32[256,512]{1,0:T(8,128)S(1)}) custom-call(bf16[256,512]{1,0:T(8,128)(2,1)S(1)} %copy-done.2, f32[256,1]{1,0:T(8,128)S(1)} %copy.11.refs_1_.refs_2_, bf16[272,256]{1,0:T(8,128)(2,1)S(1)} %collective-permute-done.1.refs_2_, bf16[272,256]{1,0:T(8,128)(2,1)S(1)} %collective-permute-done.11.refs_3_, ...), custom_call_target="tpu_custom_call" | custom-call | flops 1610612736 | bytes 2375680 | tf_op jit(solution)/shard_map/pallas_call | solution.py:135
  62.2 7.0 %collective-permute-start.14 = (bf16[272,256]{1,0:T(8,128)(2,1)S(1)}, bf16[272,256]{1,0:T(8,128)(2,1)S(1)}, u32[]{:S(2)}, u32[]{:S(2)}) collective-permute-start(bf16[272,256]{1,0:T(8,128)(2,1)S(1)} %collective-permute-done.1.refs_2_), channel_id=1, source_target_pairs={{0,1008},{8,1016},{16,0},{24,8},{32,16},{40,24},{48,32},{56,40},{6... | collective-permute-start | bytes 417800 | tf_op jit(solution)/shard_map/ppermute | solution.py:151
  69.2 3.4 %collective-permute-start.13 = (bf16[272,256]{1,0:T(8,128)(2,1)S(1)}, bf16[272,256]{1,0:T(8,128)(2,1)S(1)}, u32[]{:S(2)}, u32[]{:S(2)}) collective-permute-start(bf16[272,256]{1,0:T(8,128)(2,1)S(1)} %collective-permute-done.1.refs_2_), channel_id=1, source_target_pairs={{0,1016},{8,0},{16,8},{24,16},{32,24},{40,32},{48,40},{56,48},{64,... | collective-permute-start | bytes 417800 | tf_op jit(solution)/shard_map/ppermute | solution.py:151
  72.6 1.9 %collective-permute-start.12 = (bf16[272,256]{1,0:T(8,128)(2,1)S(1)}, bf16[272,256]{1,0:T(8,128)(2,1)S(1)}, u32[]{:S(2)}, u32[]{:S(2)}) collective-permute-start(bf16[272,256]{1,0:T(8,128)(2,1)S(1)} %collective-permute-done.1.refs_2_), channel_id=1, source_target_pairs={{0,8},{8,16},{16,24},{24,32},{32,40},{40,48},{48,56},{56,64},{64,7... | collective-permute-start | bytes 417800 | tf_op jit(solution)/shard_map/ppermute | solution.py:151
  75.6 2.8 %collective-permute-start.7 = (bf16[272,256]{1,0:T(8,128)(2,1)S(1)}, bf16[272,256]{1,0:T(8,128)(2,1)S(1)}, u32[]{:S(2)}, u32[]{:S(2)}) collective-permute-start(bf16[272,256]{1,0:T(8,128)(2,1)S(1)} %collective-permute-done.2.refs_8_), channel_id=1, source_target_pairs={{0,24},{8,32},{16,40},{24,48},{32,56},{40,64},{48,72},{56,80},{64,... | collective-permute-start | bytes 417800 | tf_op jit(solution)/shard_map/ppermute | solution.py:151
  78.4 5.5 %collective-permute-start.6 = (bf16[272,256]{1,0:T(8,128)(2,1)S(1)}, bf16[272,256]{1,0:T(8,128)(2,1)S(1)}, u32[]{:S(2)}, u32[]{:S(2)}) collective-permute-start(bf16[272,256]{1,0:T(8,128)(2,1)S(1)} %collective-permute-done.2.refs_8_), channel_id=1, source_target_pairs={{0,1008},{8,1016},{16,0},{24,8},{32,16},{40,24},{48,32},{56,40},{6... | collective-permute-start | bytes 417800 | tf_op jit(solution)/shard_map/ppermute | solution.py:151
  85.8 7.2 %collective-permute-start.4 = (bf16[272,256]{1,0:T(8,128)(2,1)S(1)}, bf16[272,256]{1,0:T(8,128)(2,1)S(1)}, u32[]{:S(2)}, u32[]{:S(2)}) collective-permute-start(bf16[272,256]{1,0:T(8,128)(2,1)S(1)} %collective-permute-done.2.refs_8_), channel_id=1, source_target_pairs={{0,1016},{8,0},{16,8},{24,16},{32,24},{40,32},{48,40},{56,48},{64,... | collective-permute-start | bytes 417800 | tf_op jit(solution)/shard_map/ppermute | solution.py:151
  93.0 2.1 %collective-permute-start.3 = (bf16[272,256]{1,0:T(8,128)(2,1)S(1)}, bf16[272,256]{1,0:T(8,128)(2,1)S(1)}, u32[]{:S(2)}, u32[]{:S(2)}) collective-permute-start(bf16[272,256]{1,0:T(8,128)(2,1)S(1)} %collective-permute-done.2.refs_8_), channel_id=1, source_target_pairs={{0,8},{8,16},{16,24},{24,32},{32,40},{40,48},{48,56},{56,64},{64,7... | collective-permute-start | bytes 417800 | tf_op jit(solution)/shard_map/ppermute | solution.py:151
  95.1 4.1 %shard_map.59 = (f32[256,4]{1,0:T(8,128)S(1)}, f32[256,512]{1,0:T(8,128)S(1)}, f32[256,512]{1,0:T(8,128)S(1)}) custom-call(bf16[256,512]{1,0:T(8,128)(2,1)S(1)} %copy-done.3, f32[256,1]{1,0:T(8,128)S(1)} %copy.11.refs_1_.refs_2_, bf16[272,256]{1,0:T(8,128)(2,1)S(1)} %collective-permute-done.8.refs_2_, bf16[272,256]{1,0:T(8,128)(2,1)S(1)} %collective-permute-done.9.refs_3_, ...), custom_call_target="tpu_custom_call" | custom-call | flops 5637144576 | bytes 3072000 | tf_op jit(solution)/shard_map/pallas_call | solution.py:135
  99.3 2.1 %shard_map.60 = (f32[256,4]{1,0:T(8,128)S(1)}, f32[256,512]{1,0:T(8,128)S(1)}, f32[256,512]{1,0:T(8,128)S(1)}) custom-call(bf16[256,512]{1,0:T(8,128)(2,1)S(1)} %copy-done.3, f32[256,1]{1,0:T(8,128)S(1)} %copy.11.refs_1_.refs_2_, bf16[272,256]{1,0:T(8,128)(2,1)S(1)} %collective-permute-done.6.refs_2_, bf16[272,256]{1,0:T(8,128)(2,1)S(1)} %collective-permute-done.7.refs_3_, ...), custom_call_target="tpu_custom_call" | custom-call | flops 1610612736 | bytes 2375680 | tf_op jit(solution)/shard_map/pallas_call | solution.py:135
  102.8 3.8 %shard_map.61 = (bf16[4,256,512]{2,1,0:T(8,128)(2,1)S(1)}, bf16[256,512]{1,0:T(8,128)(2,1)S(1)}) custom-call(s32[2]{0:T(128)S(1)} %pad_add_fusion.refs_0_.place, bf16[256,512]{1,0:T(8,128)(2,1)S(1)} %copy-done.3, f32[256,1]{1,0:T(8,128)S(1)} %copy.11.refs_1_.refs_2_, bf16[272,256]{1,0:T(8,128)(2,1)S(1)} %collective-permute-done.3.refs_3_, ...), custom_call_target="tpu_custom_call" | custom-call | flops 2952790016 | bytes 8806400 | tf_op jit(solution)/shard_map/pallas_call | solution.py:135
  106.6 6.4 %collective-permute-start.15 = (bf16[4,256,512]{2,1,0:T(8,128)(2,1)S(1)}, bf16[4,256,512]{2,1,0:T(8,128)(2,1)S(1)}, u32[]{:S(2)}, u32[]{:S(2)}) collective-permute-start(bf16[4,256,512]{2,1,0:T(8,128)(2,1)S(1)} %get-tuple-element.70), channel_id=1, source_target_pairs={{0,1},{1,0},{2,3},{3,2},{4,5},{5,4},{6,7},{7,6},{8,9},{9,8},{10,11... | collective-permute-start | bytes 3145736 | tf_op jit(solution)/shard_map/ppermute | solution.py:199
  115.4 4.8 %collective-permute-start.16 = (bf16[256,512]{1,0:T(8,128)(2,1)S(1)}, bf16[256,512]{1,0:T(8,128)(2,1)S(1)}, u32[]{:S(2)}, u32[]{:S(2)}) collective-permute-start(bf16[256,512]{1,0:T(8,128)(2,1)S(1)} %get-tuple-element.72), channel_id=1, source_target_pairs={{0,4},{2,6},{4,0},{6,2},{1,5},{3,7},{5,1},{7,3},{8,12},{10,14},{12... | collective-permute-start | bytes 786440 | tf_op jit(solution)/shard_map/ppermute | solution.py:156
  120.3 2.3 %collective-permute-start.17 = (bf16[256,512]{1,0:T(8,128)(2,1)S(1)}, bf16[256,512]{1,0:T(8,128)(2,1)S(1)}, u32[]{:S(2)}, u32[]{:S(2)}) collective-permute-start(bf16[256,512]{1,0:T(8,128)(2,1)S(1)} %get-tuple-element.73), channel_id=1, source_target_pairs={{0,2},{2,4},{4,6},{6,0},{1,3},{3,5},{5,7},{7,1},{8,10},{10,12},{12... | collective-permute-start | bytes 786440 | tf_op jit(solution)/shard_map/ppermute | solution.py:156
  122.6 4.2 %collective-permute-start.18 = (bf16[256,512]{1,0:T(8,128)(2,1)S(1)}, bf16[256,512]{1,0:T(8,128)(2,1)S(1)}, u32[]{:S(2)}, u32[]{:S(2)}) collective-permute-start(bf16[256,512]{1,0:T(8,128)(2,1)S(1)} %get-tuple-element.74), channel_id=1, source_target_pairs={{0,6},{2,0},{4,2},{6,4},{1,7},{3,1},{5,3},{7,5},{8,14},{10,8},{12,... | collective-permute-start | bytes 786440 | tf_op jit(solution)/shard_map/ppermute | solution.py:156
  126.8 5.6 %collective-permute-done.17 = bf16[256,512]{1,0:T(8,128)(2,1)S(1)} collective-permute-done((bf16[256,512]{1,0:T(8,128)(2,1)S(1)}, bf16[256,512]{1,0:T(8,128)(2,1)S(1)}, u32[]{:S(2)}, u32[]{:S(2)}) %collective-permute-start.17) | collective-permute-done | bytes 262176 | tf_op jit(solution)/shard_map/ppermute | solution.py:156
  (35 shorter events, 15.3 us)
Async XLA Ops:
  1.6 26.0 %collective-permute-start = (bf16[272,256]{1,0:T(8,128)(2,1)}, bf16[272,256]{1,0:T(8,128)(2,1)S(1)}, u32[]{:S(2)}, u32[]{:S(2)}) collective-permute-start(bf16[272,256]{1,0:T(8,128)(2,1)} %shard_map.55.refs_2_), channel_id=1, source_target_pairs={{0,32},{8,40},{16,48},{24,56},{32,64},{40,72},{48,80},{56,88},{64,... | collective-permute-start | bytes 417800 | tf_op jit(solution)/shard_map/ppermute | solution.py:151
  12.0 1.0 copy-start.1
  27.6 30.6 %collective-permute-start.1 = (bf16[272,256]{1,0:T(8,128)(2,1)S(1)}, bf16[272,256]{1,0:T(8,128)(2,1)S(1)}, u32[]{:S(2)}, u32[]{:S(2)}) collective-permute-start(bf16[272,256]{1,0:T(8,128)(2,1)S(1)} %collective-permute-done.refs_2_), channel_id=1, source_target_pairs={{0,32},{8,40},{16,48},{24,56},{32,64},{40,72},{48,80},{56,88},{64,... | collective-permute-start | bytes 417800 | tf_op jit(solution)/shard_map/ppermute | solution.py:151
  32.5 27.6 %collective-permute-start.11 = (bf16[272,256]{1,0:T(8,128)(2,1)}, bf16[272,256]{1,0:T(8,128)(2,1)S(1)}, u32[]{:S(2)}, u32[]{:S(2)}) collective-permute-start(bf16[272,256]{1,0:T(8,128)(2,1)} %shard_map.55.refs_2_), channel_id=1, source_target_pairs={{0,8},{8,16},{16,24},{24,32},{32,40},{40,48},{48,56},{56,64},{64,7... | collective-permute-start | bytes 417800 | tf_op jit(solution)/shard_map/ppermute | solution.py:151
  37.0 1.0 copy-start.2
  37.9 57.2 %copy-start.3 = (bf16[256,512]{1,0:T(8,128)(2,1)S(1)}, bf16[256,512]{1,0:T(8,128)(2,1)}, u32[]{:S(2)}) copy-start(bf16[256,512]{1,0:T(8,128)(2,1)} %refs_1_.1) | copy-start | bytes 786436
  39.6 29.6 %collective-permute-start.10 = (bf16[272,256]{1,0:T(8,128)(2,1)S(1)}, bf16[272,256]{1,0:T(8,128)(2,1)S(1)}, u32[]{:S(2)}, u32[]{:S(2)}) collective-permute-start(bf16[272,256]{1,0:T(8,128)(2,1)S(1)} %collective-permute-done.refs_2_), channel_id=1, source_target_pairs={{0,1008},{8,1016},{16,0},{24,8},{32,16},{40,24},{48,32},{56,40},{6... | collective-permute-start | bytes 417800 | tf_op jit(solution)/shard_map/ppermute | solution.py:151
  52.9 19.8 %collective-permute-start.9 = (bf16[272,256]{1,0:T(8,128)(2,1)S(1)}, bf16[272,256]{1,0:T(8,128)(2,1)S(1)}, u32[]{:S(2)}, u32[]{:S(2)}) collective-permute-start(bf16[272,256]{1,0:T(8,128)(2,1)S(1)} %collective-permute-done.refs_2_), channel_id=1, source_target_pairs={{0,1016},{8,0},{16,8},{24,16},{32,24},{40,32},{48,40},{56,48},{64,... | collective-permute-start | bytes 417800 | tf_op jit(solution)/shard_map/ppermute | solution.py:151
  54.8 23.6 %collective-permute-start.8 = (bf16[272,256]{1,0:T(8,128)(2,1)S(1)}, bf16[272,256]{1,0:T(8,128)(2,1)S(1)}, u32[]{:S(2)}, u32[]{:S(2)}) collective-permute-start(bf16[272,256]{1,0:T(8,128)(2,1)S(1)} %collective-permute-done.refs_2_), channel_id=1, source_target_pairs={{0,8},{8,16},{16,24},{24,32},{32,40},{40,48},{48,56},{56,64},{64,7... | collective-permute-start | bytes 417800 | tf_op jit(solution)/shard_map/ppermute | solution.py:151
  58.2 17.4 %collective-permute-start.2 = (bf16[272,256]{1,0:T(8,128)(2,1)S(1)}, bf16[272,256]{1,0:T(8,128)(2,1)S(1)}, u32[]{:S(2)}, u32[]{:S(2)}) collective-permute-start(bf16[272,256]{1,0:T(8,128)(2,1)S(1)} %collective-permute-done.1.refs_2_), channel_id=1, source_target_pairs={{0,32},{8,40},{16,48},{24,56},{32,64},{40,72},{48,80},{56,88},{64,... | collective-permute-start | bytes 417800 | tf_op jit(solution)/shard_map/ppermute | solution.py:151
  62.2 21.7 %collective-permute-start.14 = (bf16[272,256]{1,0:T(8,128)(2,1)S(1)}, bf16[272,256]{1,0:T(8,128)(2,1)S(1)}, u32[]{:S(2)}, u32[]{:S(2)}) collective-permute-start(bf16[272,256]{1,0:T(8,128)(2,1)S(1)} %collective-permute-done.1.refs_2_), channel_id=1, source_target_pairs={{0,1008},{8,1016},{16,0},{24,8},{32,16},{40,24},{48,32},{56,40},{6... | collective-permute-start | bytes 417800 | tf_op jit(solution)/shard_map/ppermute | solution.py:151
  69.2 16.6 %collective-permute-start.13 = (bf16[272,256]{1,0:T(8,128)(2,1)S(1)}, bf16[272,256]{1,0:T(8,128)(2,1)S(1)}, u32[]{:S(2)}, u32[]{:S(2)}) collective-permute-start(bf16[272,256]{1,0:T(8,128)(2,1)S(1)} %collective-permute-done.1.refs_2_), channel_id=1, source_target_pairs={{0,1016},{8,0},{16,8},{24,16},{32,24},{40,32},{48,40},{56,48},{64,... | collective-permute-start | bytes 417800 | tf_op jit(solution)/shard_map/ppermute | solution.py:151
  72.6 20.4 %collective-permute-start.12 = (bf16[272,256]{1,0:T(8,128)(2,1)S(1)}, bf16[272,256]{1,0:T(8,128)(2,1)S(1)}, u32[]{:S(2)}, u32[]{:S(2)}) collective-permute-start(bf16[272,256]{1,0:T(8,128)(2,1)S(1)} %collective-permute-done.1.refs_2_), channel_id=1, source_target_pairs={{0,8},{8,16},{16,24},{24,32},{32,40},{40,48},{48,56},{56,64},{64,7... | collective-permute-start | bytes 417800 | tf_op jit(solution)/shard_map/ppermute | solution.py:151
  75.6 23.7 %collective-permute-start.7 = (bf16[272,256]{1,0:T(8,128)(2,1)S(1)}, bf16[272,256]{1,0:T(8,128)(2,1)S(1)}, u32[]{:S(2)}, u32[]{:S(2)}) collective-permute-start(bf16[272,256]{1,0:T(8,128)(2,1)S(1)} %collective-permute-done.2.refs_8_), channel_id=1, source_target_pairs={{0,24},{8,32},{16,40},{24,48},{32,56},{40,64},{48,72},{56,80},{64,... | collective-permute-start | bytes 417800 | tf_op jit(solution)/shard_map/ppermute | solution.py:151
  78.4 20.9 %collective-permute-start.6 = (bf16[272,256]{1,0:T(8,128)(2,1)S(1)}, bf16[272,256]{1,0:T(8,128)(2,1)S(1)}, u32[]{:S(2)}, u32[]{:S(2)}) collective-permute-start(bf16[272,256]{1,0:T(8,128)(2,1)S(1)} %collective-permute-done.2.refs_8_), channel_id=1, source_target_pairs={{0,1008},{8,1016},{16,0},{24,8},{32,16},{40,24},{48,32},{56,40},{6... | collective-permute-start | bytes 417800 | tf_op jit(solution)/shard_map/ppermute | solution.py:151
  83.9 17.5 %collective-permute-start.5 = (bf16[272,256]{1,0:T(8,128)(2,1)S(1)}, bf16[272,256]{1,0:T(8,128)(2,1)S(1)}, u32[]{:S(2)}, u32[]{:S(2)}) collective-permute-start(bf16[272,256]{1,0:T(8,128)(2,1)S(1)} %collective-permute-done.2.refs_8_), channel_id=1, source_target_pairs={{0,16},{8,24},{16,32},{24,40},{32,48},{40,56},{48,64},{56,72},{64,... | collective-permute-start | bytes 417800 | tf_op jit(solution)/shard_map/ppermute | solution.py:151
  85.8 15.6 %collective-permute-start.4 = (bf16[272,256]{1,0:T(8,128)(2,1)S(1)}, bf16[272,256]{1,0:T(8,128)(2,1)S(1)}, u32[]{:S(2)}, u32[]{:S(2)}) collective-permute-start(bf16[272,256]{1,0:T(8,128)(2,1)S(1)} %collective-permute-done.2.refs_8_), channel_id=1, source_target_pairs={{0,1016},{8,0},{16,8},{24,16},{32,24},{40,32},{48,40},{56,48},{64,... | collective-permute-start | bytes 417800 | tf_op jit(solution)/shard_map/ppermute | solution.py:151
  93.0 9.8 %collective-permute-start.3 = (bf16[272,256]{1,0:T(8,128)(2,1)S(1)}, bf16[272,256]{1,0:T(8,128)(2,1)S(1)}, u32[]{:S(2)}, u32[]{:S(2)}) collective-permute-start(bf16[272,256]{1,0:T(8,128)(2,1)S(1)} %collective-permute-done.2.refs_8_), channel_id=1, source_target_pairs={{0,8},{8,16},{16,24},{24,32},{32,40},{40,48},{48,56},{56,64},{64,7... | collective-permute-start | bytes 417800 | tf_op jit(solution)/shard_map/ppermute | solution.py:151
  99.3 3.5 %copy-start = (bf16[512,4096]{1,0:T(8,128)(2,1)S(1)}, bf16[512,4096]{1,0:T(8,128)(2,1)}, u32[]{:S(2)}) copy-start(bf16[512,4096]{1,0:T(8,128)(2,1)} %weight_ref.1) | copy-start | bytes 12582916
  106.6 8.7 %collective-permute-start.15 = (bf16[4,256,512]{2,1,0:T(8,128)(2,1)S(1)}, bf16[4,256,512]{2,1,0:T(8,128)(2,1)S(1)}, u32[]{:S(2)}, u32[]{:S(2)}) collective-permute-start(bf16[4,256,512]{2,1,0:T(8,128)(2,1)S(1)} %get-tuple-element.70), channel_id=1, source_target_pairs={{0,1},{1,0},{2,3},{3,2},{4,5},{5,4},{6,7},{7,6},{8,9},{9,8},{10,11... | collective-permute-start | bytes 3145736 | tf_op jit(solution)/shard_map/ppermute | solution.py:199
  115.4 11.3 %collective-permute-start.16 = (bf16[256,512]{1,0:T(8,128)(2,1)S(1)}, bf16[256,512]{1,0:T(8,128)(2,1)S(1)}, u32[]{:S(2)}, u32[]{:S(2)}) collective-permute-start(bf16[256,512]{1,0:T(8,128)(2,1)S(1)} %get-tuple-element.72), channel_id=1, source_target_pairs={{0,4},{2,6},{4,0},{6,2},{1,5},{3,7},{5,1},{7,3},{8,12},{10,14},{12... | collective-permute-start | bytes 786440 | tf_op jit(solution)/shard_map/ppermute | solution.py:156
  120.3 12.1 %collective-permute-start.17 = (bf16[256,512]{1,0:T(8,128)(2,1)S(1)}, bf16[256,512]{1,0:T(8,128)(2,1)S(1)}, u32[]{:S(2)}, u32[]{:S(2)}) collective-permute-start(bf16[256,512]{1,0:T(8,128)(2,1)S(1)} %get-tuple-element.73), channel_id=1, source_target_pairs={{0,2},{2,4},{4,6},{6,0},{1,3},{3,5},{5,7},{7,1},{8,10},{10,12},{12... | collective-permute-start | bytes 786440 | tf_op jit(solution)/shard_map/ppermute | solution.py:156
  122.6 9.8 %collective-permute-start.18 = (bf16[256,512]{1,0:T(8,128)(2,1)S(1)}, bf16[256,512]{1,0:T(8,128)(2,1)S(1)}, u32[]{:S(2)}, u32[]{:S(2)}) collective-permute-start(bf16[256,512]{1,0:T(8,128)(2,1)S(1)} %get-tuple-element.74), channel_id=1, source_target_pairs={{0,6},{2,0},{4,2},{6,4},{1,7},{3,1},{5,3},{7,5},{8,14},{10,8},{12,... | collective-permute-start | bytes 786440 | tf_op jit(solution)/shard_map/ppermute | solution.py:156

commit v7 on v6

--- a/solution.py
+++ b/solution.py
@@ -175,9 +175,8 @@
     back6, back7, back9 = [along(back8, n) for n in (-2, -1, 1)]
     back15, back10, back14 = [along(back12, n) for n in (3, -2, 2)]
     back11, back13 = [along(back12, n) for n in (-1, 1)]
-    near = [back5, back3, back2, back9, back7, back6, back12]
+    near = [back5, back3, back2, back9, back7, back6, back12, back10, back15]
     state = run_stage(queries, marks, near, state)
-    state = run_stage(queries, marks, [back10, back15], state)
     return run_stage(queries, marks, [back13, back11, back14], state, weight, place)
 
 

time: 134 us -> 134 us (level)
    pallas_call x6 -> x5, Pallas kernels: 15.6 us -> 14.3 us  [run_stage(): pl.pallas_call(functools.partial(attend_stage, first, final, len(arrays),...]
  transfers between devices with their start and end apart: 19 -> 19, of which waited for: 5 -> 5; matrix products, arithmetic and copies ran while one was open for 1% -> 1% of each run, Pallas kernels for 10% -> 9%
where the time goes in v7:
time: 134 us; the launch traced here: 133 us
  starting transfers between devices  89.2 us (67%)
  waiting for transfers between devices  23 us (17%)
  Pallas kernels  17.2 us (13%)
  local copies, waits for them, and re-layouts  2.04 us (2%)
  other arithmetic  1.6 us (1%)
    ppermute x15, starting transfers between devices, along(): lax.ppermute(value, 'tok', [(i, (i + by) % size) for i in range(size)])  71.5 us
    ppermute x15, waiting for transfers between devices, along(): lax.ppermute(value, 'tok', [(i, (i + by) % size) for i in range(size)])  16.5 us
    pallas_call x5, Pallas kernels, run_stage(): pl.pallas_call(functools.partial(attend_stage, first, final, len(arrays),...  14.3 us
    ppermute x3, starting transfers between devices, around(): lax.ppermute(value, 'head', [(i, (i + by) % size) for i in range(size)])  11.3 us
    ppermute x1, starting transfers between devices, per_device(): other = lax.ppermute(send, 'srv', [(0, 1), (1, 0)])  6.34 us
    ppermute x3, waiting for transfers between devices, around(): lax.ppermute(value, 'head', [(i, (i + by) % size) for i in range(size)])  5.56 us
  transfers between devices with their start and end apart: 19, of which 5 were waited for; matrix products, arithmetic and copies ran while one was open for 1% of the time, Pallas kernels for 9%

profile of v7, /device:TPU:1, one launch (start us, length us, event | category | flops | bytes accessed | tf_op | source)
XLA Modules:
  0.0 133.4 jit_solution(2454108530519989851)
XLA Ops:
  1.6 9.6 %collective-permute-start = (bf16[272,256]{1,0:T(8,128)(2,1)}, bf16[272,256]{1,0:T(8,128)(2,1)S(1)}, u32[]{:S(2)}, u32[]{:S(2)}) collective-permute-start(bf16[272,256]{1,0:T(8,128)(2,1)} %shard_map.55.refs_2_), channel_id=1, source_target_pairs={{0,32},{8,40},{16,48},{24,56},{32,64},{40,72},{48,80},{56,88},{64,... | collective-permute-start | bytes 417800 | tf_op jit(solution)/shard_map/ppermute | solution.py:151
  14.8 12.8 %collective-permute-done.refs_2_ = bf16[272,256]{1,0:T(8,128)(2,1)S(1)} collective-permute-done((bf16[272,256]{1,0:T(8,128)(2,1)}, bf16[272,256]{1,0:T(8,128)(2,1)S(1)}, u32[]{:S(2)}, u32[]{:S(2)}) %collective-permute-start) | collective-permute-done | bytes 139296 | tf_op jit(solution)/shard_map/ppermute | solution.py:151
  27.6 4.9 %collective-permute-start.1 = (bf16[272,256]{1,0:T(8,128)(2,1)S(1)}, bf16[272,256]{1,0:T(8,128)(2,1)S(1)}, u32[]{:S(2)}, u32[]{:S(2)}) collective-permute-start(bf16[272,256]{1,0:T(8,128)(2,1)S(1)} %collective-permute-done.refs_2_), channel_id=1, source_target_pairs={{0,32},{8,40},{16,48},{24,56},{32,64},{40,72},{48,80},{56,88},{64,... | collective-permute-start | bytes 417800 | tf_op jit(solution)/shard_map/ppermute | solution.py:151
  32.5 4.5 %collective-permute-start.9 = (bf16[272,256]{1,0:T(8,128)(2,1)}, bf16[272,256]{1,0:T(8,128)(2,1)S(1)}, u32[]{:S(2)}, u32[]{:S(2)}) collective-permute-start(bf16[272,256]{1,0:T(8,128)(2,1)} %shard_map.55.refs_2_), channel_id=1, source_target_pairs={{0,8},{8,16},{16,24},{24,32},{32,40},{40,48},{48,56},{56,64},{64,7... | collective-permute-start | bytes 417800 | tf_op jit(solution)/shard_map/ppermute | solution.py:151
  39.6 13.2 %collective-permute-start.8 = (bf16[272,256]{1,0:T(8,128)(2,1)S(1)}, bf16[272,256]{1,0:T(8,128)(2,1)S(1)}, u32[]{:S(2)}, u32[]{:S(2)}) collective-permute-start(bf16[272,256]{1,0:T(8,128)(2,1)S(1)} %collective-permute-done.refs_2_), channel_id=1, source_target_pairs={{0,1008},{8,1016},{16,0},{24,8},{32,16},{40,24},{48,32},{56,40},{6... | collective-permute-start | bytes 417800 | tf_op jit(solution)/shard_map/ppermute | solution.py:151
  54.8 3.4 %collective-permute-start.6 = (bf16[272,256]{1,0:T(8,128)(2,1)S(1)}, bf16[272,256]{1,0:T(8,128)(2,1)S(1)}, u32[]{:S(2)}, u32[]{:S(2)}) collective-permute-start(bf16[272,256]{1,0:T(8,128)(2,1)S(1)} %collective-permute-done.refs_2_), channel_id=1, source_target_pairs={{0,8},{8,16},{16,24},{24,32},{32,40},{40,48},{48,56},{56,64},{64,7... | collective-permute-start | bytes 417800 | tf_op jit(solution)/shard_map/ppermute | solution.py:151
  58.2 1.9 %collective-permute-start.2 = (bf16[272,256]{1,0:T(8,128)(2,1)S(1)}, bf16[272,256]{1,0:T(8,128)(2,1)S(1)}, u32[]{:S(2)}, u32[]{:S(2)}) collective-permute-start(bf16[272,256]{1,0:T(8,128)(2,1)S(1)} %collective-permute-done.1.refs_2_), channel_id=1, source_target_pairs={{0,32},{8,40},{16,48},{24,56},{32,64},{40,72},{48,80},{56,88},{64,... | collective-permute-start | bytes 417800 | tf_op jit(solution)/shard_map/ppermute | solution.py:151
  60.1 2.1 %shard_map.58 = (f32[256,4]{1,0:T(8,128)S(1)}, f32[256,512]{1,0:T(8,128)S(1)}, f32[256,512]{1,0:T(8,128)S(1)}) custom-call(bf16[256,512]{1,0:T(8,128)(2,1)S(1)} %copy-done.2, f32[256,1]{1,0:T(8,128)S(1)} %copy.10.refs_1_.refs_2_, bf16[272,256]{1,0:T(8,128)(2,1)S(1)} %collective-permute-done.1.refs_2_, bf16[272,256]{1,0:T(8,128)(2,1)S(1)} %collective-permute-done.9.refs_3_, ...), custom_call_target="tpu_custom_call" | custom-call | flops 1610612736 | bytes 2375680 | tf_op jit(solution)/shard_map/pallas_call | solution.py:135
  62.2 7.0 %collective-permute-start.12 = (bf16[272,256]{1,0:T(8,128)(2,1)S(1)}, bf16[272,256]{1,0:T(8,128)(2,1)S(1)}, u32[]{:S(2)}, u32[]{:S(2)}) collective-permute-start(bf16[272,256]{1,0:T(8,128)(2,1)S(1)} %collective-permute-done.1.refs_2_), channel_id=1, source_target_pairs={{0,1008},{8,1016},{16,0},{24,8},{32,16},{40,24},{48,32},{56,40},{6... | collective-permute-start | bytes 417800 | tf_op jit(solution)/shard_map/ppermute | solution.py:151
  69.2 3.4 %collective-permute-start.11 = (bf16[272,256]{1,0:T(8,128)(2,1)S(1)}, bf16[272,256]{1,0:T(8,128)(2,1)S(1)}, u32[]{:S(2)}, u32[]{:S(2)}) collective-permute-start(bf16[272,256]{1,0:T(8,128)(2,1)S(1)} %collective-permute-done.1.refs_2_), channel_id=1, source_target_pairs={{0,1016},{8,0},{16,8},{24,16},{32,24},{40,32},{48,40},{56,48},{64,... | collective-permute-start | bytes 417800 | tf_op jit(solution)/shard_map/ppermute | solution.py:151
  72.6 1.9 %collective-permute-start.10 = (bf16[272,256]{1,0:T(8,128)(2,1)S(1)}, bf16[272,256]{1,0:T(8,128)(2,1)S(1)}, u32[]{:S(2)}, u32[]{:S(2)}) collective-permute-start(bf16[272,256]{1,0:T(8,128)(2,1)S(1)} %collective-permute-done.1.refs_2_), channel_id=1, source_target_pairs={{0,8},{8,16},{16,24},{24,32},{32,40},{40,48},{48,56},{56,64},{64,7... | collective-permute-start | bytes 417800 | tf_op jit(solution)/shard_map/ppermute | solution.py:151
  75.6 2.8 %collective-permute-start.14 = (bf16[272,256]{1,0:T(8,128)(2,1)S(1)}, bf16[272,256]{1,0:T(8,128)(2,1)S(1)}, u32[]{:S(2)}, u32[]{:S(2)}) collective-permute-start(bf16[272,256]{1,0:T(8,128)(2,1)S(1)} %collective-permute-done.2.refs_8_), channel_id=1, source_target_pairs={{0,24},{8,32},{16,40},{24,48},{32,56},{40,64},{48,72},{56,80},{64,... | collective-permute-start | bytes 417800 | tf_op jit(solution)/shard_map/ppermute | solution.py:151
  78.4 5.4 %collective-permute-start.13 = (bf16[272,256]{1,0:T(8,128)(2,1)S(1)}, bf16[272,256]{1,0:T(8,128)(2,1)S(1)}, u32[]{:S(2)}, u32[]{:S(2)}) collective-permute-start(bf16[272,256]{1,0:T(8,128)(2,1)S(1)} %collective-permute-done.2.refs_8_), channel_id=1, source_target_pairs={{0,1008},{8,1016},{16,0},{24,8},{32,16},{40,24},{48,32},{56,40},{6... | collective-permute-start | bytes 417800 | tf_op jit(solution)/shard_map/ppermute | solution.py:151
  83.9 2.2 %collective-permute-start.5 = (bf16[272,256]{1,0:T(8,128)(2,1)S(1)}, bf16[272,256]{1,0:T(8,128)(2,1)S(1)}, u32[]{:S(2)}, u32[]{:S(2)}) collective-permute-start(bf16[272,256]{1,0:T(8,128)(2,1)S(1)} %collective-permute-done.2.refs_8_), channel_id=1, source_target_pairs={{0,16},{8,24},{16,32},{24,40},{32,48},{40,56},{48,64},{56,72},{64,... | collective-permute-start | bytes 417800 | tf_op jit(solution)/shard_map/ppermute | solution.py:151
  86.1 7.2 %collective-permute-start.4 = (bf16[272,256]{1,0:T(8,128)(2,1)S(1)}, bf16[272,256]{1,0:T(8,128)(2,1)S(1)}, u32[]{:S(2)}, u32[]{:S(2)}) collective-permute-start(bf16[272,256]{1,0:T(8,128)(2,1)S(1)} %collective-permute-done.2.refs_8_), channel_id=1, source_target_pairs={{0,1016},{8,0},{16,8},{24,16},{32,24},{40,32},{48,40},{56,48},{64,... | collective-permute-start | bytes 417800 | tf_op jit(solution)/shard_map/ppermute | solution.py:151
  93.3 2.1 %collective-permute-start.3 = (bf16[272,256]{1,0:T(8,128)(2,1)S(1)}, bf16[272,256]{1,0:T(8,128)(2,1)S(1)}, u32[]{:S(2)}, u32[]{:S(2)}) collective-permute-start(bf16[272,256]{1,0:T(8,128)(2,1)S(1)} %collective-permute-done.2.refs_8_), channel_id=1, source_target_pairs={{0,8},{8,16},{16,24},{24,32},{32,40},{40,48},{48,56},{56,64},{64,7... | collective-permute-start | bytes 417800 | tf_op jit(solution)/shard_map/ppermute | solution.py:151
  95.5 5.0 %shard_map.59 = (f32[256,4]{1,0:T(8,128)S(1)}, f32[256,512]{1,0:T(8,128)S(1)}, f32[256,512]{1,0:T(8,128)S(1)}) custom-call(bf16[256,512]{1,0:T(8,128)(2,1)S(1)} %copy-done.3, f32[256,1]{1,0:T(8,128)S(1)} %copy.10.refs_1_.refs_2_, bf16[272,256]{1,0:T(8,128)(2,1)S(1)} %collective-permute-done.6.refs_2_, bf16[272,256]{1,0:T(8,128)(2,1)S(1)} %collective-permute-done.7.refs_3_, ...), custom_call_target="tpu_custom_call" | custom-call | flops 7247757312 | bytes 3350528 | tf_op jit(solution)/shard_map/pallas_call | solution.py:135
  100.5 2.6 %collective-permute-done.3.refs_3_ = bf16[272,256]{1,0:T(8,128)(2,1)S(1)} collective-permute-done((bf16[272,256]{1,0:T(8,128)(2,1)S(1)}, bf16[272,256]{1,0:T(8,128)(2,1)S(1)}, u32[]{:S(2)}, u32[]{:S(2)}) %collective-permute-start.3) | collective-permute-done | bytes 139296 | tf_op jit(solution)/shard_map/ppermute | solution.py:151
  103.1 3.8 %shard_map.60 = (bf16[4,256,512]{2,1,0:T(8,128)(2,1)S(1)}, bf16[256,512]{1,0:T(8,128)(2,1)S(1)}) custom-call(s32[2]{0:T(128)S(1)} %pad_add_fusion.refs_0_.place, bf16[256,512]{1,0:T(8,128)(2,1)S(1)} %copy-done.3, f32[256,1]{1,0:T(8,128)S(1)} %copy.10.refs_1_.refs_2_, bf16[272,256]{1,0:T(8,128)(2,1)S(1)} %collective-permute-done.3.refs_3_, ...), custom_call_target="tpu_custom_call" | custom-call | flops 2952790016 | bytes 8806400 | tf_op jit(solution)/shard_map/pallas_call | solution.py:135
  106.9 6.3 %collective-permute-start.15 = (bf16[4,256,512]{2,1,0:T(8,128)(2,1)S(1)}, bf16[4,256,512]{2,1,0:T(8,128)(2,1)S(1)}, u32[]{:S(2)}, u32[]{:S(2)}) collective-permute-start(bf16[4,256,512]{2,1,0:T(8,128)(2,1)S(1)} %get-tuple-element.64), channel_id=1, source_target_pairs={{0,1},{1,0},{2,3},{3,2},{4,5},{5,4},{6,7},{7,6},{8,9},{9,8},{10,11... | collective-permute-start | bytes 3145736 | tf_op jit(solution)/shard_map/ppermute | solution.py:198
  115.6 4.8 %collective-permute-start.16 = (bf16[256,512]{1,0:T(8,128)(2,1)S(1)}, bf16[256,512]{1,0:T(8,128)(2,1)S(1)}, u32[]{:S(2)}, u32[]{:S(2)}) collective-permute-start(bf16[256,512]{1,0:T(8,128)(2,1)S(1)} %get-tuple-element.66), channel_id=1, source_target_pairs={{0,4},{2,6},{4,0},{6,2},{1,5},{3,7},{5,1},{7,3},{8,12},{10,14},{12... | collective-permute-start | bytes 786440 | tf_op jit(solution)/shard_map/ppermute | solution.py:156
  120.5 2.3 %collective-permute-start.17 = (bf16[256,512]{1,0:T(8,128)(2,1)S(1)}, bf16[256,512]{1,0:T(8,128)(2,1)S(1)}, u32[]{:S(2)}, u32[]{:S(2)}) collective-permute-start(bf16[256,512]{1,0:T(8,128)(2,1)S(1)} %get-tuple-element.67), channel_id=1, source_target_pairs={{0,2},{2,4},{4,6},{6,0},{1,3},{3,5},{5,7},{7,1},{8,10},{10,12},{12... | collective-permute-start | bytes 786440 | tf_op jit(solution)/shard_map/ppermute | solution.py:156
  122.8 4.2 %collective-permute-start.18 = (bf16[256,512]{1,0:T(8,128)(2,1)S(1)}, bf16[256,512]{1,0:T(8,128)(2,1)S(1)}, u32[]{:S(2)}, u32[]{:S(2)}) collective-permute-start(bf16[256,512]{1,0:T(8,128)(2,1)S(1)} %get-tuple-element.68), channel_id=1, source_target_pairs={{0,6},{2,0},{4,2},{6,4},{1,7},{3,1},{5,3},{7,5},{8,14},{10,8},{12,... | collective-permute-start | bytes 786440 | tf_op jit(solution)/shard_map/ppermute | solution.py:156
  127.0 5.6 %collective-permute-done.17 = bf16[256,512]{1,0:T(8,128)(2,1)S(1)} collective-permute-done((bf16[256,512]{1,0:T(8,128)(2,1)S(1)}, bf16[256,512]{1,0:T(8,128)(2,1)S(1)}, u32[]{:S(2)}, u32[]{:S(2)}) %collective-permute-start.17) | collective-permute-done | bytes 262176 | tf_op jit(solution)/shard_map/ppermute | solution.py:156
  (34 shorter events, 14.0 us)
Async XLA Ops:
  1.6 26.0 %collective-permute-start = (bf16[272,256]{1,0:T(8,128)(2,1)}, bf16[272,256]{1,0:T(8,128)(2,1)S(1)}, u32[]{:S(2)}, u32[]{:S(2)}) collective-permute-start(bf16[272,256]{1,0:T(8,128)(2,1)} %shard_map.55.refs_2_), channel_id=1, source_target_pairs={{0,32},{8,40},{16,48},{24,56},{32,64},{40,72},{48,80},{56,88},{64,... | collective-permute-start | bytes 417800 | tf_op jit(solution)/shard_map/ppermute | solution.py:151
  12.0 1.0 copy-start.1
  27.6 30.6 %collective-permute-start.1 = (bf16[272,256]{1,0:T(8,128)(2,1)S(1)}, bf16[272,256]{1,0:T(8,128)(2,1)S(1)}, u32[]{:S(2)}, u32[]{:S(2)}) collective-permute-start(bf16[272,256]{1,0:T(8,128)(2,1)S(1)} %collective-permute-done.refs_2_), channel_id=1, source_target_pairs={{0,32},{8,40},{16,48},{24,56},{32,64},{40,72},{48,80},{56,88},{64,... | collective-permute-start | bytes 417800 | tf_op jit(solution)/shard_map/ppermute | solution.py:151
  32.5 27.6 %collective-permute-start.9 = (bf16[272,256]{1,0:T(8,128)(2,1)}, bf16[272,256]{1,0:T(8,128)(2,1)S(1)}, u32[]{:S(2)}, u32[]{:S(2)}) collective-permute-start(bf16[272,256]{1,0:T(8,128)(2,1)} %shard_map.55.refs_2_), channel_id=1, source_target_pairs={{0,8},{8,16},{16,24},{24,32},{32,40},{40,48},{48,56},{56,64},{64,7... | collective-permute-start | bytes 417800 | tf_op jit(solution)/shard_map/ppermute | solution.py:151
  37.0 1.0 copy-start.2
  37.9 57.5 %copy-start.3 = (bf16[256,512]{1,0:T(8,128)(2,1)S(1)}, bf16[256,512]{1,0:T(8,128)(2,1)}, u32[]{:S(2)}) copy-start(bf16[256,512]{1,0:T(8,128)(2,1)} %refs_1_.1) | copy-start | bytes 786436
  39.6 29.6 %collective-permute-start.8 = (bf16[272,256]{1,0:T(8,128)(2,1)S(1)}, bf16[272,256]{1,0:T(8,128)(2,1)S(1)}, u32[]{:S(2)}, u32[]{:S(2)}) collective-permute-start(bf16[272,256]{1,0:T(8,128)(2,1)S(1)} %collective-permute-done.refs_2_), channel_id=1, source_target_pairs={{0,1008},{8,1016},{16,0},{24,8},{32,16},{40,24},{48,32},{56,40},{6... | collective-permute-start | bytes 417800 | tf_op jit(solution)/shard_map/ppermute | solution.py:151
  52.9 19.8 %collective-permute-start.7 = (bf16[272,256]{1,0:T(8,128)(2,1)S(1)}, bf16[272,256]{1,0:T(8,128)(2,1)S(1)}, u32[]{:S(2)}, u32[]{:S(2)}) collective-permute-start(bf16[272,256]{1,0:T(8,128)(2,1)S(1)} %collective-permute-done.refs_2_), channel_id=1, source_target_pairs={{0,1016},{8,0},{16,8},{24,16},{32,24},{40,32},{48,40},{56,48},{64,... | collective-permute-start | bytes 417800 | tf_op jit(solution)/shard_map/ppermute | solution.py:151
  54.8 23.6 %collective-permute-start.6 = (bf16[272,256]{1,0:T(8,128)(2,1)S(1)}, bf16[272,256]{1,0:T(8,128)(2,1)S(1)}, u32[]{:S(2)}, u32[]{:S(2)}) collective-permute-start(bf16[272,256]{1,0:T(8,128)(2,1)S(1)} %collective-permute-done.refs_2_), channel_id=1, source_target_pairs={{0,8},{8,16},{16,24},{24,32},{32,40},{40,48},{48,56},{56,64},{64,7... | collective-permute-start | bytes 417800 | tf_op jit(solution)/shard_map/ppermute | solution.py:151
  58.2 17.4 %collective-permute-start.2 = (bf16[272,256]{1,0:T(8,128)(2,1)S(1)}, bf16[272,256]{1,0:T(8,128)(2,1)S(1)}, u32[]{:S(2)}, u32[]{:S(2)}) collective-permute-start(bf16[272,256]{1,0:T(8,128)(2,1)S(1)} %collective-permute-done.1.refs_2_), channel_id=1, source_target_pairs={{0,32},{8,40},{16,48},{24,56},{32,64},{40,72},{48,80},{56,88},{64,... | collective-permute-start | bytes 417800 | tf_op jit(solution)/shard_map/ppermute | solution.py:151
  62.2 21.7 %collective-permute-start.12 = (bf16[272,256]{1,0:T(8,128)(2,1)S(1)}, bf16[272,256]{1,0:T(8,128)(2,1)S(1)}, u32[]{:S(2)}, u32[]{:S(2)}) collective-permute-start(bf16[272,256]{1,0:T(8,128)(2,1)S(1)} %collective-permute-done.1.refs_2_), channel_id=1, source_target_pairs={{0,1008},{8,1016},{16,0},{24,8},{32,16},{40,24},{48,32},{56,40},{6... | collective-permute-start | bytes 417800 | tf_op jit(solution)/shard_map/ppermute | solution.py:151
  69.2 16.8 %collective-permute-start.11 = (bf16[272,256]{1,0:T(8,128)(2,1)S(1)}, bf16[272,256]{1,0:T(8,128)(2,1)S(1)}, u32[]{:S(2)}, u32[]{:S(2)}) collective-permute-start(bf16[272,256]{1,0:T(8,128)(2,1)S(1)} %collective-permute-done.1.refs_2_), channel_id=1, source_target_pairs={{0,1016},{8,0},{16,8},{24,16},{32,24},{40,32},{48,40},{56,48},{64,... | collective-permute-start | bytes 417800 | tf_op jit(solution)/shard_map/ppermute | solution.py:151
  72.6 20.7 %collective-permute-start.10 = (bf16[272,256]{1,0:T(8,128)(2,1)S(1)}, bf16[272,256]{1,0:T(8,128)(2,1)S(1)}, u32[]{:S(2)}, u32[]{:S(2)}) collective-permute-start(bf16[272,256]{1,0:T(8,128)(2,1)S(1)} %collective-permute-done.1.refs_2_), channel_id=1, source_target_pairs={{0,8},{8,16},{16,24},{24,32},{32,40},{40,48},{48,56},{56,64},{64,7... | collective-permute-start | bytes 417800 | tf_op jit(solution)/shard_map/ppermute | solution.py:151
  75.6 19.9 %collective-permute-start.14 = (bf16[272,256]{1,0:T(8,128)(2,1)S(1)}, bf16[272,256]{1,0:T(8,128)(2,1)S(1)}, u32[]{:S(2)}, u32[]{:S(2)}) collective-permute-start(bf16[272,256]{1,0:T(8,128)(2,1)S(1)} %collective-permute-done.2.refs_8_), channel_id=1, source_target_pairs={{0,24},{8,32},{16,40},{24,48},{32,56},{40,64},{48,72},{56,80},{64,... | collective-permute-start | bytes 417800 | tf_op jit(solution)/shard_map/ppermute | solution.py:151
  78.4 17.1 %collective-permute-start.13 = (bf16[272,256]{1,0:T(8,128)(2,1)S(1)}, bf16[272,256]{1,0:T(8,128)(2,1)S(1)}, u32[]{:S(2)}, u32[]{:S(2)}) collective-permute-start(bf16[272,256]{1,0:T(8,128)(2,1)S(1)} %collective-permute-done.2.refs_8_), channel_id=1, source_target_pairs={{0,1008},{8,1016},{16,0},{24,8},{32,16},{40,24},{48,32},{56,40},{6... | collective-permute-start | bytes 417800 | tf_op jit(solution)/shard_map/ppermute | solution.py:151
  83.9 19.2 %copy-start = (bf16[512,4096]{1,0:T(8,128)(2,1)S(1)}, bf16[512,4096]{1,0:T(8,128)(2,1)}, u32[]{:S(2)}) copy-start(bf16[512,4096]{1,0:T(8,128)(2,1)} %weight_ref.1) | copy-start | bytes 12582916
  83.9 16.6 %collective-permute-start.5 = (bf16[272,256]{1,0:T(8,128)(2,1)S(1)}, bf16[272,256]{1,0:T(8,128)(2,1)S(1)}, u32[]{:S(2)}, u32[]{:S(2)}) collective-permute-start(bf16[272,256]{1,0:T(8,128)(2,1)S(1)} %collective-permute-done.2.refs_8_), channel_id=1, source_target_pairs={{0,16},{8,24},{16,32},{24,40},{32,48},{40,56},{48,64},{56,72},{64,... | collective-permute-start | bytes 417800 | tf_op jit(solution)/shard_map/ppermute | solution.py:151
  86.1 14.4 %collective-permute-start.4 = (bf16[272,256]{1,0:T(8,128)(2,1)S(1)}, bf16[272,256]{1,0:T(8,128)(2,1)S(1)}, u32[]{:S(2)}, u32[]{:S(2)}) collective-permute-start(bf16[272,256]{1,0:T(8,128)(2,1)S(1)} %collective-permute-done.2.refs_8_), channel_id=1, source_target_pairs={{0,1016},{8,0},{16,8},{24,16},{32,24},{40,32},{48,40},{56,48},{64,... | collective-permute-start | bytes 417800 | tf_op jit(solution)/shard_map/ppermute | solution.py:151
  93.3 9.7 %collective-permute-start.3 = (bf16[272,256]{1,0:T(8,128)(2,1)S(1)}, bf16[272,256]{1,0:T(8,128)(2,1)S(1)}, u32[]{:S(2)}, u32[]{:S(2)}) collective-permute-start(bf16[272,256]{1,0:T(8,128)(2,1)S(1)} %collective-permute-done.2.refs_8_), channel_id=1, source_target_pairs={{0,8},{8,16},{16,24},{24,32},{32,40},{40,48},{48,56},{56,64},{64,7... | collective-permute-start | bytes 417800 | tf_op jit(solution)/shard_map/ppermute | solution.py:151
  106.9 8.6 %collective-permute-start.15 = (bf16[4,256,512]{2,1,0:T(8,128)(2,1)S(1)}, bf16[4,256,512]{2,1,0:T(8,128)(2,1)S(1)}, u32[]{:S(2)}, u32[]{:S(2)}) collective-permute-start(bf16[4,256,512]{2,1,0:T(8,128)(2,1)S(1)} %get-tuple-element.64), channel_id=1, source_target_pairs={{0,1},{1,0},{2,3},{3,2},{4,5},{5,4},{6,7},{7,6},{8,9},{9,8},{10,11... | collective-permute-start | bytes 3145736 | tf_op jit(solution)/shard_map/ppermute | solution.py:198
  115.6 11.3 %collective-permute-start.16 = (bf16[256,512]{1,0:T(8,128)(2,1)S(1)}, bf16[256,512]{1,0:T(8,128)(2,1)S(1)}, u32[]{:S(2)}, u32[]{:S(2)}) collective-permute-start(bf16[256,512]{1,0:T(8,128)(2,1)S(1)} %get-tuple-element.66), channel_id=1, source_target_pairs={{0,4},{2,6},{4,0},{6,2},{1,5},{3,7},{5,1},{7,3},{8,12},{10,14},{12... | collective-permute-start | bytes 786440 | tf_op jit(solution)/shard_map/ppermute | solution.py:156
  120.5 12.1 %collective-permute-start.17 = (bf16[256,512]{1,0:T(8,128)(2,1)S(1)}, bf16[256,512]{1,0:T(8,128)(2,1)S(1)}, u32[]{:S(2)}, u32[]{:S(2)}) collective-permute-start(bf16[256,512]{1,0:T(8,128)(2,1)S(1)} %get-tuple-element.67), channel_id=1, source_target_pairs={{0,2},{2,4},{4,6},{6,0},{1,3},{3,5},{5,7},{7,1},{8,10},{10,12},{12... | collective-permute-start | bytes 786440 | tf_op jit(solution)/shard_map/ppermute | solution.py:156
  122.8 9.8 %collective-permute-start.18 = (bf16[256,512]{1,0:T(8,128)(2,1)S(1)}, bf16[256,512]{1,0:T(8,128)(2,1)S(1)}, u32[]{:S(2)}, u32[]{:S(2)}) collective-permute-start(bf16[256,512]{1,0:T(8,128)(2,1)S(1)} %get-tuple-element.68), channel_id=1, source_target_pairs={{0,6},{2,0},{4,2},{6,4},{1,7},{3,1},{5,3},{7,5},{8,14},{10,8},{12,... | collective-permute-start | bytes 786440 | tf_op jit(solution)/shard_map/ppermute | solution.py:156
